TPU v7x, 256 devices: a whole 4x4x8 slice. The times are simulated.
256 devices in a mesh: ctx: 8 (over z), chan: 8 (over y, core), req: 4 (over x).
Axes of the slice: x: 4, y: 4, z: 8, core: 2. Of those that a mesh axis runs over, the one named last changes fastest.
Arguments:
- window_input: bfloat16 [4096, 8192], P(('req', 'ctx'), 'chan'), parts along dimension 0, may hold values from -6 to 6
- gate_values: bfloat16 [4096, 8192], P(('req', 'ctx'), 'chan'), parts along dimension 0, may hold values from -6 to 6
- page_pool: bfloat16 [4096, 8, 8192], P(('req', 'ctx', 'chan')), parts along dimension 0, may hold values from -6 to 6
- page_table: int32 [2048], P('req'), parts along dimension 0, may hold values from 0 to 1023, as said below
- filter_len: int32 [8192], P('chan'), may hold values from 1024 to 4096
- residues: float32 [8192, 16], P('chan'), may hold values from -0.06 to 0.06
- decays: float32 [8192, 16], P('chan'), may hold values from 0.0001 to 0.1
- skip_gain: float32 [8192], P('chan'), may hold values from 0.5 to 1.5
Outputs:
- gated_output: bfloat16 [4096, 8192], P(('req', 'ctx'), 'chan'), parts along dimension 0
There are 4 independent parts, one for each index of `req`. A program takes and returns all parts, laid end to end along the dimension named above; an argument that names none is the same for every part. Nothing has to cross between parts.
Inputs may be any that keep to these rules, and one draw needn't show every extreme that they name: `page_table`: the entries are distinct; pool page i lies on device i // 16 of ctx+chan. Of the 64 cache pages of each aligned block of the table (the cached positions of one index of ctx), at most 2 lie on one device, and in every block some device holds exactly 2.
All inputs are finite; a program needn't handle non-finite values.
Results may differ from a plain program's by a relative error of at most 0.009.
Values may be sent and summed in bfloat16 or wider, within the bound.
No kernel may reach another device: no remote copies, remote signals or barrier semaphores. Data moves between devices by JAX's collectives and lax.ppermute only.
A program may use at most 64 MiB of HBM per device.

v0:
```python
import math

import jax
import jax.numpy as jnp
from jax import lax
from jax.sharding import PartitionSpec as P

COLS = 128


TWO_PI = 2.0 * math.pi
precise = lax.Precision.HIGHEST


def page_ranks(owners, owner_count):
    onehot = (owners[..., None] == jnp.arange(owner_count, dtype=jnp.int32)).astype(jnp.int32)
    counted = jnp.cumsum(onehot, axis=1)
    return jnp.sum(counted * onehot, axis=-1) - 1


def dft_table(count_out, count_in, period, offset):
    product_index = (
        (jnp.arange(count_out, dtype=jnp.int32)[:, None] + offset)
        * jnp.arange(count_in, dtype=jnp.int32)[None, :]
        % period
    )
    table_angle = TWO_PI / period * product_index.astype(jnp.float32)
    return (jnp.cos(table_angle), jnp.sin(table_angle))


def split_table(table):
    high_part = table.astype(jnp.bfloat16)
    low_part = (table - high_part.astype(jnp.float32)).astype(jnp.bfloat16)
    return (high_part, low_part)


def split_product(table, data_rows):
    high_part, low_part = split_table(table)
    first = jnp.dot(high_part, data_rows, preferred_element_type=jnp.float32)
    return first + jnp.dot(low_part, data_rows, preferred_element_type=jnp.float32)


def filter_spectrum(row_count, col_count, decay_rates, weights, lengths):
    seq_len = row_count * col_count
    freq_index = (
        jnp.arange(row_count, dtype=jnp.int32)[:, None]
        + row_count * jnp.arange(col_count, dtype=jnp.int32)[None, :]
    )
    base_angle = TWO_PI / seq_len * freq_index.astype(jnp.float32)
    half_square = (jnp.sin(0.5 * base_angle) ** 2)[..., None]
    sin_base = jnp.sin(base_angle)[..., None]
    phase_angle = (
        TWO_PI
        / seq_len
        * (freq_index[..., None] * lengths[None, None, :] % seq_len).astype(jnp.float32)
    )
    phase_half = jnp.sin(0.5 * phase_angle) ** 2
    phase_sin = jnp.sin(phase_angle)
    length_float = lengths.astype(jnp.float32)

    def add_mode(mode_index, partial_value):
        spec_re, spec_im = partial_value
        decay_rate = lax.dynamic_index_in_dim(decay_rates, mode_index, 1, keepdims=False)
        weight = lax.dynamic_index_in_dim(weights, mode_index, 1, keepdims=False)
        damping = jnp.exp(-decay_rate)
        den_re = -jnp.expm1(-decay_rate) + 2.0 * damping * half_square
        den_im = damping * sin_base
        tail_damp = jnp.exp(-decay_rate * length_float)
        num_re = -jnp.expm1(-decay_rate * length_float) + 2.0 * tail_damp * phase_half
        num_im = tail_damp * phase_sin
        mode_scale = weight / (den_re * den_re + den_im * den_im)
        spec_re = spec_re + mode_scale * (num_re * den_re + num_im * den_im)
        spec_im = spec_im + mode_scale * (num_im * den_re - num_re * den_im)
        return (spec_re, spec_im)

    zeros = jnp.zeros((row_count, col_count, lengths.shape[0]), jnp.float32)
    return lax.fori_loop(0, decay_rates.shape[1], add_mode, (zeros, zeros))


def convolve(signal, spec_re, spec_im, row_count, col_count, win_rows):
    seq_len = row_count * col_count
    channels = signal.shape[1]
    signal_rows = signal.reshape(row_count, col_count * channels)
    cos_rows, sin_rows = dft_table(row_count, row_count, row_count, 0)
    part_re = split_product(cos_rows, signal_rows).reshape(row_count, col_count, channels)
    part_im = -split_product(sin_rows, signal_rows).reshape(row_count, col_count, channels)
    twist_cos, twist_sin = dft_table(row_count, col_count, seq_len, 0)
    twist_cos = twist_cos[..., None]
    twist_sin = twist_sin[..., None]
    turned_re = part_re * twist_cos + part_im * twist_sin
    turned_im = part_im * twist_cos - part_re * twist_sin
    cos_cols, sin_cols = dft_table(col_count, col_count, col_count, 0)
    freq_re = jnp.einsum("abc,db->adc", turned_re, cos_cols, precision=precise) + jnp.einsum(
        "abc,db->adc", turned_im, sin_cols, precision=precise
    )
    freq_im = jnp.einsum("abc,db->adc", turned_im, cos_cols, precision=precise) - jnp.einsum(
        "abc,db->adc", turned_re, sin_cols, precision=precise
    )
    product_re = freq_re * spec_re - freq_im * spec_im
    product_im = freq_re * spec_im + freq_im * spec_re
    back_re = jnp.einsum("adc,db->abc", product_re, cos_cols, precision=precise) - jnp.einsum(
        "adc,db->abc", product_im, sin_cols, precision=precise
    )
    back_im = jnp.einsum("adc,db->abc", product_im, cos_cols, precision=precise) + jnp.einsum(
        "adc,db->abc", product_re, sin_cols, precision=precise
    )
    reverted_re = back_re * twist_cos - back_im * twist_sin
    reverted_im = back_im * twist_cos + back_re * twist_sin
    cos_win, sin_win = dft_table(win_rows, row_count, row_count, row_count - win_rows)
    result = jnp.dot(
        cos_win, reverted_re.reshape(row_count, col_count * channels), precision=precise
    )
    result = result - jnp.dot(
        sin_win, reverted_im.reshape(row_count, col_count * channels), precision=precise
    )
    return (result / seq_len).reshape(win_rows * col_count, channels)


def local(
    window_input, gate_values, page_pool, page_table, filter_len, residues, decays, skip_gain
):
    ctx_count = lax.axis_size("ctx")
    chan_count = lax.axis_size("chan")
    owner_count = ctx_count * chan_count
    ctx_pos = lax.axis_index("ctx")
    owner_self = ctx_pos * chan_count + lax.axis_index("chan")
    pool_pages = page_pool.shape[0]
    page_len = page_pool.shape[1]
    model_width = page_pool.shape[2]
    slab_width = model_width // chan_count
    pencil = slab_width // ctx_count
    capacity = pool_pages // ctx_count
    per_block = page_table.shape[0] // ctx_count
    page_rows = page_table.reshape(ctx_count, per_block)
    owners = page_rows // pool_pages
    pool_slots = page_rows % pool_pages
    page_rank = page_ranks(owners, owner_count)
    is_mine = owners == owner_self
    selected = is_mine[..., None] & (page_rank[..., None] == jnp.arange(capacity, dtype=jnp.int32))
    send_slots = jnp.sum(jnp.where(selected, pool_slots[..., None], 0), axis=1)
    outgoing = page_pool[send_slots.reshape(-1)]
    parcel = outgoing.reshape(ctx_count, capacity, page_len, chan_count, slab_width)
    parcel = jnp.transpose(parcel, (0, 3, 1, 2, 4)).reshape(
        owner_count, capacity, page_len, slab_width
    )
    arrived = lax.all_to_all(parcel, ("ctx", "chan"), split_axis=0, concat_axis=0, tiled=True)
    own_row = lax.dynamic_index_in_dim(owners, ctx_pos, 0, keepdims=False)
    rank_row = lax.dynamic_index_in_dim(page_rank, ctx_pos, 0, keepdims=False)
    gathered = arrived.reshape(owner_count * capacity, page_len, slab_width)[
        own_row * capacity + rank_row
    ]
    cache_block = gathered.reshape(per_block * page_len, slab_width)
    cache_seq, window_seq = (
        lax.all_to_all(cache_block, "ctx", split_axis=1, concat_axis=0, tiled=True),
        lax.all_to_all(window_input, "ctx", split_axis=1, concat_axis=0, tiled=True),
    )
    signal = jnp.concatenate([cache_seq, window_seq], axis=0)
    col_count = COLS
    row_count = signal.shape[0] // col_count
    win_rows = window_seq.shape[0] // col_count
    pencil_start = ctx_pos * pencil
    decay_part = lax.dynamic_slice_in_dim(decays, pencil_start, pencil, 0)
    weight_part = lax.dynamic_slice_in_dim(residues, pencil_start, pencil, 0)
    length_part = lax.dynamic_slice_in_dim(filter_len, pencil_start, pencil, 0)
    spec_re, spec_im = filter_spectrum(row_count, col_count, decay_part, weight_part, length_part)
    convolved = convolve(signal, spec_re, spec_im, row_count, col_count, win_rows)
    conv_home = lax.all_to_all(
        convolved.astype(jnp.bfloat16), "ctx", split_axis=0, concat_axis=1, tiled=True
    ).astype(convolved.dtype)
    mixed_out = gate_values.astype(jnp.float32) * (
        conv_home + skip_gain[None, :] * window_input.astype(jnp.float32)
    )
    return mixed_out.astype(jnp.bfloat16)


def solution(mesh):
    in_specs = (
        P(("req", "ctx"), "chan"),
        P(("req", "ctx"), "chan"),
        P(("req", "ctx", "chan"), None, None),
        P("req"),
        P("chan"),
        P("chan", None),
        P("chan", None),
        P("chan"),
    )
    out_specs = P(("req", "ctx"), "chan")
    return jax.shard_map(local, mesh=mesh, in_specs=in_specs, out_specs=out_specs, check_vma=False)
```

profile of v0, /device:TPU:4, one launch (start us, length us, event | category | flops | bytes accessed | tf_op | source)
XLA Modules:
  0.0 532.7 jit_solution(3585356285883039196)
XLA Ops:
  4.8 3.1 copy.85
  7.9 12.2 %all-to-all-start = ((bf16[64,2,8,1024]{3,2,1,0:T(8,128)(2,1)}), bf16[64,2,8,1024]{3,2,1,0:T(8,128)(2,1)S(1)}, u32[]{:S(2)}, u32[]{:S(2)}) async-start(bf16[64,2,8,1024]{3,2,1,0:T(8,128)(2,1)} %bitcast.4), calls=%async_computation | async-start | bytes 4194304 | tf_op jit(solution)/shard_map/all_to_all | solution.py:146
  21.8 49.7 %all-to-all-done = bf16[64,2,8,1024]{3,2,1,0:T(8,128)(2,1)S(1)} async-done(((bf16[64,2,8,1024]{3,2,1,0:T(8,128)(2,1)}), bf16[64,2,8,1024]{3,2,1,0:T(8,128)(2,1)S(1)}, u32[]{:S(2)}, u32[]{:S(2)}) %all-to-all-start) | async-done | bytes 2097184 | tf_op jit(solution)/shard_map/all_to_all | solution.py:146
  71.5 3.4 all-to-all-start.2
  75.7 3.2 gather_fusion.1
  81.6 5.7 %all-to-all-done.2 = bf16[128,8,128]{0,2,1:T(8,128)(2,1)S(1)} async-done(((bf16[128,8,128]{0,2,1:T(8,128)(2,1)}), bf16[128,8,128]{0,2,1:T(8,128)(2,1)S(1)}, u32[]{:S(2)}, u32[]{:S(2)}) %all-to-all-start.2) | async-done | bytes 262176 | tf_op jit(solution)/shard_map/all_to_all | solution.py:155
  87.3 4.2 all-to-all-start.1
  91.6 375.7 %while.18 = (s32[]{:T(128)}, f32[40,128,128]{2,1,0:T(8,128)S(1)}, f32[40,128,128]{2,1,0:T(8,128)}, f32[128,16]{0,1:T(8,128)S(1)}, f32[128,16]{0,1:T(8,128)S(1)},...) while((s32[]{:T(128)}, f32[40,128,128]{2,1,0:T(8,128)S(1)}, ...), condition=%wide.region_4.5_spmd.clone.clone.clone, body=%wide.region_3.4_spmd.clone.clone.clone.sunk | while | flops 21653252 | bytes 10599047 | solution.py:77
  91.8 22.4 %fusion.194 = (f32[40,128,128]{2,1,0:T(8,128)}, f32[40,128,128]{2,1,0:T(8,128)S(1)}) fusion(f32[40,128,128]{2,1,0:T(8,128)} %get-tuple-element.421, s32[128]{0:T(128)S(1)} %get-tuple-element.437, s32[40,128]{1,0:T(8,128)S(1)} %get-tuple-element.438, f32[128]{0:T(128)S(1)} %get-tuple-element.398, f32[128]{0:T(128)S(1)} %get-tuple-element.399, ...), kind=kLoop, calls=%fused_computation.18.clone.1 | loop fusion | flops 21626880 | bytes 10551297 | tf_op jit(solution)/shard_map/while/body/eval_jaxpr/add | solution.py:73
  114.4 23.3 %fusion.194 = (f32[40,128,128]{2,1,0:T(8,128)}, f32[40,128,128]{2,1,0:T(8,128)S(1)}) fusion(f32[40,128,128]{2,1,0:T(8,128)} %get-tuple-element.421, s32[128]{0:T(128)S(1)} %get-tuple-element.437, s32[40,128]{1,0:T(8,128)S(1)} %get-tuple-element.438, f32[128]{0:T(128)S(1)} %get-tuple-element.398, f32[128]{0:T(128)S(1)} %get-tuple-element.399, ...), kind=kLoop, calls=%fused_computation.18.clone.1 | loop fusion | flops 21626880 | bytes 10551297 | tf_op jit(solution)/shard_map/while/body/eval_jaxpr/add | solution.py:73
  138.0 23.3 %fusion.194 = (f32[40,128,128]{2,1,0:T(8,128)}, f32[40,128,128]{2,1,0:T(8,128)S(1)}) fusion(f32[40,128,128]{2,1,0:T(8,128)} %get-tuple-element.421, s32[128]{0:T(128)S(1)} %get-tuple-element.437, s32[40,128]{1,0:T(8,128)S(1)} %get-tuple-element.438, f32[128]{0:T(128)S(1)} %get-tuple-element.398, f32[128]{0:T(128)S(1)} %get-tuple-element.399, ...), kind=kLoop, calls=%fused_computation.18.clone.1 | loop fusion | flops 21626880 | bytes 10551297 | tf_op jit(solution)/shard_map/while/body/eval_jaxpr/add | solution.py:73
  161.5 23.3 %fusion.194 = (f32[40,128,128]{2,1,0:T(8,128)}, f32[40,128,128]{2,1,0:T(8,128)S(1)}) fusion(f32[40,128,128]{2,1,0:T(8,128)} %get-tuple-element.421, s32[128]{0:T(128)S(1)} %get-tuple-element.437, s32[40,128]{1,0:T(8,128)S(1)} %get-tuple-element.438, f32[128]{0:T(128)S(1)} %get-tuple-element.398, f32[128]{0:T(128)S(1)} %get-tuple-element.399, ...), kind=kLoop, calls=%fused_computation.18.clone.1 | loop fusion | flops 21626880 | bytes 10551297 | tf_op jit(solution)/shard_map/while/body/eval_jaxpr/add | solution.py:73
  185.0 23.3 %fusion.194 = (f32[40,128,128]{2,1,0:T(8,128)}, f32[40,128,128]{2,1,0:T(8,128)S(1)}) fusion(f32[40,128,128]{2,1,0:T(8,128)} %get-tuple-element.421, s32[128]{0:T(128)S(1)} %get-tuple-element.437, s32[40,128]{1,0:T(8,128)S(1)} %get-tuple-element.438, f32[128]{0:T(128)S(1)} %get-tuple-element.398, f32[128]{0:T(128)S(1)} %get-tuple-element.399, ...), kind=kLoop, calls=%fused_computation.18.clone.1 | loop fusion | flops 21626880 | bytes 10551297 | tf_op jit(solution)/shard_map/while/body/eval_jaxpr/add | solution.py:73
  208.6 23.3 %fusion.194 = (f32[40,128,128]{2,1,0:T(8,128)}, f32[40,128,128]{2,1,0:T(8,128)S(1)}) fusion(f32[40,128,128]{2,1,0:T(8,128)} %get-tuple-element.421, s32[128]{0:T(128)S(1)} %get-tuple-element.437, s32[40,128]{1,0:T(8,128)S(1)} %get-tuple-element.438, f32[128]{0:T(128)S(1)} %get-tuple-element.398, f32[128]{0:T(128)S(1)} %get-tuple-element.399, ...), kind=kLoop, calls=%fused_computation.18.clone.1 | loop fusion | flops 21626880 | bytes 10551297 | tf_op jit(solution)/shard_map/while/body/eval_jaxpr/add | solution.py:73
  232.1 23.3 %fusion.194 = (f32[40,128,128]{2,1,0:T(8,128)}, f32[40,128,128]{2,1,0:T(8,128)S(1)}) fusion(f32[40,128,128]{2,1,0:T(8,128)} %get-tuple-element.421, s32[128]{0:T(128)S(1)} %get-tuple-element.437, s32[40,128]{1,0:T(8,128)S(1)} %get-tuple-element.438, f32[128]{0:T(128)S(1)} %get-tuple-element.398, f32[128]{0:T(128)S(1)} %get-tuple-element.399, ...), kind=kLoop, calls=%fused_computation.18.clone.1 | loop fusion | flops 21626880 | bytes 10551297 | tf_op jit(solution)/shard_map/while/body/eval_jaxpr/add | solution.py:73
  255.7 23.3 %fusion.194 = (f32[40,128,128]{2,1,0:T(8,128)}, f32[40,128,128]{2,1,0:T(8,128)S(1)}) fusion(f32[40,128,128]{2,1,0:T(8,128)} %get-tuple-element.421, s32[128]{0:T(128)S(1)} %get-tuple-element.437, s32[40,128]{1,0:T(8,128)S(1)} %get-tuple-element.438, f32[128]{0:T(128)S(1)} %get-tuple-element.398, f32[128]{0:T(128)S(1)} %get-tuple-element.399, ...), kind=kLoop, calls=%fused_computation.18.clone.1 | loop fusion | flops 21626880 | bytes 10551297 | tf_op jit(solution)/shard_map/while/body/eval_jaxpr/add | solution.py:73
  279.2 23.3 %fusion.194 = (f32[40,128,128]{2,1,0:T(8,128)}, f32[40,128,128]{2,1,0:T(8,128)S(1)}) fusion(f32[40,128,128]{2,1,0:T(8,128)} %get-tuple-element.421, s32[128]{0:T(128)S(1)} %get-tuple-element.437, s32[40,128]{1,0:T(8,128)S(1)} %get-tuple-element.438, f32[128]{0:T(128)S(1)} %get-tuple-element.398, f32[128]{0:T(128)S(1)} %get-tuple-element.399, ...), kind=kLoop, calls=%fused_computation.18.clone.1 | loop fusion | flops 21626880 | bytes 10551297 | tf_op jit(solution)/shard_map/while/body/eval_jaxpr/add | solution.py:73
  302.7 23.3 %fusion.194 = (f32[40,128,128]{2,1,0:T(8,128)}, f32[40,128,128]{2,1,0:T(8,128)S(1)}) fusion(f32[40,128,128]{2,1,0:T(8,128)} %get-tuple-element.421, s32[128]{0:T(128)S(1)} %get-tuple-element.437, s32[40,128]{1,0:T(8,128)S(1)} %get-tuple-element.438, f32[128]{0:T(128)S(1)} %get-tuple-element.398, f32[128]{0:T(128)S(1)} %get-tuple-element.399, ...), kind=kLoop, calls=%fused_computation.18.clone.1 | loop fusion | flops 21626880 | bytes 10551297 | tf_op jit(solution)/shard_map/while/body/eval_jaxpr/add | solution.py:73
  326.3 23.3 %fusion.194 = (f32[40,128,128]{2,1,0:T(8,128)}, f32[40,128,128]{2,1,0:T(8,128)S(1)}) fusion(f32[40,128,128]{2,1,0:T(8,128)} %get-tuple-element.421, s32[128]{0:T(128)S(1)} %get-tuple-element.437, s32[40,128]{1,0:T(8,128)S(1)} %get-tuple-element.438, f32[128]{0:T(128)S(1)} %get-tuple-element.398, f32[128]{0:T(128)S(1)} %get-tuple-element.399, ...), kind=kLoop, calls=%fused_computation.18.clone.1 | loop fusion | flops 21626880 | bytes 10551297 | tf_op jit(solution)/shard_map/while/body/eval_jaxpr/add | solution.py:73
  349.8 23.3 %fusion.194 = (f32[40,128,128]{2,1,0:T(8,128)}, f32[40,128,128]{2,1,0:T(8,128)S(1)}) fusion(f32[40,128,128]{2,1,0:T(8,128)} %get-tuple-element.421, s32[128]{0:T(128)S(1)} %get-tuple-element.437, s32[40,128]{1,0:T(8,128)S(1)} %get-tuple-element.438, f32[128]{0:T(128)S(1)} %get-tuple-element.398, f32[128]{0:T(128)S(1)} %get-tuple-element.399, ...), kind=kLoop, calls=%fused_computation.18.clone.1 | loop fusion | flops 21626880 | bytes 10551297 | tf_op jit(solution)/shard_map/while/body/eval_jaxpr/add | solution.py:73
  373.3 23.3 %fusion.194 = (f32[40,128,128]{2,1,0:T(8,128)}, f32[40,128,128]{2,1,0:T(8,128)S(1)}) fusion(f32[40,128,128]{2,1,0:T(8,128)} %get-tuple-element.421, s32[128]{0:T(128)S(1)} %get-tuple-element.437, s32[40,128]{1,0:T(8,128)S(1)} %get-tuple-element.438, f32[128]{0:T(128)S(1)} %get-tuple-element.398, f32[128]{0:T(128)S(1)} %get-tuple-element.399, ...), kind=kLoop, calls=%fused_computation.18.clone.1 | loop fusion | flops 21626880 | bytes 10551297 | tf_op jit(solution)/shard_map/while/body/eval_jaxpr/add | solution.py:73
  396.9 23.3 %fusion.194 = (f32[40,128,128]{2,1,0:T(8,128)}, f32[40,128,128]{2,1,0:T(8,128)S(1)}) fusion(f32[40,128,128]{2,1,0:T(8,128)} %get-tuple-element.421, s32[128]{0:T(128)S(1)} %get-tuple-element.437, s32[40,128]{1,0:T(8,128)S(1)} %get-tuple-element.438, f32[128]{0:T(128)S(1)} %get-tuple-element.398, f32[128]{0:T(128)S(1)} %get-tuple-element.399, ...), kind=kLoop, calls=%fused_computation.18.clone.1 | loop fusion | flops 21626880 | bytes 10551297 | tf_op jit(solution)/shard_map/while/body/eval_jaxpr/add | solution.py:73
  420.4 23.3 %fusion.194 = (f32[40,128,128]{2,1,0:T(8,128)}, f32[40,128,128]{2,1,0:T(8,128)S(1)}) fusion(f32[40,128,128]{2,1,0:T(8,128)} %get-tuple-element.421, s32[128]{0:T(128)S(1)} %get-tuple-element.437, s32[40,128]{1,0:T(8,128)S(1)} %get-tuple-element.438, f32[128]{0:T(128)S(1)} %get-tuple-element.398, f32[128]{0:T(128)S(1)} %get-tuple-element.399, ...), kind=kLoop, calls=%fused_computation.18.clone.1 | loop fusion | flops 21626880 | bytes 10551297 | tf_op jit(solution)/shard_map/while/body/eval_jaxpr/add | solution.py:73
  443.9 23.3 %fusion.194 = (f32[40,128,128]{2,1,0:T(8,128)}, f32[40,128,128]{2,1,0:T(8,128)S(1)}) fusion(f32[40,128,128]{2,1,0:T(8,128)} %get-tuple-element.421, s32[128]{0:T(128)S(1)} %get-tuple-element.437, s32[40,128]{1,0:T(8,128)S(1)} %get-tuple-element.438, f32[128]{0:T(128)S(1)} %get-tuple-element.398, f32[128]{0:T(128)S(1)} %get-tuple-element.399, ...), kind=kLoop, calls=%fused_computation.18.clone.1 | loop fusion | flops 21626880 | bytes 10551297 | tf_op jit(solution)/shard_map/while/body/eval_jaxpr/add | solution.py:73
  469.9 3.2 reshape.358
  488.5 3.8 fusion.35
  492.3 2.9 fusion.59
  500.7 4.0 fusion.34
  504.7 3.1 fusion.28
  507.8 2.8 fusion.39
  511.4 7.1 %all-to-all-start.3 = ((bf16[8,128,128]{2,1,0:T(8,128)(2,1)}), bf16[8,128,128]{2,1,0:T(8,128)(2,1)S(1)}, u32[]{:S(2)}, u32[]{:S(2)}) async-start(bf16[8,128,128]{2,1,0:T(8,128)(2,1)} %copy.93), calls=%async_computation.3 | async-start | bytes 524288 | tf_op jit(solution)/shard_map/all_to_all | solution.py:167
  518.7 11.6 %all-to-all-done.3 = bf16[8,128,128]{2,1,0:T(8,128)(2,1)S(1)} async-done(((bf16[8,128,128]{2,1,0:T(8,128)(2,1)}), bf16[8,128,128]{2,1,0:T(8,128)(2,1)S(1)}, u32[]{:S(2)}, u32[]{:S(2)}) %all-to-all-start.3) | async-done | bytes 262176 | tf_op jit(solution)/shard_map/all_to_all | solution.py:167
  (124 shorter events, 39.3 us)
Async XLA Ops:
  0.0 2.7 copy-start
  7.9 12.2 %copy-start.5 = (bf16[128,1024]{1,0:T(8,128)(2,1)S(1)}, bf16[128,1024]{1,0:T(8,128)(2,1)}, u32[]{:S(2)}) copy-start(bf16[128,1024]{1,0:T(8,128)(2,1)} %param.10) | copy-start | bytes 786436
  7.9 63.6 %all-to-all-start = ((bf16[64,2,8,1024]{3,2,1,0:T(8,128)(2,1)}), bf16[64,2,8,1024]{3,2,1,0:T(8,128)(2,1)S(1)}, u32[]{:S(2)}, u32[]{:S(2)}) async-start(bf16[64,2,8,1024]{3,2,1,0:T(8,128)(2,1)} %bitcast.4), calls=%async_computation | async-start | bytes 4194304 | tf_op jit(solution)/shard_map/all_to_all | solution.py:146
  71.5 3.4 copy-start.4
  71.5 15.8 %all-to-all-start.2 = ((bf16[128,8,128]{0,2,1:T(8,128)(2,1)}), bf16[128,8,128]{0,2,1:T(8,128)(2,1)S(1)}, u32[]{:S(2)}, u32[]{:S(2)}) async-start(bf16[128,8,128]{0,2,1:T(8,128)(2,1)} %bitcast.10), calls=%async_computation.2 | async-start | bytes 524288 | tf_op jit(solution)/shard_map/all_to_all | solution.py:155
  87.3 380.2 %all-to-all-start.1 = ((bf16[512,8,128]{2,0,1:T(8,128)(2,1)}), bf16[512,8,128]{2,0,1:T(8,128)(2,1)}, u32[]{:S(2)}, u32[]{:S(2)}) async-start(bf16[512,8,128]{2,0,1:T(8,128)(2,1)} %copy.86), calls=%async_computation.1 | async-start | bytes 2097152 | tf_op jit(solution)/shard_map/all_to_all | solution.py:154
  473.2 2.0 copy-start.3
  485.7 2.8 copy-start.2
  507.8 10.7 %copy-start.6 = (bf16[128,1024]{1,0:T(8,128)(2,1)S(1)}, bf16[128,1024]{1,0:T(8,128)(2,1)}, u32[]{:S(2)}) copy-start(bf16[128,1024]{1,0:T(8,128)(2,1)} %param.11) | copy-start | bytes 786436
  507.8 22.6 %copy-start.7 = (f32[1024]{0:T(1024)S(1)}, f32[1024]{0:T(1024)}, u32[]{:S(2)}) copy-start(f32[1024]{0:T(1024)} %param.17) | copy-start | bytes 12292
  507.8 24.7 %copy-start.1 = (bf16[16,8,8192]{2,1,0:T(8,128)(2,1)S(1)}, bf16[16,8,8192]{2,1,0:T(8,128)(2,1)}, u32[]{:S(2)}) copy-start(bf16[16,8,8192]{2,1,0:T(8,128)(2,1)} %param.12) | copy-start | bytes 6291460
  511.4 18.8 %all-to-all-start.3 = ((bf16[8,128,128]{2,1,0:T(8,128)(2,1)}), bf16[8,128,128]{2,1,0:T(8,128)(2,1)S(1)}, u32[]{:S(2)}, u32[]{:S(2)}) async-start(bf16[8,128,128]{2,1,0:T(8,128)(2,1)} %copy.93), calls=%async_computation.3 | async-start | bytes 524288 | tf_op jit(solution)/shard_map/all_to_all | solution.py:167
where the time goes:
time: 541 us; the launch traced here: 533 us
  other arithmetic  383 us (71%)
  waiting for transfers between devices  67.1 us (12%)
  matrix products  34.2 us (6%)
  starting transfers between devices  27 us (5%)
  local copies, waits for them, and re-layouts  20.3 us (4%)
    add x16, other arithmetic, add_mode(): spec_im = spec_im + mode_scale * (num_im * den_re - num_re * den_im)  372 us
    all_to_all x1, waiting for transfers between devices, local(): lax.all_to_all(parcel, ('ctx', 'chan'), split_axis=0, concat_axis=0, tile...  49.7 us
    all_to_all x1, starting transfers between devices, local(): lax.all_to_all(parcel, ('ctx', 'chan'), split_axis=0, concat_axis=0, tile...  12.2 us
    all_to_all x1, waiting for transfers between devices, local(): lax.all_to_all(convolved.astype(jnp.bfloat16), 'ctx', split_axis=0, conca...  11.6 us
  transfers between devices with their start and end apart: 4, of which 3 were waited for; matrix products, arithmetic and copies ran while one was open for 72% of the time, Pallas kernels for 0%

commit v1 on v0

v1 whole, which is shorter than its diff:
```python
import functools

import jax
import jax.numpy as jnp
from jax import lax
from jax.experimental import pallas as pl
from jax.experimental.pallas import tpu as pltpu
from jax.sharding import PartitionSpec as P

LANES = 128
SUBS = 8
VMEM_LIMIT = 32 * 1024 * 1024


def row(ref, index):
    return jnp.broadcast_to(ref[index : index + 1, :], (SUBS, LANES))


def shift_down(value, count):
    moved = pltpu.roll(value, count, 0)
    rows = lax.broadcasted_iota(jnp.int32, value.shape, 0)
    return jnp.where(rows >= count, moved, 0.0)


def segment_states(read, steps, lam):
    def body(step, states):
        value = read(step)
        return tuple(s * l + value for s, l in zip(states, lam))

    zero = jnp.zeros((SUBS, LANES), jnp.float32)
    return lax.fori_loop(0, steps, body, tuple(zero for _ in lam), unroll=4)


def exclusive_scan(end, decay, steps):
    total = end
    for count in (1, 2, 4):
        total = total + jnp.exp(-decay * float(steps * count)) * shift_down(total, count)
    return shift_down(total, 1)


def segment_outputs(read, write, steps, lam, gain, begin):
    def body(step, states):
        value = read(step)
        new = tuple(s * l + g * value for s, l, g in zip(states, lam, gain))
        parts = list(new)
        while len(parts) > 1:
            parts = [a + b for a, b in zip(parts[::2], parts[1::2])]
        write(step, parts[0])
        return new

    lax.fori_loop(0, steps, body, tuple(begin), unroll=4)


def window_kernel(modes, steps, window_ref, decay_ref, weight_ref, out_ref, signal):
    signal[...] = window_ref[...].astype(jnp.float32)
    decay = [row(decay_ref, r) for r in range(modes)]
    lam = [jnp.exp(-d) for d in decay]

    def read(step):
        return signal[pl.ds(step, SUBS, stride=steps), :]

    def write(step, value):
        out_ref[pl.ds(step, SUBS, stride=steps), :] = value

    ends = segment_states(read, steps, lam)
    gain = [row(weight_ref, r) for r in range(modes)]
    begin = [
        gain[r] * exclusive_scan(ends[r], row(decay_ref, r), steps) for r in range(modes)
    ]
    segment_outputs(read, write, steps, lam, gain, begin)


def cache_kernel(
    modes,
    steps,
    slots_ref,
    pages_ref,
    length_ref,
    decay_ref,
    weight_ref,
    window_part_ref,
    out_ref,
    signal,
    result,
):
    page_count = slots_ref.shape[0]
    cached = page_count * SUBS
    rows = lax.broadcasted_iota(jnp.int32, (SUBS, LANES), 0)
    length = jnp.broadcast_to(length_ref[...], (SUBS, LANES))
    first = cached - length

    lam_page = [jnp.exp(-float(SUBS) * row(decay_ref, r)) for r in range(modes)]

    def scan_page(page, states):
        value = pages_ref[slots_ref[page]].astype(jnp.float32)
        start = pl.multiple_of(page * SUBS, SUBS)
        signal[pl.ds(start, SUBS), :] = value
        value = jnp.where(rows + page * SUBS > first, value, 0.0)
        return tuple(s * l + value for s, l in zip(states, lam_page))

    zero = jnp.zeros((SUBS, LANES), jnp.float32)
    states = lax.fori_loop(0, page_count, scan_page, tuple(zero for _ in range(modes)), unroll=4)
    rows_float = rows.astype(jnp.float32)
    history = []
    for r in range(modes):
        decay = row(decay_ref, r)
        weighted = states[r] * jnp.exp(-decay * (float(SUBS - 1) - rows_float))
        total = jnp.sum(weighted, axis=0, keepdims=True)
        history.append(jnp.broadcast_to(total, (SUBS, LANES)) * row(weight_ref, r))

    window = steps * SUBS
    shift = cached // 2
    reach = cached - window
    while shift >= 1:
        keep = window + min(shift - 1, reach) if shift > 1 else window
        keep = min(keep, cached - shift)
        size = 128 if shift >= 128 else 64 if shift >= 64 else 32 if shift >= 32 else 16 if shift >= 16 else 8
        chunk = min(size, 64)
        count = -(-keep // chunk)
        wide = (jnp.broadcast_to(first[0:1, :], (chunk, LANES)) & shift) != 0

        def move(index, carry, chunk=chunk, wide=wide, shift=shift):
            start = pl.multiple_of(index * chunk, chunk)
            near = signal[pl.ds(start, chunk), :]
            far = signal[pl.ds(start + shift, chunk), :]
            signal[pl.ds(start, chunk), :] = jnp.where(wide, far, near)
            return carry

        lax.fori_loop(0, count, move, 0)
        shift //= 2
    signal[0:SUBS, :] = jnp.where(rows > 0, signal[0:SUBS, :], 0.0)

    lam = [jnp.exp(-row(decay_ref, r)) for r in range(modes)]

    def read(step):
        return signal[pl.ds(step, SUBS, stride=steps), :]

    def write(step, value):
        result[pl.ds(step, SUBS, stride=steps), :] = value

    ends = segment_states(read, steps, lam)
    length_float = length.astype(jnp.float32)
    gain = [
        -row(weight_ref, r) * jnp.exp(-row(decay_ref, r) * length_float) for r in range(modes)
    ]
    begin = []
    for r in range(modes):
        decay = row(decay_ref, r)
        from_cache = history[r] * jnp.exp(-decay * (float(steps) * rows_float))
        begin.append(from_cache + gain[r] * exclusive_scan(ends[r], decay, steps))
    segment_outputs(read, write, steps, lam, gain, begin)
    out_ref[...] = (result[...] + window_part_ref[...]).astype(jnp.bfloat16)


def gate_kernel(conv_ref, window_ref, gate_ref, skip_ref, out_ref):
    for block in range(conv_ref.shape[0]):
        lanes = slice(block * LANES, (block + 1) * LANES)
        mixed = conv_ref[block].astype(jnp.float32) + skip_ref[:, lanes] * window_ref[
            :, lanes
        ].astype(jnp.float32)
        out_ref[:, lanes] = (gate_ref[:, lanes].astype(jnp.float32) * mixed).astype(jnp.bfloat16)


def vmem(count):
    return [pl.BlockSpec(memory_space=pltpu.VMEM) for _ in range(count)]


def params():
    return pltpu.CompilerParams(vmem_limit_bytes=VMEM_LIMIT)


def window_conv(window_seq, decay, weight):
    window = window_seq.shape[0]
    modes = decay.shape[0]
    return pl.pallas_call(
        functools.partial(window_kernel, modes, window // SUBS),
        out_shape=jax.ShapeDtypeStruct((window, LANES), jnp.float32),
        in_specs=vmem(3),
        out_specs=pl.BlockSpec(memory_space=pltpu.VMEM),
        scratch_shapes=[pltpu.VMEM((window, LANES), jnp.float32)],
        compiler_params=params(),
        cost_estimate=pl.CostEstimate(
            flops=12 * window * LANES * modes, bytes_accessed=6 * window * LANES, transcendentals=0
        ),
        name="window_conv",
    )(window_seq, decay, weight)


def cache_conv(slots, pages, length, decay, weight, window_part):
    window = window_part.shape[0]
    modes = decay.shape[0]
    cached = slots.shape[0] * SUBS
    return pl.pallas_call(
        functools.partial(cache_kernel, modes, window // SUBS),
        out_shape=jax.ShapeDtypeStruct((window, LANES), jnp.bfloat16),
        in_specs=[pl.BlockSpec(memory_space=pltpu.SMEM)] + vmem(5),
        out_specs=pl.BlockSpec(memory_space=pltpu.VMEM),
        scratch_shapes=[
            pltpu.VMEM((cached + 64, LANES), jnp.float32),
            pltpu.VMEM((window, LANES), jnp.float32),
        ],
        compiler_params=params(),
        cost_estimate=pl.CostEstimate(
            flops=4 * cached * LANES * modes, bytes_accessed=4 * cached * LANES, transcendentals=0
        ),
        name="cache_conv",
    )(slots, pages, length, decay, weight, window_part)


def gate_out(conv_home, window_input, gate_values, skip_gain):
    return pl.pallas_call(
        gate_kernel,
        out_shape=jax.ShapeDtypeStruct(gate_values.shape, jnp.bfloat16),
        in_specs=vmem(4),
        out_specs=pl.BlockSpec(memory_space=pltpu.VMEM),
        compiler_params=params(),
        name="gate_out",
    )(conv_home, window_input, gate_values, skip_gain)


def local(
    window_input, gate_values, page_pool, page_table, filter_len, residues, decays, skip_gain
):
    ctx_count = lax.axis_size("ctx")
    chan_count = lax.axis_size("chan")
    ctx_pos = lax.axis_index("ctx")
    pool_pages, page_len, width = page_pool.shape
    pencil = window_input.shape[1] // ctx_count
    parcel = jnp.transpose(page_pool.reshape(pool_pages, page_len, -1, pencil), (2, 0, 1, 3))
    arrived = lax.all_to_all(parcel, ("chan", "ctx"), split_axis=0, concat_axis=0, tiled=True)
    arrived = arrived.reshape(-1, page_len, pencil)
    window_seq = lax.all_to_all(window_input, "ctx", split_axis=1, concat_axis=0, tiled=True)
    owners = page_table // pool_pages
    source = (owners % chan_count) * ctx_count + owners // chan_count
    slots = source * pool_pages + page_table % pool_pages
    start = ctx_pos * pencil
    decay = lax.dynamic_slice_in_dim(decays, start, pencil, 0).T
    weight = lax.dynamic_slice_in_dim(residues, start, pencil, 0).T
    length = lax.dynamic_slice_in_dim(filter_len, start, pencil, 0)[None, :]
    window_part = window_conv(window_seq, decay, weight)
    convolved = cache_conv(slots, arrived, length, decay, weight, window_part)
    conv_home = lax.all_to_all(
        convolved.reshape(ctx_count, -1, pencil), "ctx", split_axis=0, concat_axis=0, tiled=True
    )
    return gate_out(conv_home, window_input, gate_values, skip_gain[None, :])


def solution(mesh):
    in_specs = (
        P(("req", "ctx"), "chan"),
        P(("req", "ctx"), "chan"),
        P(("req", "ctx", "chan"), None, None),
        P("req"),
        P("chan"),
        P("chan", None),
        P("chan", None),
        P("chan"),
    )
    out_specs = P(("req", "ctx"), "chan")
    return jax.shard_map(local, mesh=mesh, in_specs=in_specs, out_specs=out_specs, check_vma=False)
```

time: 541 us -> 109 us (0.20); the launches traced: 533 us -> 108 us
  other arithmetic: 383 us -> 0.02 us
  matrix products: 34.2 us -> 0 us
  blocking collectives: 0 us -> 17.2 us
  Pallas kernels: 0 us -> 15.7 us
  local copies, waits for them, and re-layouts: 20.3 us -> 5.27 us
  starting transfers between devices: 27 us -> 14.2 us
  waiting for transfers between devices: 67.1 us -> 55.6 us
    add x19 -> x1, other arithmetic: 374 us -> 0.02 us  [local(): slots = source * pool_pages + page_table % pool_pages]
    dot_general x14 -> x0, matrix products: 34.2 us -> none  [the longest x1 3.99 us: convolve(): jnp.einsum('adc,db->abc', product_re, sin_cols, precision=precise)]
    all_to_all x3 -> x1, starting transfers between devices: 23.6 us -> 5.74 us  [local(): lax.all_to_all(parcel, ('chan', 'ctx'), split_axis=0, concat_axis=0, tile...]
    all_to_all x0 -> x1, blocking collectives: none -> 17.2 us  [local(): lax.all_to_all(convolved.reshape(ctx_count, -1, pencil), 'ctx', split_axi...]
    pallas_call x0 -> x3, Pallas kernels: none -> 15.7 us  [the longest x1 12.3 us: cache_conv(): pl.pallas_call(functools.partial(cache_kernel, modes, window // SUBS), ou...]
    all_to_all x3 -> x1, waiting for transfers between devices: 61.3 us -> 45.6 us  [local(): lax.all_to_all(parcel, ('chan', 'ctx'), split_axis=0, concat_axis=0, tile...]
  transfers between devices with their start and end apart: 4 -> 2, of which waited for: 3 -> 2; matrix products, arithmetic and copies ran while one was open for 72% -> 3% of each run, Pallas kernels for 0% -> 2%
where the time goes in v1:
time: 109 us; the launch traced here: 108 us
  waiting for transfers between devices  55.6 us (51%)
  blocking collectives  17.2 us (16%)
  Pallas kernels  15.7 us (14%)
  starting transfers between devices  14.2 us (13%)
  local copies, waits for them, and re-layouts  5.27 us (5%)
    all_to_all x1, waiting for transfers between devices, local(): lax.all_to_all(parcel, ('chan', 'ctx'), split_axis=0, concat_axis=0, tile...  45.6 us
    all_to_all x1, blocking collectives, local(): lax.all_to_all(convolved.reshape(ctx_count, -1, pencil), 'ctx', split_axi...  17.2 us
    pallas_call x1, Pallas kernels, cache_conv(): pl.pallas_call(functools.partial(cache_kernel, modes, window // SUBS), ou...  12.3 us
    all_to_all x1, waiting for transfers between devices, local(): lax.all_to_all(window_input, 'ctx', split_axis=1, concat_axis=0, tiled=True)  9.96 us
    all_to_all x1, starting transfers between devices, local(): lax.all_to_all(window_input, 'ctx', split_axis=1, concat_axis=0, tiled=True)  8.47 us
    all_to_all x1, starting transfers between devices, local(): lax.all_to_all(parcel, ('chan', 'ctx'), split_axis=0, concat_axis=0, tile...  5.74 us
    pallas_call x1, Pallas kernels, window_conv(): pl.pallas_call(functools.partial(window_kernel, modes, window // SUBS), o...  2.62 us
  transfers between devices with their start and end apart: 2, of which 2 were waited for; matrix products, arithmetic and copies ran while one was open for 3% of the time, Pallas kernels for 2%

profile of v1, /device:TPU:4, one launch (start us, length us, event | category | flops | bytes accessed | tf_op | source)
XLA Modules:
  0.0 108.1 jit_solution(14866736282646731770)
XLA Ops:
  0.0 0.0 copy-start
  0.0 1.8 %copy_bitcast_fusion.1 = bf16[128,8,128]{2,0,1:T(8,128)(2,1)} fusion(bf16[128,1024]{1,0:T(8,128)(2,1)} %window_ref.1), kind=kLoop, calls=%fused_computation.1 | loop fusion | bytes 524288 | tf_op jit(solution)/shard_map/all_to_all | solution.py:232
  1.9 8.5 %all-to-all-start.1 = ((bf16[128,8,128]{2,0,1:T(8,128)(2,1)}), bf16[128,8,128]{2,0,1:T(8,128)(2,1)S(1)}, u32[]{:S(2)}, u32[]{:S(2)}) async-start(bf16[128,8,128]{2,0,1:T(8,128)(2,1)} %copy_bitcast_fusion.1), calls=%async_computation.1 | async-start | bytes 524288 | tf_op jit(solution)/shard_map/all_to_all | solution.py:232
  10.3 0.0 copy-done
  10.3 1.9 %copy_bitcast_fusion = bf16[64,16,8,128]{3,2,1,0:T(8,128)(2,1)} fusion(bf16[16,8,8192]{2,1,0:T(8,128)(2,1)S(1)} %copy-done), kind=kLoop, calls=%fused_computation | loop fusion | bytes 4194304 | tf_op jit(solution)/shard_map/transpose | solution.py:229
  12.2 0.0 copy-start.4
  12.2 10.0 %all-to-all-done.1 = bf16[128,8,128]{2,0,1:T(8,128)(2,1)S(1)} async-done(((bf16[128,8,128]{2,0,1:T(8,128)(2,1)}), bf16[128,8,128]{2,0,1:T(8,128)(2,1)S(1)}, u32[]{:S(2)}, u32[]{:S(2)}) %all-to-all-start.1) | async-done | bytes 262176 | tf_op jit(solution)/shard_map/all_to_all | solution.py:232
  22.2 5.7 %all-to-all-start = ((bf16[64,16,8,128]{3,2,1,0:T(8,128)(2,1)}), bf16[64,16,8,128]{3,2,1,0:T(8,128)(2,1)}, u32[]{:S(2)}, u32[]{:S(2)}) async-start(bf16[64,16,8,128]{3,2,1,0:T(8,128)(2,1)} %copy_bitcast_fusion), calls=%async_computation | async-start | bytes 4194304 | tf_op jit(solution)/shard_map/all_to_all | solution.py:230
  28.0 0.8 dynamic-slice_bitcast_fusion.2.length_ref
  28.7 0.7 dynamic-slice_bitcast_fusion
  29.4 0.0 copy-done.4
  29.5 0.0 copy-start.1
  29.5 0.0 copy-start.2
  29.5 0.0 copy-start.3
  29.5 2.6 %window_conv.1.window_part_ref = f32[1024,128]{1,0:T(8,128)S(1)} custom-call(bf16[1024,128]{1,0:T(8,128)(2,1)S(1)} %bitcast.22, f32[16,128]{1,0:T(8,128)S(1)} %get-tuple-element.6.decay_ref, f32[16,128]{1,0:T(8,128)S(1)} %get-tuple-element.5.weight_ref), custom_call_target="tpu_custom_call" | custom-call | flops 25165824 | bytes 786432 | tf_op jit(solution)/shard_map/window_conv/pallas_call | solution.py:175
  32.1 45.6 %all-to-all-done = bf16[64,16,8,128]{3,2,1,0:T(8,128)(2,1)} async-done(((bf16[64,16,8,128]{3,2,1,0:T(8,128)(2,1)}), bf16[64,16,8,128]{3,2,1,0:T(8,128)(2,1)}, u32[]{:S(2)}, u32[]{:S(2)}) %all-to-all-start) | async-done | bytes 2097184 | tf_op jit(solution)/shard_map/all_to_all | solution.py:230
  77.8 12.3 %cache_conv.1 = bf16[1024,128]{1,0:T(8,128)(2,1)S(1)} custom-call(s32[512]{0:T(512)S(1)} %fusion.3.slots_ref, bf16[1024,8,128]{2,1,0:T(8,128)(2,1)} %bitcast.2.pages_ref, s32[1,128]{1,0:T(1,128)S(1)} %dynamic-slice_bitcast_fusion.2.length_ref, f32[16,128]{1,0:T(8,128)S(1)} %get-tuple-element.6.decay_ref, f32[16,128]{1,0:T(8,128)S(1)} %get-tuple-element.5.weight_ref, ...), custom_call_target="tpu_custom_call" | custom-call | flops 33554432 | bytes 2097152 | tf_op jit(solution)/shard_map/cache_conv/pallas_call | solution.py:193
  90.0 17.2 %all_to_all.29.conv_ref = bf16[8,128,128]{2,1,0:T(8,128)(2,1)S(1)} all-to-all(bf16[8,128,128]{2,1,0:T(8,128)(2,1)S(1)} %bitcast.23), channel_id=1, replica_groups=mesh['ctx'=8,'chan'=8,'req'=4] {'ctx'}, dimensions={0} | all-to-all | bytes 524288 | tf_op jit(solution)/shard_map/all_to_all | solution.py:242
  107.2 0.0 copy-done.1
  107.2 0.0 copy-done.2
  107.2 0.0 copy-done.3
  107.2 0.8 gate_out.1
  (1 shorter events, 0.0 us)
Async XLA Ops:
  0.0 10.3 %copy-start = (bf16[16,8,8192]{2,1,0:T(8,128)(2,1)S(1)}, bf16[16,8,8192]{2,1,0:T(8,128)(2,1)}, u32[]{:S(2)}) copy-start(bf16[16,8,8192]{2,1,0:T(8,128)(2,1)} %param.10) | copy-start | bytes 6291460
  1.9 20.3 %all-to-all-start.1 = ((bf16[128,8,128]{2,0,1:T(8,128)(2,1)}), bf16[128,8,128]{2,0,1:T(8,128)(2,1)S(1)}, u32[]{:S(2)}, u32[]{:S(2)}) async-start(bf16[128,8,128]{2,0,1:T(8,128)(2,1)} %copy_bitcast_fusion.1), calls=%async_computation.1 | async-start | bytes 524288 | tf_op jit(solution)/shard_map/all_to_all | solution.py:232
  12.2 17.2 %copy-start.4 = (s32[512]{0:T(512)S(1)}, s32[512]{0:T(512)}, u32[]{:S(2)}) copy-start(s32[512]{0:T(512)} %param.11) | copy-start | bytes 6148
  22.2 55.6 %all-to-all-start = ((bf16[64,16,8,128]{3,2,1,0:T(8,128)(2,1)}), bf16[64,16,8,128]{3,2,1,0:T(8,128)(2,1)}, u32[]{:S(2)}, u32[]{:S(2)}) async-start(bf16[64,16,8,128]{3,2,1,0:T(8,128)(2,1)} %copy_bitcast_fusion), calls=%async_computation | async-start | bytes 4194304 | tf_op jit(solution)/shard_map/all_to_all | solution.py:230
  29.5 77.8 %copy-start.1 = (bf16[128,1024]{1,0:T(8,128)(2,1)S(1)}, bf16[128,1024]{1,0:T(8,128)(2,1)}, u32[]{:S(2)}) copy-start(bf16[128,1024]{1,0:T(8,128)(2,1)} %window_ref.1) | copy-start | bytes 786436
  29.5 77.8 %copy-start.2 = (bf16[128,1024]{1,0:T(8,128)(2,1)S(1)}, bf16[128,1024]{1,0:T(8,128)(2,1)}, u32[]{:S(2)}) copy-start(bf16[128,1024]{1,0:T(8,128)(2,1)} %gate_ref.1) | copy-start | bytes 786436
  29.5 77.7 %copy-start.3 = (f32[1024]{0:T(1024)S(1)}, f32[1024]{0:T(1024)}, u32[]{:S(2)}) copy-start(f32[1024]{0:T(1024)} %param.15) | copy-start | bytes 12292

commit v2 on v1

--- a/solution.py
+++ b/solution.py
@@ -31,11 +31,11 @@
     return lax.fori_loop(0, steps, body, tuple(zero for _ in lam), unroll=4)
 
 
-def exclusive_scan(end, decay, steps):
+def inclusive_scan(end, decay, steps):
     total = end
     for count in (1, 2, 4):
         total = total + jnp.exp(-decay * float(steps * count)) * shift_down(total, count)
-    return shift_down(total, 1)
+    return total
 
 
 def segment_outputs(read, write, steps, lam, gain, begin):
@@ -51,23 +51,63 @@
     lax.fori_loop(0, steps, body, tuple(begin), unroll=4)
 
 
-def window_kernel(modes, steps, window_ref, decay_ref, weight_ref, out_ref, signal):
-    signal[...] = window_ref[...].astype(jnp.float32)
-    decay = [row(decay_ref, r) for r in range(modes)]
-    lam = [jnp.exp(-d) for d in decay]
-
-    def read(step):
-        return signal[pl.ds(step, SUBS, stride=steps), :]
-
-    def write(step, value):
-        out_ref[pl.ds(step, SUBS, stride=steps), :] = value
-
-    ends = segment_states(read, steps, lam)
-    gain = [row(weight_ref, r) for r in range(modes)]
-    begin = [
-        gain[r] * exclusive_scan(ends[r], row(decay_ref, r), steps) for r in range(modes)
-    ]
-    segment_outputs(read, write, steps, lam, gain, begin)
+def window_kernel(modes, steps, window_ref, decay_ref, weight_ref, skip_ref, base_ref, end_ref, signal, result):
+    tiles = window_ref.shape[1] // LANES
+
+    def tile(index, carry):
+        lanes = pl.ds(pl.multiple_of(index * LANES, LANES), LANES)
+
+        def wide(ref, r):
+            return jnp.broadcast_to(ref[r : r + 1, lanes], (SUBS, LANES))
+
+        signal[...] = window_ref[:, lanes].astype(jnp.float32)
+        lam = [jnp.exp(-wide(decay_ref, r)) for r in range(modes)]
+        skip = wide(skip_ref, 0)
+
+        def read(step):
+            return signal[pl.ds(step, SUBS, stride=steps), :]
+
+        def write(step, value):
+            result[pl.ds(step, SUBS, stride=steps), :] = value + skip * read(step)
+
+        ends = segment_states(read, steps, lam)
+        gain = [wide(weight_ref, r) for r in range(modes)]
+        begin = []
+        for r in range(modes):
+            total = inclusive_scan(ends[r], wide(decay_ref, r), steps)
+            end_ref[r : r + 1, lanes] = total[SUBS - 1 : SUBS, :]
+            begin.append(gain[r] * shift_down(total, 1))
+        segment_outputs(read, write, steps, lam, gain, begin)
+        base_ref[:, lanes] = result[...]
+        return carry
+
+    lax.fori_loop(0, tiles, tile, 0)
+
+
+def carry_kernel(modes, base_ref, state_ref, decay_ref, weight_ref, out_ref):
+    tiles = base_ref.shape[1] // LANES
+    ahead = lax.broadcasted_iota(jnp.int32, (SUBS, LANES), 0).astype(jnp.float32) + 1.0
+
+    def tile(index, carry):
+        lanes = pl.ds(pl.multiple_of(index * LANES, LANES), LANES)
+
+        def wide(ref, r):
+            return jnp.broadcast_to(ref[r : r + 1, lanes], (SUBS, LANES))
+
+        term = [
+            wide(weight_ref, r) * wide(state_ref, r) * jnp.exp(-wide(decay_ref, r) * ahead)
+            for r in range(modes)
+        ]
+        lam = [jnp.exp(-float(SUBS) * wide(decay_ref, r)) for r in range(modes)]
+        for first in range(0, base_ref.shape[0], SUBS):
+            parts = list(term)
+            while len(parts) > 1:
+                parts = [a + b for a, b in zip(parts[::2], parts[1::2])]
+            out_ref[first : first + SUBS, lanes] = base_ref[first : first + SUBS, lanes] + parts[0]
+            term = [t * l for t, l in zip(term, lam)]
+        return carry
+
+    lax.fori_loop(0, tiles, tile, 0)
 
 
 def cache_kernel(
@@ -78,7 +118,6 @@
     length_ref,
     decay_ref,
     weight_ref,
-    window_part_ref,
     out_ref,
     signal,
     result,
@@ -147,17 +186,15 @@
     for r in range(modes):
         decay = row(decay_ref, r)
         from_cache = history[r] * jnp.exp(-decay * (float(steps) * rows_float))
-        begin.append(from_cache + gain[r] * exclusive_scan(ends[r], decay, steps))
+        begin.append(from_cache + gain[r] * shift_down(inclusive_scan(ends[r], decay, steps), 1))
     segment_outputs(read, write, steps, lam, gain, begin)
-    out_ref[...] = (result[...] + window_part_ref[...]).astype(jnp.bfloat16)
-
-
-def gate_kernel(conv_ref, window_ref, gate_ref, skip_ref, out_ref):
+    out_ref[...] = result[...].astype(jnp.bfloat16)
+
+
+def gate_kernel(conv_ref, base_ref, gate_ref, out_ref):
     for block in range(conv_ref.shape[0]):
         lanes = slice(block * LANES, (block + 1) * LANES)
-        mixed = conv_ref[block].astype(jnp.float32) + skip_ref[:, lanes] * window_ref[
-            :, lanes
-        ].astype(jnp.float32)
+        mixed = conv_ref[block].astype(jnp.float32) + base_ref[:, lanes]
         out_ref[:, lanes] = (gate_ref[:, lanes].astype(jnp.float32) * mixed).astype(jnp.bfloat16)
 
 
@@ -169,31 +206,49 @@
     return pltpu.CompilerParams(vmem_limit_bytes=VMEM_LIMIT)
 
 
-def window_conv(window_seq, decay, weight):
-    window = window_seq.shape[0]
+def window_conv(window, decay, weight, skip):
+    rows, width = window.shape
     modes = decay.shape[0]
     return pl.pallas_call(
-        functools.partial(window_kernel, modes, window // SUBS),
-        out_shape=jax.ShapeDtypeStruct((window, LANES), jnp.float32),
-        in_specs=vmem(3),
-        out_specs=pl.BlockSpec(memory_space=pltpu.VMEM),
-        scratch_shapes=[pltpu.VMEM((window, LANES), jnp.float32)],
+        functools.partial(window_kernel, modes, rows // SUBS),
+        out_shape=(
+            jax.ShapeDtypeStruct((rows, width), jnp.float32),
+            jax.ShapeDtypeStruct((modes, width), jnp.float32),
+        ),
+        in_specs=vmem(4),
+        out_specs=tuple(vmem(2)),
+        scratch_shapes=[pltpu.VMEM((rows, LANES), jnp.float32)] * 2,
         compiler_params=params(),
         cost_estimate=pl.CostEstimate(
-            flops=12 * window * LANES * modes, bytes_accessed=6 * window * LANES, transcendentals=0
+            flops=12 * rows * width * modes, bytes_accessed=6 * rows * width, transcendentals=0
         ),
         name="window_conv",
-    )(window_seq, decay, weight)
-
-
-def cache_conv(slots, pages, length, decay, weight, window_part):
-    window = window_part.shape[0]
+    )(window, decay, weight, skip)
+
+
+def add_carry(base, state, decay, weight):
+    rows, width = base.shape
+    modes = decay.shape[0]
+    return pl.pallas_call(
+        functools.partial(carry_kernel, modes),
+        out_shape=jax.ShapeDtypeStruct((rows, width), jnp.float32),
+        in_specs=vmem(4),
+        out_specs=pl.BlockSpec(memory_space=pltpu.VMEM),
+        compiler_params=params(),
+        cost_estimate=pl.CostEstimate(
+            flops=3 * rows * width * modes, bytes_accessed=8 * rows * width, transcendentals=0
+        ),
+        name="add_carry",
+    )(base, state, decay, weight)
+
+
+def cache_conv(slots, pages, length, decay, weight, window):
     modes = decay.shape[0]
     cached = slots.shape[0] * SUBS
     return pl.pallas_call(
         functools.partial(cache_kernel, modes, window // SUBS),
         out_shape=jax.ShapeDtypeStruct((window, LANES), jnp.bfloat16),
-        in_specs=[pl.BlockSpec(memory_space=pltpu.SMEM)] + vmem(5),
+        in_specs=[pl.BlockSpec(memory_space=pltpu.SMEM)] + vmem(4),
         out_specs=pl.BlockSpec(memory_space=pltpu.VMEM),
         scratch_shapes=[
             pltpu.VMEM((cached + 64, LANES), jnp.float32),
@@ -204,18 +259,28 @@
             flops=4 * cached * LANES * modes, bytes_accessed=4 * cached * LANES, transcendentals=0
         ),
         name="cache_conv",
-    )(slots, pages, length, decay, weight, window_part)
-
-
-def gate_out(conv_home, window_input, gate_values, skip_gain):
+    )(slots, pages, length, decay, weight)
+
+
+def gate_out(conv_home, base, gate_values):
     return pl.pallas_call(
         gate_kernel,
         out_shape=jax.ShapeDtypeStruct(gate_values.shape, jnp.bfloat16),
-        in_specs=vmem(4),
+        in_specs=vmem(3),
         out_specs=pl.BlockSpec(memory_space=pltpu.VMEM),
         compiler_params=params(),
         name="gate_out",
-    )(conv_home, window_input, gate_values, skip_gain)
+    )(conv_home, base, gate_values)
+
+
+def start_states(ends, decay, rows, count):
+    state = lax.ppermute(ends, "ctx", [(i, i + 1) for i in range(count - 1)])
+    hop = 1
+    while hop < count:
+        before = lax.ppermute(state, "ctx", [(i, i + hop) for i in range(count - hop)])
+        state = state + jnp.exp(-decay * float(rows * hop)) * before
+        hop *= 2
+    return state
 
 
 def local(
@@ -225,11 +290,11 @@
     chan_count = lax.axis_size("chan")
     ctx_pos = lax.axis_index("ctx")
     pool_pages, page_len, width = page_pool.shape
+    rows = window_input.shape[0]
     pencil = window_input.shape[1] // ctx_count
     parcel = jnp.transpose(page_pool.reshape(pool_pages, page_len, -1, pencil), (2, 0, 1, 3))
     arrived = lax.all_to_all(parcel, ("chan", "ctx"), split_axis=0, concat_axis=0, tiled=True)
     arrived = arrived.reshape(-1, page_len, pencil)
-    window_seq = lax.all_to_all(window_input, "ctx", split_axis=1, concat_axis=0, tiled=True)
     owners = page_table // pool_pages
     source = (owners % chan_count) * ctx_count + owners // chan_count
     slots = source * pool_pages + page_table % pool_pages
@@ -237,12 +302,14 @@
     decay = lax.dynamic_slice_in_dim(decays, start, pencil, 0).T
     weight = lax.dynamic_slice_in_dim(residues, start, pencil, 0).T
     length = lax.dynamic_slice_in_dim(filter_len, start, pencil, 0)[None, :]
-    window_part = window_conv(window_seq, decay, weight)
-    convolved = cache_conv(slots, arrived, length, decay, weight, window_part)
+    base, ends = window_conv(window_input, decays.T, residues.T, skip_gain[None, :])
+    state = start_states(ends, decays.T, rows, ctx_count)
+    base = add_carry(base, state, decays.T, residues.T)
+    convolved = cache_conv(slots, arrived, length, decay, weight, rows * ctx_count)
     conv_home = lax.all_to_all(
         convolved.reshape(ctx_count, -1, pencil), "ctx", split_axis=0, concat_axis=0, tiled=True
     )
-    return gate_out(conv_home, window_input, gate_values, skip_gain[None, :])
+    return gate_out(conv_home, base, gate_values)
 
 
 def solution(mesh):

time: 109 us -> 107 us (0.982)
  starting transfers between devices: 14.2 us -> 39.8 us
  blocking collectives: 17.2 us -> 0 us
  waiting for transfers between devices: 55.6 us -> 44 us
  Pallas kernels: 15.7 us -> 17.5 us
    all_to_all x1, waiting for transfers between devices: 45.6 us -> 0.01 us  [local(): lax.all_to_all(parcel, ('chan', 'ctx'), split_axis=0, concat_axis=0, tile...]
    ppermute x0 -> x4, waiting for transfers between devices: none -> 43.1 us  [the longest x1 39.4 us: start_states(): state = lax.ppermute(ends, 'ctx', [(i, i + 1) for i in range(count - 1)])]
    ppermute x0 -> x4, starting transfers between devices: none -> 21.2 us  [the longest x3 17.8 us: start_states(): lax.ppermute(state, 'ctx', [(i, i + hop) for i in range(count - hop)])]
    all_to_all x1 -> x0, blocking collectives: 17.2 us -> none  [local(): lax.all_to_all(convolved.reshape(ctx_count, -1, pencil), 'ctx', split_axi...]
    all_to_all x1, waiting for transfers between devices: 9.96 us -> 0.84 us  [local(): lax.all_to_all(convolved.reshape(ctx_count, -1, pencil), 'ctx', split_axi...]
    all_to_all x1, starting transfers between devices: 5.74 us -> 12.5 us  [local(): lax.all_to_all(parcel, ('chan', 'ctx'), split_axis=0, concat_axis=0, tile...]
    unnamed x10 -> x14, local copies, waits for them, and re-layouts: 0.03 us -> 2.56 us
    all_to_all x1, starting transfers between devices: 8.47 us -> 6.06 us  [local(): lax.all_to_all(convolved.reshape(ctx_count, -1, pencil), 'ctx', split_axi...]
  transfers between devices with their start and end apart: 2 -> 6, of which waited for: 2 -> 4; matrix products, arithmetic and copies ran while one was open for 3% -> 1% of each run, Pallas kernels for 2% -> 16%
where the time goes in v2:
time: 107 us
  waiting for transfers between devices  44 us (41%)
  starting transfers between devices  39.8 us (37%)
  Pallas kernels  17.5 us (16%)
  local copies, waits for them, and re-layouts  5.26 us (5%)
    ppermute x1, waiting for transfers between devices, start_states(): state = lax.ppermute(ends, 'ctx', [(i, i + 1) for i in range(count - 1)])  39.4 us
    ppermute x3, starting transfers between devices, start_states(): lax.ppermute(state, 'ctx', [(i, i + hop) for i in range(count - hop)])  17.8 us
    pallas_call x1, Pallas kernels, cache_conv(): pl.pallas_call(functools.partial(cache_kernel, modes, window // SUBS), ou...  12.9 us
    all_to_all x1, starting transfers between devices, local(): lax.all_to_all(parcel, ('chan', 'ctx'), split_axis=0, concat_axis=0, tile...  12.5 us
    all_to_all x1, starting transfers between devices, local(): lax.all_to_all(convolved.reshape(ctx_count, -1, pencil), 'ctx', split_axi...  6.06 us
    ppermute x3, waiting for transfers between devices, start_states(): lax.ppermute(state, 'ctx', [(i, i + hop) for i in range(count - hop)])  3.75 us
    ppermute x1, starting transfers between devices, start_states(): state = lax.ppermute(ends, 'ctx', [(i, i + 1) for i in range(count - 1)])  3.4 us
    pallas_call x1, Pallas kernels, window_conv(): pl.pallas_call(functools.partial(window_kernel, modes, rows // SUBS), out...  3.02 us
  transfers between devices with their start and end apart: 6, of which 4 were waited for; matrix products, arithmetic and copies ran while one was open for 1% of the time, Pallas kernels for 16%

profile of v2, /device:TPU:4, one launch (start us, length us, event | category | flops | bytes accessed | tf_op | source)
XLA Modules:
  0.0 106.7 jit_solution(10873031002336050104)
XLA Ops:
  0.0 0.0 copy-start
  0.0 1.6 %copy-done = bf16[16,8,8192]{2,1,0:T(8,128)(2,1)S(1)} copy-done((bf16[16,8,8192]{2,1,0:T(8,128)(2,1)S(1)}, bf16[16,8,8192]{2,1,0:T(8,128)(2,1)}, u32[]{:S(2)}) %copy-start) | copy-done | bytes 2097176
  1.6 1.9 %copy_bitcast_fusion = bf16[64,16,8,128]{3,2,1,0:T(8,128)(2,1)} fusion(bf16[16,8,8192]{2,1,0:T(8,128)(2,1)S(1)} %copy-done), kind=kLoop, calls=%fused_computation | loop fusion | bytes 4194304 | tf_op jit(solution)/shard_map/transpose | solution.py:295
  3.5 0.0 copy-start.1
  3.5 0.0 copy-start.2
  3.5 0.0 copy-start.4
  3.5 0.0 copy-start.5
  3.5 0.0 copy-start.6
  3.5 12.5 %all-to-all-start = ((bf16[64,16,8,128]{3,2,1,0:T(8,128)(2,1)}), bf16[64,16,8,128]{3,2,1,0:T(8,128)(2,1)}, u32[]{:S(2)}, u32[]{:S(2)}) async-start(bf16[64,16,8,128]{3,2,1,0:T(8,128)(2,1)} %copy_bitcast_fusion), calls=%async_computation | async-start | bytes 4194304 | tf_op jit(solution)/shard_map/all_to_all | solution.py:296
  16.0 0.0 copy-done.1
  16.1 0.0 copy-done.2
  16.1 0.0 copy-done.4
  16.1 0.0 copy-done.5
  16.1 3.0 %window_conv.1 = (f32[128,1024]{1,0:T(8,128)S(1)}, f32[16,1024]{1,0:T(8,128)S(1)}) custom-call(bf16[128,1024]{1,0:T(8,128)(2,1)S(1)} %copy-done.4, f32[16,1024]{1,0:T(8,128)S(1)} %bitcast.19, f32[16,1024]{1,0:T(8,128)S(1)} %bitcast.21, f32[1,1024]{1,0:T(1,128)S(1)} %bitcast.23), custom_call_target="tpu_custom_call" | custom-call | flops 25165824 | bytes 786432 | tf_op jit(solution)/shard_map/window_conv/pallas_call | solution.py:212
  19.1 3.4 %collective-permute-start = (f32[16,1024]{1,0:T(8,128)S(1)}, f32[16,1024]{1,0:T(8,128)S(1)}, u32[]{:S(2)}, u32[]{:S(2)}) collective-permute-start(f32[16,1024]{1,0:T(8,128)S(1)} %get-tuple-element.8), channel_id=1, source_target_pairs={{0,32},{32,64},{64,96},{96,128},{128,160},{160,192},{192,224},{1,3... | collective-permute-start | bytes 196616 | tf_op jit(solution)/shard_map/ppermute | solution.py:277
  22.5 0.0 copy-done.6
  22.6 39.4 %collective-permute-done = f32[16,1024]{1,0:T(8,128)S(1)} collective-permute-done((f32[16,1024]{1,0:T(8,128)S(1)}, f32[16,1024]{1,0:T(8,128)S(1)}, u32[]{:S(2)}, u32[]{:S(2)}) %collective-permute-start) | collective-permute-done | bytes 65568 | tf_op jit(solution)/shard_map/ppermute | solution.py:277
  62.0 4.5 %collective-permute-start.1 = (f32[16,1024]{1,0:T(8,128)S(1)}, f32[16,1024]{1,0:T(8,128)S(1)}, u32[]{:S(2)}, u32[]{:S(2)}) collective-permute-start(f32[16,1024]{1,0:T(8,128)S(1)} %collective-permute-done), channel_id=1, source_target_pairs={{0,32},{32,64},{64,96},{96,128},{128,160},{160,192},{192,224},{1,3... | collective-permute-start | bytes 196616 | tf_op jit(solution)/shard_map/ppermute | solution.py:280
  66.5 1.9 %collective-permute-done.1 = f32[16,1024]{1,0:T(8,128)S(1)} collective-permute-done((f32[16,1024]{1,0:T(8,128)S(1)}, f32[16,1024]{1,0:T(8,128)S(1)}, u32[]{:S(2)}, u32[]{:S(2)}) %collective-permute-start.1) | collective-permute-done | bytes 65568 | tf_op jit(solution)/shard_map/ppermute | solution.py:280
  68.4 5.5 %collective-permute-start.2 = (f32[16,1024]{1,0:T(8,128)S(1)}, f32[16,1024]{1,0:T(8,128)S(1)}, u32[]{:S(2)}, u32[]{:S(2)}) collective-permute-start(f32[16,1024]{1,0:T(8,128)S(1)} %multiply_add_fusion.2), channel_id=1, source_target_pairs={{0,64},{32,96},{64,128},{96,160},{128,192},{160,224},{1,65},{33,97... | collective-permute-start | bytes 196616 | tf_op jit(solution)/shard_map/ppermute | solution.py:280
  73.9 0.8 dynamic-slice_bitcast_fusion.2.length_ref
  74.7 0.0 all-to-all-done
  74.7 12.9 %cache_conv.1 = bf16[1024,128]{1,0:T(8,128)(2,1)} custom-call(s32[512]{0:T(512)S(1)} %fusion.3.slots_ref, bf16[1024,8,128]{2,1,0:T(8,128)(2,1)} %bitcast.2.pages_ref, s32[1,128]{1,0:T(1,128)S(1)} %dynamic-slice_bitcast_fusion.2.length_ref, f32[16,128]{1,0:T(8,128)S(1)} %dynamic-slice_bitcast_fusion.1.decay_ref, ...), custom_call_target="tpu_custom_call" | custom-call | flops 33554432 | bytes 2097152 | tf_op jit(solution)/shard_map/cache_conv/pallas_call | solution.py:248
  87.6 6.1 %all-to-all-start.1 = ((bf16[8,128,128]{2,1,0:T(8,128)(2,1)}), bf16[8,128,128]{2,1,0:T(8,128)(2,1)S(1)}, u32[]{:S(2)}, u32[]{:S(2)}) async-start(bf16[8,128,128]{2,1,0:T(8,128)(2,1)} %bitcast.6), calls=%async_computation.1 | async-start | bytes 524288 | tf_op jit(solution)/shard_map/all_to_all | solution.py:309
  93.6 0.0 collective-permute-done.2
  93.6 7.8 %collective-permute-start.3 = (f32[16,1024]{1,0:T(8,128)S(1)}, f32[16,1024]{1,0:T(8,128)S(1)}, u32[]{:S(2)}, u32[]{:S(2)}) collective-permute-start(f32[16,1024]{1,0:T(8,128)S(1)} %multiply_add_fusion.1), channel_id=1, source_target_pairs={{0,128},{32,160},{64,192},{96,224},{1,129},{33,161},{65,193},{97,2... | collective-permute-start | bytes 196616 | tf_op jit(solution)/shard_map/ppermute | solution.py:280
  101.5 1.9 %collective-permute-done.3 = f32[16,1024]{1,0:T(8,128)S(1)} collective-permute-done((f32[16,1024]{1,0:T(8,128)S(1)}, f32[16,1024]{1,0:T(8,128)S(1)}, u32[]{:S(2)}, u32[]{:S(2)}) %collective-permute-start.3) | collective-permute-done | bytes 65568 | tf_op jit(solution)/shard_map/ppermute | solution.py:280
  103.4 0.8 add_carry.1.base_ref
  104.2 0.8 all-to-all-done.1.conv_ref
  105.0 0.0 copy-start.3
  105.0 0.9 copy-done.3
  105.9 0.8 gate_out.1
  (6 shorter events, 0.1 us)
Async XLA Ops:
  0.0 1.6 %copy-start = (bf16[16,8,8192]{2,1,0:T(8,128)(2,1)S(1)}, bf16[16,8,8192]{2,1,0:T(8,128)(2,1)}, u32[]{:S(2)}) copy-start(bf16[16,8,8192]{2,1,0:T(8,128)(2,1)} %param.10) | copy-start | bytes 6291460
  3.5 12.5 %copy-start.1 = (f32[1024,16]{0,1:T(8,128)S(1)}, f32[1024,16]{0,1:T(8,128)}, u32[]{:S(2)}) copy-start(f32[1024,16]{0,1:T(8,128)} %param.14) | copy-start | bytes 196612
  3.5 12.6 %copy-start.2 = (f32[1024,16]{0,1:T(8,128)S(1)}, f32[1024,16]{0,1:T(8,128)}, u32[]{:S(2)}) copy-start(f32[1024,16]{0,1:T(8,128)} %param.13) | copy-start | bytes 196612
  3.5 12.6 %copy-start.4 = (bf16[128,1024]{1,0:T(8,128)(2,1)S(1)}, bf16[128,1024]{1,0:T(8,128)(2,1)}, u32[]{:S(2)}) copy-start(bf16[128,1024]{1,0:T(8,128)(2,1)} %window_ref.1) | copy-start | bytes 786436
  3.5 12.6 %copy-start.5 = (f32[1024]{0:T(1024)S(1)}, f32[1024]{0:T(1024)}, u32[]{:S(2)}) copy-start(f32[1024]{0:T(1024)} %param.15) | copy-start | bytes 12292
  3.5 19.0 %copy-start.6 = (s32[512]{0:T(512)S(1)}, s32[512]{0:T(512)}, u32[]{:S(2)}) copy-start(s32[512]{0:T(512)} %param.11) | copy-start | bytes 6148
  3.5 71.1 %all-to-all-start = ((bf16[64,16,8,128]{3,2,1,0:T(8,128)(2,1)}), bf16[64,16,8,128]{3,2,1,0:T(8,128)(2,1)}, u32[]{:S(2)}, u32[]{:S(2)}) async-start(bf16[64,16,8,128]{3,2,1,0:T(8,128)(2,1)} %copy_bitcast_fusion), calls=%async_computation | async-start | bytes 4194304 | tf_op jit(solution)/shard_map/all_to_all | solution.py:296
  19.1 42.9 %collective-permute-start = (f32[16,1024]{1,0:T(8,128)S(1)}, f32[16,1024]{1,0:T(8,128)S(1)}, u32[]{:S(2)}, u32[]{:S(2)}) collective-permute-start(f32[16,1024]{1,0:T(8,128)S(1)} %get-tuple-element.8), channel_id=1, source_target_pairs={{0,32},{32,64},{64,96},{96,128},{128,160},{160,192},{192,224},{1,3... | collective-permute-start | bytes 196616 | tf_op jit(solution)/shard_map/ppermute | solution.py:277
  62.0 6.4 %collective-permute-start.1 = (f32[16,1024]{1,0:T(8,128)S(1)}, f32[16,1024]{1,0:T(8,128)S(1)}, u32[]{:S(2)}, u32[]{:S(2)}) collective-permute-start(f32[16,1024]{1,0:T(8,128)S(1)} %collective-permute-done), channel_id=1, source_target_pairs={{0,32},{32,64},{64,96},{96,128},{128,160},{160,192},{192,224},{1,3... | collective-permute-start | bytes 196616 | tf_op jit(solution)/shard_map/ppermute | solution.py:280
  68.4 25.2 %collective-permute-start.2 = (f32[16,1024]{1,0:T(8,128)S(1)}, f32[16,1024]{1,0:T(8,128)S(1)}, u32[]{:S(2)}, u32[]{:S(2)}) collective-permute-start(f32[16,1024]{1,0:T(8,128)S(1)} %multiply_add_fusion.2), channel_id=1, source_target_pairs={{0,64},{32,96},{64,128},{96,160},{128,192},{160,224},{1,65},{33,97... | collective-permute-start | bytes 196616 | tf_op jit(solution)/shard_map/ppermute | solution.py:280
  87.6 17.4 %all-to-all-start.1 = ((bf16[8,128,128]{2,1,0:T(8,128)(2,1)}), bf16[8,128,128]{2,1,0:T(8,128)(2,1)S(1)}, u32[]{:S(2)}, u32[]{:S(2)}) async-start(bf16[8,128,128]{2,1,0:T(8,128)(2,1)} %bitcast.6), calls=%async_computation.1 | async-start | bytes 524288 | tf_op jit(solution)/shard_map/all_to_all | solution.py:309
  93.6 9.7 %collective-permute-start.3 = (f32[16,1024]{1,0:T(8,128)S(1)}, f32[16,1024]{1,0:T(8,128)S(1)}, u32[]{:S(2)}, u32[]{:S(2)}) collective-permute-start(f32[16,1024]{1,0:T(8,128)S(1)} %multiply_add_fusion.1), channel_id=1, source_target_pairs={{0,128},{32,160},{64,192},{96,224},{1,129},{33,161},{65,193},{97,2... | collective-permute-start | bytes 196616 | tf_op jit(solution)/shard_map/ppermute | solution.py:280
  105.0 1.0 copy-start.3

commit v3 on v2

--- a/solution.py
+++ b/solution.py
@@ -84,44 +84,21 @@
     lax.fori_loop(0, tiles, tile, 0)
 
 
-def carry_kernel(modes, base_ref, state_ref, decay_ref, weight_ref, out_ref):
-    tiles = base_ref.shape[1] // LANES
-    ahead = lax.broadcasted_iota(jnp.int32, (SUBS, LANES), 0).astype(jnp.float32) + 1.0
-
-    def tile(index, carry):
-        lanes = pl.ds(pl.multiple_of(index * LANES, LANES), LANES)
-
-        def wide(ref, r):
-            return jnp.broadcast_to(ref[r : r + 1, lanes], (SUBS, LANES))
-
-        term = [
-            wide(weight_ref, r) * wide(state_ref, r) * jnp.exp(-wide(decay_ref, r) * ahead)
-            for r in range(modes)
-        ]
-        lam = [jnp.exp(-float(SUBS) * wide(decay_ref, r)) for r in range(modes)]
-        for first in range(0, base_ref.shape[0], SUBS):
-            parts = list(term)
-            while len(parts) > 1:
-                parts = [a + b for a, b in zip(parts[::2], parts[1::2])]
-            out_ref[first : first + SUBS, lanes] = base_ref[first : first + SUBS, lanes] + parts[0]
-            term = [t * l for t, l in zip(term, lam)]
-        return carry
-
-    lax.fori_loop(0, tiles, tile, 0)
-
-
 def cache_kernel(
     modes,
     steps,
+    place_ref,
     slots_ref,
     pages_ref,
     length_ref,
     decay_ref,
     weight_ref,
-    out_ref,
-    signal,
-    result,
+    *rest,
 ):
+    end_refs, (out_ref, signal, result, before) = rest[:SUBS], rest[SUBS:]
+    for hop, end_ref in enumerate(end_refs):
+        segment = lax.rem(place_ref[0] + (SUBS - hop), SUBS)
+        before[pl.ds(segment, modes, stride=SUBS), :] = end_ref[...]
     page_count = slots_ref.shape[0]
     cached = page_count * SUBS
     rows = lax.broadcasted_iota(jnp.int32, (SUBS, LANES), 0)
@@ -186,6 +163,8 @@
     for r in range(modes):
         decay = row(decay_ref, r)
         from_cache = history[r] * jnp.exp(-decay * (float(steps) * rows_float))
+        prior = inclusive_scan(before[r * SUBS : (r + 1) * SUBS, :], decay, steps)
+        from_cache = from_cache + row(weight_ref, r) * shift_down(prior, 1)
         begin.append(from_cache + gain[r] * shift_down(inclusive_scan(ends[r], decay, steps), 1))
     segment_outputs(read, write, steps, lam, gain, begin)
     out_ref[...] = result[...].astype(jnp.bfloat16)
@@ -226,40 +205,25 @@
     )(window, decay, weight, skip)
 
 
-def add_carry(base, state, decay, weight):
-    rows, width = base.shape
-    modes = decay.shape[0]
-    return pl.pallas_call(
-        functools.partial(carry_kernel, modes),
-        out_shape=jax.ShapeDtypeStruct((rows, width), jnp.float32),
-        in_specs=vmem(4),
-        out_specs=pl.BlockSpec(memory_space=pltpu.VMEM),
-        compiler_params=params(),
-        cost_estimate=pl.CostEstimate(
-            flops=3 * rows * width * modes, bytes_accessed=8 * rows * width, transcendentals=0
-        ),
-        name="add_carry",
-    )(base, state, decay, weight)
-
-
-def cache_conv(slots, pages, length, decay, weight, window):
+def cache_conv(place, slots, pages, length, decay, weight, ends, window):
     modes = decay.shape[0]
     cached = slots.shape[0] * SUBS
     return pl.pallas_call(
         functools.partial(cache_kernel, modes, window // SUBS),
         out_shape=jax.ShapeDtypeStruct((window, LANES), jnp.bfloat16),
-        in_specs=[pl.BlockSpec(memory_space=pltpu.SMEM)] + vmem(4),
+        in_specs=[pl.BlockSpec(memory_space=pltpu.SMEM)] * 2 + vmem(4 + len(ends)),
         out_specs=pl.BlockSpec(memory_space=pltpu.VMEM),
         scratch_shapes=[
             pltpu.VMEM((cached + 64, LANES), jnp.float32),
             pltpu.VMEM((window, LANES), jnp.float32),
+            pltpu.VMEM((modes * SUBS, LANES), jnp.float32),
         ],
         compiler_params=params(),
         cost_estimate=pl.CostEstimate(
             flops=4 * cached * LANES * modes, bytes_accessed=4 * cached * LANES, transcendentals=0
         ),
         name="cache_conv",
-    )(slots, pages, length, decay, weight)
+    )(place, slots, pages, length, decay, weight, *ends)
 
 
 def gate_out(conv_home, base, gate_values):
@@ -273,14 +237,16 @@
     )(conv_home, base, gate_values)
 
 
-def start_states(ends, decay, rows, count):
-    state = lax.ppermute(ends, "ctx", [(i, i + 1) for i in range(count - 1)])
-    hop = 1
-    while hop < count:
-        before = lax.ppermute(state, "ctx", [(i, i + hop) for i in range(count - hop)])
-        state = state + jnp.exp(-decay * float(rows * hop)) * before
-        hop *= 2
-    return state
+def end_states(ends, place, count):
+    pencil = ends.shape[1] // count
+
+    def block(hop):
+        return lax.dynamic_slice_in_dim(ends, (place + hop) % count * pencil, pencil, 1)
+
+    return [block(0)] + [
+        lax.ppermute(block(hop), "ctx", [(i, (i + hop) % count) for i in range(count)])
+        for hop in range(1, count)
+    ]
 
 
 def local(
@@ -303,9 +269,10 @@
     weight = lax.dynamic_slice_in_dim(residues, start, pencil, 0).T
     length = lax.dynamic_slice_in_dim(filter_len, start, pencil, 0)[None, :]
     base, ends = window_conv(window_input, decays.T, residues.T, skip_gain[None, :])
-    state = start_states(ends, decays.T, rows, ctx_count)
-    base = add_carry(base, state, decays.T, residues.T)
-    convolved = cache_conv(slots, arrived, length, decay, weight, rows * ctx_count)
+    ends = end_states(ends, ctx_pos, ctx_count)
+    convolved = cache_conv(
+        ctx_pos[None], slots, arrived, length, decay, weight, ends, rows * ctx_count
+    )
     conv_home = lax.all_to_all(
         convolved.reshape(ctx_count, -1, pencil), "ctx", split_axis=0, concat_axis=0, tiled=True
     )

time: 107 us -> 99 us (0.925)
  blocking collectives: 0 us -> 14.8 us
  starting transfers between devices: 39.8 us -> 28.6 us
  waiting for transfers between devices: 44 us -> 34.6 us
  Pallas kernels: 17.5 us -> 16.2 us
    all_to_all x0 -> x1, blocking collectives: none -> 14.8 us  [local(): lax.all_to_all(convolved.reshape(ctx_count, -1, pencil), 'ctx', split_axi...]
    ppermute x4 -> x7, waiting for transfers between devices: 43.1 us -> 34.6 us  [end_states(): lax.ppermute(block(hop), 'ctx', [(i, (i + hop) % count) for i in range(co...]
    all_to_all x1 -> x0, starting transfers between devices: 6.06 us -> none  [local(): lax.all_to_all(convolved.reshape(ctx_count, -1, pencil), 'ctx', split_axi...]
    ppermute x4 -> x7, starting transfers between devices: 21.2 us -> 16.1 us  [end_states(): lax.ppermute(block(hop), 'ctx', [(i, (i + hop) % count) for i in range(co...]
  transfers between devices with their start and end apart: 6 -> 8, of which waited for: 4 -> 2; matrix products, arithmetic and copies ran while one was open for 1% -> 1% of each run, Pallas kernels for 16% -> 3%
where the time goes in v3:
time: 99 us; the launch traced here: 98.7 us
  waiting for transfers between devices  34.6 us (35%)
  starting transfers between devices  28.6 us (29%)
  Pallas kernels  16.2 us (16%)
  blocking collectives  14.8 us (15%)
  local copies, waits for them, and re-layouts  4.34 us (4%)
    ppermute x7, waiting for transfers between devices, end_states(): lax.ppermute(block(hop), 'ctx', [(i, (i + hop) % count) for i in range(co...  34.6 us
    ppermute x7, starting transfers between devices, end_states(): lax.ppermute(block(hop), 'ctx', [(i, (i + hop) % count) for i in range(co...  16.1 us
    all_to_all x1, blocking collectives, local(): lax.all_to_all(convolved.reshape(ctx_count, -1, pencil), 'ctx', split_axi...  14.8 us
    all_to_all x1, starting transfers between devices, local(): lax.all_to_all(parcel, ('chan', 'ctx'), split_axis=0, concat_axis=0, tile...  12.5 us
    pallas_call x1, Pallas kernels, cache_conv(): pl.pallas_call(functools.partial(cache_kernel, modes, window // SUBS), ou...  12.3 us
    pallas_call x1, Pallas kernels, window_conv(): pl.pallas_call(functools.partial(window_kernel, modes, rows // SUBS), out...  3.02 us
  transfers between devices with their start and end apart: 8, of which 2 were waited for; matrix products, arithmetic and copies ran while one was open for 1% of the time, Pallas kernels for 3%

profile of v3, /device:TPU:4, one launch (start us, length us, event | category | flops | bytes accessed | tf_op | source)
XLA Modules:
  0.0 98.7 jit_solution(9751657452045809661)
XLA Ops:
  0.0 0.0 copy-start
  0.0 1.6 %copy-done = bf16[16,8,8192]{2,1,0:T(8,128)(2,1)S(1)} copy-done((bf16[16,8,8192]{2,1,0:T(8,128)(2,1)S(1)}, bf16[16,8,8192]{2,1,0:T(8,128)(2,1)}, u32[]{:S(2)}) %copy-start) | copy-done | bytes 2097176
  1.6 1.9 %copy_bitcast_fusion = bf16[64,16,8,128]{3,2,1,0:T(8,128)(2,1)} fusion(bf16[16,8,8192]{2,1,0:T(8,128)(2,1)S(1)} %copy-done), kind=kLoop, calls=%fused_computation | loop fusion | bytes 4194304 | tf_op jit(solution)/shard_map/transpose | solution.py:261
  3.5 0.0 copy-start.6
  3.5 12.5 %all-to-all-start = ((bf16[64,16,8,128]{3,2,1,0:T(8,128)(2,1)}), bf16[64,16,8,128]{3,2,1,0:T(8,128)(2,1)}, u32[]{:S(2)}, u32[]{:S(2)}) async-start(bf16[64,16,8,128]{3,2,1,0:T(8,128)(2,1)} %copy_bitcast_fusion), calls=%async_computation | async-start | bytes 4194304 | tf_op jit(solution)/shard_map/all_to_all | solution.py:262
  16.1 0.0 copy-start.1
  16.2 0.0 copy-done.2
  16.2 0.0 copy-done.3
  16.2 0.0 copy-done.4
  16.2 0.0 copy-done.5
  16.2 3.0 %window_conv.1 = (f32[128,1024]{1,0:T(8,128)S(1)}, f32[16,1024]{1,0:T(8,128)S(1)}) custom-call(bf16[128,1024]{1,0:T(8,128)(2,1)S(1)} %copy-done.2, f32[16,1024]{1,0:T(8,128)S(1)} %bitcast.19, f32[16,1024]{1,0:T(8,128)S(1)} %bitcast.18, f32[1,1024]{1,0:T(1,128)S(1)} %bitcast.20), custom_call_target="tpu_custom_call" | custom-call | flops 25165824 | bytes 786432 | tf_op jit(solution)/shard_map/window_conv/pallas_call | solution.py:191
  19.3 1.6 %collective-permute-start = (f32[16,128]{1,0:T(8,128)S(1)}, f32[16,128]{1,0:T(8,128)S(1)}, u32[]{:S(2)}, u32[]{:S(2)}) collective-permute-start(f32[16,128]{1,0:T(8,128)S(1)} %get-tuple-element.15), channel_id=1, source_target_pairs={{0,32},{32,64},{64,96},{96,128},{128,160},{160,192},{192,224},{224... | collective-permute-start | bytes 24584 | tf_op jit(solution)/shard_map/ppermute | solution.py:247
  20.9 2.4 %collective-permute-start.1 = (f32[16,128]{1,0:T(8,128)S(1)}, f32[16,128]{1,0:T(8,128)S(1)}, u32[]{:S(2)}, u32[]{:S(2)}) collective-permute-start(f32[16,128]{1,0:T(8,128)S(1)} %get-tuple-element.14), channel_id=1, source_target_pairs={{0,64},{32,96},{64,128},{96,160},{128,192},{160,224},{192,0},{224,... | collective-permute-start | bytes 24584 | tf_op jit(solution)/shard_map/ppermute | solution.py:247
  23.2 2.7 %collective-permute-start.2 = (f32[16,128]{1,0:T(8,128)S(1)}, f32[16,128]{1,0:T(8,128)S(1)}, u32[]{:S(2)}, u32[]{:S(2)}) collective-permute-start(f32[16,128]{1,0:T(8,128)S(1)} %get-tuple-element.13), channel_id=1, source_target_pairs={{0,96},{32,128},{64,160},{96,192},{128,224},{160,0},{192,32},{224,... | collective-permute-start | bytes 24584 | tf_op jit(solution)/shard_map/ppermute | solution.py:247
  25.9 2.4 %collective-permute-start.3 = (f32[16,128]{1,0:T(8,128)S(1)}, f32[16,128]{1,0:T(8,128)S(1)}, u32[]{:S(2)}, u32[]{:S(2)}) collective-permute-start(f32[16,128]{1,0:T(8,128)S(1)} %get-tuple-element.12), channel_id=1, source_target_pairs={{0,128},{32,160},{64,192},{96,224},{128,0},{160,32},{192,64},{224,... | collective-permute-start | bytes 24584 | tf_op jit(solution)/shard_map/ppermute | solution.py:247
  28.3 2.7 %collective-permute-start.4 = (f32[16,128]{1,0:T(8,128)S(1)}, f32[16,128]{1,0:T(8,128)S(1)}, u32[]{:S(2)}, u32[]{:S(2)}) collective-permute-start(f32[16,128]{1,0:T(8,128)S(1)} %get-tuple-element.11), channel_id=1, source_target_pairs={{0,160},{32,192},{64,224},{96,0},{128,32},{160,64},{192,96},{224,1... | collective-permute-start | bytes 24584 | tf_op jit(solution)/shard_map/ppermute | solution.py:247
  30.9 0.0 copy-done.6
  31.0 33.7 %collective-permute-done.rest_1_ = f32[16,128]{1,0:T(8,128)S(1)} collective-permute-done((f32[16,128]{1,0:T(8,128)S(1)}, f32[16,128]{1,0:T(8,128)S(1)}, u32[]{:S(2)}, u32[]{:S(2)}) %collective-permute-start) | collective-permute-done | bytes 8224 | tf_op jit(solution)/shard_map/ppermute | solution.py:247
  64.7 2.4 %collective-permute-start.5 = (f32[16,128]{1,0:T(8,128)S(1)}, f32[16,128]{1,0:T(8,128)S(1)}, u32[]{:S(2)}, u32[]{:S(2)}) collective-permute-start(f32[16,128]{1,0:T(8,128)S(1)} %get-tuple-element.10), channel_id=1, source_target_pairs={{0,192},{32,224},{64,0},{96,32},{128,64},{160,96},{192,128},{224,1... | collective-permute-start | bytes 24584 | tf_op jit(solution)/shard_map/ppermute | solution.py:247
  67.1 0.0 collective-permute-done.1.rest_2_
  67.1 2.1 %collective-permute-start.6 = (f32[16,128]{1,0:T(8,128)S(1)}, f32[16,128]{1,0:T(8,128)S(1)}, u32[]{:S(2)}, u32[]{:S(2)}) collective-permute-start(f32[16,128]{1,0:T(8,128)S(1)} %get-tuple-element.9), channel_id=1, source_target_pairs={{0,224},{32,0},{64,32},{96,64},{128,96},{160,128},{192,160},{224,1... | collective-permute-start | bytes 24584 | tf_op jit(solution)/shard_map/ppermute | solution.py:247
  69.1 0.8 dynamic-slice_bitcast_fusion.2.length_ref
  69.9 0.0 collective-permute-done.2.rest_3_
  69.9 0.0 collective-permute-done.3.rest_4_
  69.9 0.0 collective-permute-done.4.rest_5_
  69.9 0.0 collective-permute-done.5.rest_6_
  69.9 0.8 collective-permute-done.6.rest_7_
  70.7 0.0 all-to-all-done
  70.7 12.3 %cache_conv.1 = bf16[1024,128]{1,0:T(8,128)(2,1)S(1)} custom-call(s32[1]{0:T(128)} %bitcast.place_ref, s32[512]{0:T(512)S(1)} %fusion.3.slots_ref, bf16[1024,8,128]{2,1,0:T(8,128)(2,1)} %bitcast.3.pages_ref, s32[1,128]{1,0:T(1,128)S(1)} %dynamic-slice_bitcast_fusion.2.length_ref, f32[16,128]{1,0:T(8,128)S(1)} %get-tuple-element.18.decay_ref, ...), custom_call_target="tpu_custom_call" | custom-call | flops 33554432 | bytes 2097152 | tf_op jit(solution)/shard_map/cache_conv/pallas_call | solution.py:211
  83.1 14.8 %all_to_all.10.conv_ref = bf16[8,128,128]{2,1,0:T(8,128)(2,1)S(1)} all-to-all(bf16[8,128,128]{2,1,0:T(8,128)(2,1)S(1)} %bitcast.17), channel_id=1, replica_groups=mesh['ctx'=8,'chan'=8,'req'=4] {'ctx'}, dimensions={0} | all-to-all | bytes 524288 | tf_op jit(solution)/shard_map/all_to_all | solution.py:276
  97.9 0.0 copy-done.1
  97.9 0.8 gate_out.1
  (7 shorter events, 0.1 us)
Async XLA Ops:
  0.0 1.6 %copy-start = (bf16[16,8,8192]{2,1,0:T(8,128)(2,1)S(1)}, bf16[16,8,8192]{2,1,0:T(8,128)(2,1)}, u32[]{:S(2)}) copy-start(bf16[16,8,8192]{2,1,0:T(8,128)(2,1)} %param.10) | copy-start | bytes 6291460
  3.5 12.7 %copy-start.2 = (bf16[128,1024]{1,0:T(8,128)(2,1)S(1)}, bf16[128,1024]{1,0:T(8,128)(2,1)}, u32[]{:S(2)}) copy-start(bf16[128,1024]{1,0:T(8,128)(2,1)} %window_ref.1) | copy-start | bytes 786436
  3.5 12.7 %copy-start.3 = (f32[1024,16]{0,1:T(8,128)S(1)}, f32[1024,16]{0,1:T(8,128)}, u32[]{:S(2)}) copy-start(f32[1024,16]{0,1:T(8,128)} %param.13) | copy-start | bytes 196612
  3.5 12.7 %copy-start.4 = (f32[1024,16]{0,1:T(8,128)S(1)}, f32[1024,16]{0,1:T(8,128)}, u32[]{:S(2)}) copy-start(f32[1024,16]{0,1:T(8,128)} %param.14) | copy-start | bytes 196612
  3.5 12.7 %copy-start.5 = (f32[1024]{0:T(1024)S(1)}, f32[1024]{0:T(1024)}, u32[]{:S(2)}) copy-start(f32[1024]{0:T(1024)} %param.15) | copy-start | bytes 12292
  3.5 27.4 %copy-start.6 = (s32[512]{0:T(512)S(1)}, s32[512]{0:T(512)}, u32[]{:S(2)}) copy-start(s32[512]{0:T(512)} %param.11) | copy-start | bytes 6148
  3.5 67.2 %all-to-all-start = ((bf16[64,16,8,128]{3,2,1,0:T(8,128)(2,1)}), bf16[64,16,8,128]{3,2,1,0:T(8,128)(2,1)}, u32[]{:S(2)}, u32[]{:S(2)}) async-start(bf16[64,16,8,128]{3,2,1,0:T(8,128)(2,1)} %copy_bitcast_fusion), calls=%async_computation | async-start | bytes 4194304 | tf_op jit(solution)/shard_map/all_to_all | solution.py:262
  16.1 81.8 %copy-start.1 = (bf16[128,1024]{1,0:T(8,128)(2,1)S(1)}, bf16[128,1024]{1,0:T(8,128)(2,1)}, u32[]{:S(2)}) copy-start(bf16[128,1024]{1,0:T(8,128)(2,1)} %gate_ref.1) | copy-start | bytes 786436
  19.3 45.4 %collective-permute-start = (f32[16,128]{1,0:T(8,128)S(1)}, f32[16,128]{1,0:T(8,128)S(1)}, u32[]{:S(2)}, u32[]{:S(2)}) collective-permute-start(f32[16,128]{1,0:T(8,128)S(1)} %get-tuple-element.15), channel_id=1, source_target_pairs={{0,32},{32,64},{64,96},{96,128},{128,160},{160,192},{192,224},{224... | collective-permute-start | bytes 24584 | tf_op jit(solution)/shard_map/ppermute | solution.py:247
  20.9 46.2 %collective-permute-start.1 = (f32[16,128]{1,0:T(8,128)S(1)}, f32[16,128]{1,0:T(8,128)S(1)}, u32[]{:S(2)}, u32[]{:S(2)}) collective-permute-start(f32[16,128]{1,0:T(8,128)S(1)} %get-tuple-element.14), channel_id=1, source_target_pairs={{0,64},{32,96},{64,128},{96,160},{128,192},{160,224},{192,0},{224,... | collective-permute-start | bytes 24584 | tf_op jit(solution)/shard_map/ppermute | solution.py:247
  23.2 46.7 %collective-permute-start.2 = (f32[16,128]{1,0:T(8,128)S(1)}, f32[16,128]{1,0:T(8,128)S(1)}, u32[]{:S(2)}, u32[]{:S(2)}) collective-permute-start(f32[16,128]{1,0:T(8,128)S(1)} %get-tuple-element.13), channel_id=1, source_target_pairs={{0,96},{32,128},{64,160},{96,192},{128,224},{160,0},{192,32},{224,... | collective-permute-start | bytes 24584 | tf_op jit(solution)/shard_map/ppermute | solution.py:247
  25.9 44.0 %collective-permute-start.3 = (f32[16,128]{1,0:T(8,128)S(1)}, f32[16,128]{1,0:T(8,128)S(1)}, u32[]{:S(2)}, u32[]{:S(2)}) collective-permute-start(f32[16,128]{1,0:T(8,128)S(1)} %get-tuple-element.12), channel_id=1, source_target_pairs={{0,128},{32,160},{64,192},{96,224},{128,0},{160,32},{192,64},{224,... | collective-permute-start | bytes 24584 | tf_op jit(solution)/shard_map/ppermute | solution.py:247
  28.3 41.6 %collective-permute-start.4 = (f32[16,128]{1,0:T(8,128)S(1)}, f32[16,128]{1,0:T(8,128)S(1)}, u32[]{:S(2)}, u32[]{:S(2)}) collective-permute-start(f32[16,128]{1,0:T(8,128)S(1)} %get-tuple-element.11), channel_id=1, source_target_pairs={{0,160},{32,192},{64,224},{96,0},{128,32},{160,64},{192,96},{224,1... | collective-permute-start | bytes 24584 | tf_op jit(solution)/shard_map/ppermute | solution.py:247
  64.7 5.2 %collective-permute-start.5 = (f32[16,128]{1,0:T(8,128)S(1)}, f32[16,128]{1,0:T(8,128)S(1)}, u32[]{:S(2)}, u32[]{:S(2)}) collective-permute-start(f32[16,128]{1,0:T(8,128)S(1)} %get-tuple-element.10), channel_id=1, source_target_pairs={{0,192},{32,224},{64,0},{96,32},{128,64},{160,96},{192,128},{224,1... | collective-permute-start | bytes 24584 | tf_op jit(solution)/shard_map/ppermute | solution.py:247
  67.1 3.7 %collective-permute-start.6 = (f32[16,128]{1,0:T(8,128)S(1)}, f32[16,128]{1,0:T(8,128)S(1)}, u32[]{:S(2)}, u32[]{:S(2)}) collective-permute-start(f32[16,128]{1,0:T(8,128)S(1)} %get-tuple-element.9), channel_id=1, source_target_pairs={{0,224},{32,0},{64,32},{96,64},{128,96},{160,128},{192,160},{224,1... | collective-permute-start | bytes 24584 | tf_op jit(solution)/shard_map/ppermute | solution.py:247

commit v4 on v2

--- a/solution.py
+++ b/solution.py
@@ -9,7 +9,10 @@
 
 LANES = 128
 SUBS = 8
-VMEM_LIMIT = 32 * 1024 * 1024
+RANKS = 2
+KEPT = 3
+CHUNK = 64
+VMEM_LIMIT = 16 * 1024 * 1024
 
 
 def row(ref, index):
@@ -110,59 +113,141 @@
     lax.fori_loop(0, tiles, tile, 0)
 
 
-def cache_kernel(
-    modes,
-    steps,
-    slots_ref,
-    pages_ref,
-    length_ref,
-    decay_ref,
-    weight_ref,
-    out_ref,
-    signal,
-    result,
+def split_masks(params_ref, lanes, modes, cached):
+    return float(cached) - jnp.broadcast_to(params_ref[modes : modes + 1, lanes], (SUBS, LANES))
+
+
+def select_kernel(modes, cached, place_ref, slots_ref, pool_ref, *rest):
+    param_refs, parcel_ref = rest[:-1], rest[-1]
+    groups = len(param_refs)
+    pencils = param_refs[0].shape[1] // LANES
+    blocks = slots_ref.shape[0] // RANKS
+    span = float(cached // blocks)
+    slots = [slots_ref[i] for i in range(blocks * RANKS)]
+    for hop, params_ref in enumerate(param_refs):
+        group = lax.rem(place_ref[0] + (groups - hop), groups)
+
+        def pencil(index, carry, params_ref=params_ref, group=group):
+            lanes = pl.ds(pl.multiple_of(index * LANES, LANES), LANES)
+            dest = group * pencils + index
+            far = pl.ds(pl.multiple_of(dest * LANES, LANES), LANES)
+            first = split_masks(params_ref, lanes, modes, cached)
+
+            def page(block, rank):
+                return pool_ref[slots[block * RANKS + rank], :, far].astype(jnp.float32)
+
+            for kind in range(KEPT):
+                for rank in range(RANKS):
+                    value = page(kind, rank)
+                    for block in range(kind + KEPT, blocks, KEPT):
+                        later = first >= span * float(block - KEPT + 1)
+                        value = jnp.where(later, page(block, rank), value)
+                    parcel_ref[dest, kind * RANKS + rank] = value.astype(jnp.bfloat16)
+            return carry
+
+        lax.fori_loop(0, pencils, pencil, 0, unroll=2)
+
+
+def state_kernel(modes, cached, place_ref, count_ref, slots_ref, where_ref, pool_ref, *rest):
+    param_refs, (_, state_ref, powers) = rest[:-3], rest[-3:]
+    groups = len(param_refs)
+    pencils = param_refs[0].shape[1] // LANES
+    last_page = cached // SUBS - 1
+    rows = lax.broadcasted_iota(jnp.int32, (SUBS, LANES), 0).astype(jnp.float32)
+    pairs = (count_ref[0] + 1) // 2
+    for hop, params_ref in enumerate(param_refs):
+        group = lax.rem(place_ref[0] + (groups - hop), groups)
+
+        def pencil(index, carry, params_ref=params_ref, group=group):
+            lanes = pl.ds(pl.multiple_of(index * LANES, LANES), LANES)
+            dest = group * pencils + index
+            far = pl.ds(pl.multiple_of(dest * LANES, LANES), LANES)
+            first = split_masks(params_ref, lanes, modes, cached)
+            decay = params_ref[0:modes, lanes]
+
+            def prepare(pair, carry):
+                for part in range(2):
+                    entry = pair * 2 + part
+                    ahead = ((last_page - where_ref[entry]) * SUBS).astype(jnp.float32)
+                    powers[entry] = jnp.exp(-decay * ahead)
+                return carry
+
+            lax.fori_loop(0, pairs, prepare, 0)
+
+            def gather(pair, states):
+                for part in range(2):
+                    entry = pair * 2 + part
+                    value = pool_ref[slots_ref[entry], :, far].astype(jnp.float32)
+                    position = (where_ref[entry] * SUBS).astype(jnp.float32) + rows
+                    value = jnp.where(position > first, value, 0.0)
+                    states = tuple(
+                        s + jnp.broadcast_to(powers[entry, r : r + 1, :], (SUBS, LANES)) * value
+                        for r, s in enumerate(states)
+                    )
+                return states
+
+            zero = jnp.zeros((SUBS, LANES), jnp.float32)
+            states = lax.fori_loop(0, pairs, gather, tuple(zero for _ in range(modes)))
+            for r in range(modes):
+                rate = jnp.broadcast_to(params_ref[r : r + 1, lanes], (SUBS, LANES))
+                weighted = states[r] * jnp.exp(-rate * (float(SUBS - 1) - rows))
+                state_ref[group, r : r + 1, lanes] = jnp.sum(weighted, axis=0, keepdims=True)
+            return carry
+
+        lax.fori_loop(0, pencils, pencil, 0)
+
+
+def tail_kernel(
+    modes, steps, blocks, order_ref, pages_ref, length_ref, decay_ref, weight_ref, out_ref, signal, result
 ):
-    page_count = slots_ref.shape[0]
-    cached = page_count * SUBS
+    cached = order_ref.shape[0] * SUBS
+    per_block = order_ref.shape[0] // blocks
+    span = per_block * SUBS
     rows = lax.broadcasted_iota(jnp.int32, (SUBS, LANES), 0)
     length = jnp.broadcast_to(length_ref[...], (SUBS, LANES))
     first = cached - length
-
-    lam_page = [jnp.exp(-float(SUBS) * row(decay_ref, r)) for r in range(modes)]
-
-    def scan_page(page, states):
-        value = pages_ref[slots_ref[page]].astype(jnp.float32)
-        start = pl.multiple_of(page * SUBS, SUBS)
-        signal[pl.ds(start, SUBS), :] = value
-        value = jnp.where(rows + page * SUBS > first, value, 0.0)
-        return tuple(s * l + value for s, l in zip(states, lam_page))
-
-    zero = jnp.zeros((SUBS, LANES), jnp.float32)
-    states = lax.fori_loop(0, page_count, scan_page, tuple(zero for _ in range(modes)), unroll=4)
-    rows_float = rows.astype(jnp.float32)
-    history = []
-    for r in range(modes):
-        decay = row(decay_ref, r)
-        weighted = states[r] * jnp.exp(-decay * (float(SUBS - 1) - rows_float))
-        total = jnp.sum(weighted, axis=0, keepdims=True)
-        history.append(jnp.broadcast_to(total, (SUBS, LANES)) * row(weight_ref, r))
+    from_block = [first >= span * block for block in range(blocks)]
+    turn = []
+    for kind in range(KEPT):
+        member = None
+        for block in range(kind, blocks, KEPT):
+            here = from_block[block]
+            if block + 1 < blocks:
+                here = here & jnp.logical_not(from_block[block + 1])
+            member = here if member is None else member | here
+        turn.append(member)
+
+    def place(index, carry):
+        kinds = []
+        for kind in range(KEPT):
+            value = pages_ref[order_ref[kind * per_block + index]].astype(jnp.float32)
+            for block in range(kind + KEPT, blocks, KEPT):
+                other = pages_ref[order_ref[block * per_block + index]].astype(jnp.float32)
+                value = jnp.where(from_block[block - KEPT + 1], other, value)
+            kinds.append(value)
+        start = pl.multiple_of(index * SUBS, SUBS)
+        for ahead in range(KEPT):
+            value = jnp.where(
+                turn[1],
+                kinds[(1 + ahead) % KEPT],
+                jnp.where(turn[2], kinds[(2 + ahead) % KEPT], kinds[ahead]),
+            )
+            signal[pl.ds(start + ahead * span, SUBS), :] = value
+        return carry
+
+    lax.fori_loop(0, per_block, place, 0, unroll=2)
 
     window = steps * SUBS
-    shift = cached // 2
-    reach = cached - window
+    shift = span // 2
     while shift >= 1:
-        keep = window + min(shift - 1, reach) if shift > 1 else window
-        keep = min(keep, cached - shift)
-        size = 128 if shift >= 128 else 64 if shift >= 64 else 32 if shift >= 32 else 16 if shift >= 16 else 8
-        chunk = min(size, 64)
-        count = -(-keep // chunk)
-        wide = (jnp.broadcast_to(first[0:1, :], (chunk, LANES)) & shift) != 0
-
-        def move(index, carry, chunk=chunk, wide=wide, shift=shift):
-            start = pl.multiple_of(index * chunk, chunk)
-            near = signal[pl.ds(start, chunk), :]
-            far = signal[pl.ds(start + shift, chunk), :]
-            signal[pl.ds(start, chunk), :] = jnp.where(wide, far, near)
+        count = -(-(window + shift - 1) // CHUNK)
+        wide = (jnp.broadcast_to(first[0:1, :], (CHUNK, LANES)) & shift) != 0
+
+        def move(index, carry, wide=wide, shift=shift):
+            start = pl.multiple_of(index * CHUNK, CHUNK)
+            near = signal[pl.ds(start, CHUNK), :]
+            far = signal[pl.ds(start + shift, CHUNK), :]
+            signal[pl.ds(start, CHUNK), :] = jnp.where(wide, far, near)
             return carry
 
         lax.fori_loop(0, count, move, 0)
@@ -182,11 +267,10 @@
     gain = [
         -row(weight_ref, r) * jnp.exp(-row(decay_ref, r) * length_float) for r in range(modes)
     ]
-    begin = []
-    for r in range(modes):
-        decay = row(decay_ref, r)
-        from_cache = history[r] * jnp.exp(-decay * (float(steps) * rows_float))
-        begin.append(from_cache + gain[r] * shift_down(inclusive_scan(ends[r], decay, steps), 1))
+    begin = [
+        gain[r] * shift_down(inclusive_scan(ends[r], row(decay_ref, r), steps), 1)
+        for r in range(modes)
+    ]
     segment_outputs(read, write, steps, lam, gain, begin)
     out_ref[...] = result[...].astype(jnp.bfloat16)
 
@@ -242,24 +326,59 @@
     )(base, state, decay, weight)
 
 
-def cache_conv(slots, pages, length, decay, weight, window):
+def smem(count):
+    return [pl.BlockSpec(memory_space=pltpu.SMEM) for _ in range(count)]
+
+
+def select_pages(place, slots, pool, params_of, modes, cached):
+    groups = len(params_of)
+    pencils = params_of[0].shape[1] // LANES
+    shape = (groups * pencils, KEPT * RANKS, pool.shape[1], LANES)
+    return pl.pallas_call(
+        functools.partial(select_kernel, modes, cached),
+        out_shape=jax.ShapeDtypeStruct(shape, pool.dtype),
+        in_specs=smem(2) + vmem(1 + groups),
+        out_specs=pl.BlockSpec(memory_space=pltpu.VMEM),
+        compiler_params=params(),
+        name="select_pages",
+    )(place, slots, pool, *params_of)
+
+
+def page_states(place, count, slots, where, pool, params_of, parcel, modes, cached):
+    groups = len(params_of)
+    width = params_of[0].shape[1]
+    return pl.pallas_call(
+        functools.partial(state_kernel, modes, cached),
+        out_shape=jax.ShapeDtypeStruct((groups, modes, width), jnp.float32),
+        in_specs=smem(4) + vmem(1 + groups) + [pl.BlockSpec(memory_space=pl.ANY)],
+        out_specs=pl.BlockSpec(memory_space=pltpu.VMEM),
+        scratch_shapes=[pltpu.VMEM((slots.shape[0], modes, LANES), jnp.float32)],
+        compiler_params=params(),
+        cost_estimate=pl.CostEstimate(
+            flops=4 * pool.size * modes, bytes_accessed=2 * pool.size, transcendentals=0
+        ),
+        name="page_states",
+    )(place, count, slots, where, pool, *params_of, parcel)
+
+
+def tail_conv(order, pages, length, decay, weight, window, blocks):
     modes = decay.shape[0]
-    cached = slots.shape[0] * SUBS
+    span = order.shape[0] // blocks * SUBS
     return pl.pallas_call(
-        functools.partial(cache_kernel, modes, window // SUBS),
+        functools.partial(tail_kernel, modes, window // SUBS, blocks),
         out_shape=jax.ShapeDtypeStruct((window, LANES), jnp.bfloat16),
-        in_specs=[pl.BlockSpec(memory_space=pltpu.SMEM)] + vmem(4),
+        in_specs=smem(1) + vmem(4),
         out_specs=pl.BlockSpec(memory_space=pltpu.VMEM),
         scratch_shapes=[
-            pltpu.VMEM((cached + 64, LANES), jnp.float32),
+            pltpu.VMEM((KEPT * span + CHUNK, LANES), jnp.float32),
             pltpu.VMEM((window, LANES), jnp.float32),
         ],
         compiler_params=params(),
         cost_estimate=pl.CostEstimate(
-            flops=4 * cached * LANES * modes, bytes_accessed=4 * cached * LANES, transcendentals=0
+            flops=12 * window * LANES * modes, bytes_accessed=8 * window * LANES, transcendentals=0
         ),
-        name="cache_conv",
-    )(slots, pages, length, decay, weight)
+        name="tail_conv",
+    )(order, pages, length, decay, weight)
 
 
 def gate_out(conv_home, base, gate_values):
@@ -283,33 +402,99 @@
     return state
 
 
+def spread(value, axis, count):
+    return [value] + [
+        lax.ppermute(value, axis, [(i, (i + hop) % count) for i in range(count)])
+        for hop in range(1, count)
+    ]
+
+
+def sum_halving(value, axis, place, count):
+    hop = 1
+    while hop < count:
+        bit = place // hop % 2
+        pairs = value.reshape(value.shape[0] // 2, 2, *value.shape[1:])
+        keep = lax.dynamic_index_in_dim(pairs, bit, 1, keepdims=False)
+        send = lax.dynamic_index_in_dim(pairs, 1 - bit, 1, keepdims=False)
+        value = keep + lax.ppermute(send, axis, [(i, i ^ hop) for i in range(count)])
+        hop *= 2
+    return value[0]
+
+
+def sum_doubling(value, axis, count):
+    hop = 1
+    while hop < count:
+        value = value + lax.ppermute(value, axis, [(i, i ^ hop) for i in range(count)])
+        hop *= 2
+    return value
+
+
 def local(
     window_input, gate_values, page_pool, page_table, filter_len, residues, decays, skip_gain
 ):
     ctx_count = lax.axis_size("ctx")
     chan_count = lax.axis_size("chan")
     ctx_pos = lax.axis_index("ctx")
-    pool_pages, page_len, width = page_pool.shape
-    rows = window_input.shape[0]
-    pencil = window_input.shape[1] // ctx_count
-    parcel = jnp.transpose(page_pool.reshape(pool_pages, page_len, -1, pencil), (2, 0, 1, 3))
+    chan_pos = lax.axis_index("chan")
+    pool_pages, page_len, _ = page_pool.shape
+    rows, slab = window_input.shape
+    modes = decays.shape[1]
+    pencil = slab // ctx_count
+    cached = page_table.shape[0] * page_len
+    rates = decays.T
+    weights = residues.T
+
+    packed = jnp.concatenate([rates, filter_len.astype(jnp.float32)[None, :]], axis=0)
+    params_of = spread(packed, "chan", chan_count)
+
+    owners = page_table // pool_pages
+    slots = page_table % pool_pages
+    table = owners.reshape(ctx_count, -1)
+    per_block = table.shape[1]
+    index = jnp.arange(per_block, dtype=jnp.int32)
+    earlier = (table[:, :, None] == table[:, None, :]) & (index[None, :] < index[:, None])[None]
+    rank = jnp.sum(earlier.astype(jnp.int32), axis=2)
+    block = jnp.arange(ctx_count, dtype=jnp.int32)[:, None]
+    source = table % chan_count * ctx_count + table // chan_count
+    order = (source * (KEPT * RANKS) + block % KEPT * RANKS + rank).reshape(-1)
+    mine = table == ctx_pos * chan_count + chan_pos
+    picked = mine[:, None, :] & (rank[:, None, :] == jnp.arange(RANKS, dtype=jnp.int32)[None, :, None])
+    slot_rows = slots.reshape(ctx_count, 1, per_block)
+    send_slots = jnp.sum(jnp.where(picked, slot_rows, 0), axis=2).reshape(-1)
+    page_rows = jnp.arange(page_table.shape[0], dtype=jnp.int32).reshape(ctx_count, 1, per_block)
+    send_pages = jnp.sum(jnp.where(picked, page_rows + 1, 0), axis=2).reshape(-1) - 1
+    used = send_pages >= 0
+    entry = jnp.arange(used.shape[0], dtype=jnp.int32)
+    before = jnp.sum((used[None, :] & (entry[None, :] < entry[:, None])).astype(jnp.int32), axis=1)
+    chosen = used[None, :] & (before[None, :] == entry[:, None])
+    list_slots = jnp.sum(jnp.where(chosen, send_slots[None, :], 0), axis=1)
+    list_pages = jnp.sum(jnp.where(chosen, send_pages[None, :] + 1, 0), axis=1) - 1
+    count = jnp.sum(used.astype(jnp.int32))
+
+    base, ends = window_conv(window_input, rates, weights, skip_gain[None, :])
+    state = start_states(ends, rates, rows, ctx_count)
+
+    parcel = select_pages(chan_pos[None], send_slots, page_pool, params_of, modes, cached)
     arrived = lax.all_to_all(parcel, ("chan", "ctx"), split_axis=0, concat_axis=0, tiled=True)
     arrived = arrived.reshape(-1, page_len, pencil)
-    owners = page_table // pool_pages
-    source = (owners % chan_count) * ctx_count + owners // chan_count
-    slots = source * pool_pages + page_table % pool_pages
+
+    from_pages = page_states(
+        chan_pos[None], count[None], list_slots, list_pages, page_pool, params_of, parcel, modes, cached
+    )
+    from_cache = sum_halving(from_pages, "chan", chan_pos, chan_count)
+    from_cache = sum_doubling(from_cache, "ctx", ctx_count)
+    state = state + jnp.exp(-rates * (ctx_pos * rows).astype(jnp.float32)) * from_cache
+    base = add_carry(base, state, rates, weights)
+
     start = ctx_pos * pencil
-    decay = lax.dynamic_slice_in_dim(decays, start, pencil, 0).T
-    weight = lax.dynamic_slice_in_dim(residues, start, pencil, 0).T
+    rate = lax.dynamic_slice_in_dim(rates, start, pencil, 1)
+    weight = lax.dynamic_slice_in_dim(weights, start, pencil, 1)
     length = lax.dynamic_slice_in_dim(filter_len, start, pencil, 0)[None, :]
-    base, ends = window_conv(window_input, decays.T, residues.T, skip_gain[None, :])
-    state = start_states(ends, decays.T, rows, ctx_count)
-    base = add_carry(base, state, decays.T, residues.T)
-    convolved = cache_conv(slots, arrived, length, decay, weight, rows * ctx_count)
-    conv_home = lax.all_to_all(
-        convolved.reshape(ctx_count, -1, pencil), "ctx", split_axis=0, concat_axis=0, tiled=True
+    tail = tail_conv(order, arrived, length, rate, weight, rows * ctx_count, ctx_count)
+    tail_home = lax.all_to_all(
+        tail.reshape(ctx_count, -1, pencil), "ctx", split_axis=0, concat_axis=0, tiled=True
     )
-    return gate_out(conv_home, base, gate_values)
+    return gate_out(tail_home, base, gate_values)
 
 
 def solution(mesh):

time: 107 us -> 116 us (1.084)
  waiting for transfers between devices: 44 us -> 19.6 us
  starting transfers between devices: 39.8 us -> 55.1 us
  Pallas kernels: 17.5 us -> 29.8 us
  other arithmetic: 0.08 us -> 3.8 us
  local copies, waits for them, and re-layouts: 5.26 us -> 6.45 us
    ppermute x1, waiting for transfers between devices: 39.4 us -> 0.01 us  [start_states(): state = lax.ppermute(ends, 'ctx', [(i, i + 1) for i in range(count - 1)])]
    ppermute x0 -> x13, starting transfers between devices: none -> 19.4 us  [the longest x7 8.96 us: spread(): lax.ppermute(value, axis, [(i, (i + hop) % count) for i in range(count)])]
    pallas_call x1 -> x3, Pallas kernels: 12.9 us -> 25.2 us  [the longest x1 16.6 us: page_states(): pl.pallas_call(functools.partial(state_kernel, modes, cached), out_shape=...]
    ppermute x0 -> x13, waiting for transfers between devices: none -> 11.3 us  [the longest x3 8.25 us: sum_doubling(): lax.ppermute(value, axis, [(i, i ^ hop) for i in range(count)])]
    ppermute x3, waiting for transfers between devices: 3.75 us -> 8.3 us  [start_states(): lax.ppermute(state, 'ctx', [(i, i + hop) for i in range(count - hop)])]
    all_to_all x1, starting transfers between devices: 6.06 us -> 3.41 us  [local(): lax.all_to_all(tail.reshape(ctx_count, -1, pencil), 'ctx', split_axis=0,...]
    unnamed x14 -> x18, local copies, waits for them, and re-layouts: 2.56 us -> 4.92 us
    transpose x3 -> x0, local copies, waits for them, and re-layouts: 1.93 us -> none  [the longest x1 1.91 us: local(): jnp.transpose(page_pool.reshape(pool_pages, page_len, -1, pencil), (2, 0,...]
  transfers between devices with their start and end apart: 6 -> 19, of which waited for: 4 -> 5; matrix products, arithmetic and copies ran while one was open for 1% -> 3% of each run, Pallas kernels for 16% -> 25%
where the time goes in v4:
time: 116 us; the launch traced here: 115 us
  starting transfers between devices  55.1 us (48%)
  Pallas kernels  29.8 us (26%)
  waiting for transfers between devices  19.6 us (17%)
  local copies, waits for them, and re-layouts  6.45 us (6%)
  other arithmetic  3.8 us (3%)
    ppermute x3, starting transfers between devices, start_states(): lax.ppermute(state, 'ctx', [(i, i + hop) for i in range(count - hop)])  17.1 us
    pallas_call x1, Pallas kernels, page_states(): pl.pallas_call(functools.partial(state_kernel, modes, cached), out_shape=...  16.6 us
    all_to_all x1, starting transfers between devices, local(): lax.all_to_all(parcel, ('chan', 'ctx'), split_axis=0, concat_axis=0, tile...  11.3 us
    ppermute x7, starting transfers between devices, spread(): lax.ppermute(value, axis, [(i, (i + hop) % count) for i in range(count)])  8.96 us
    ppermute x3, waiting for transfers between devices, start_states(): lax.ppermute(state, 'ctx', [(i, i + hop) for i in range(count - hop)])  8.3 us
    ppermute x3, waiting for transfers between devices, sum_doubling(): lax.ppermute(value, axis, [(i, i ^ hop) for i in range(count)])  8.25 us
    pallas_call x1, Pallas kernels, tail_conv(): pl.pallas_call(functools.partial(tail_kernel, modes, window // SUBS, bloc...  5.8 us
    ppermute x3, starting transfers between devices, sum_doubling(): lax.ppermute(value, axis, [(i, i ^ hop) for i in range(count)])  5.7 us
  transfers between devices with their start and end apart: 19, of which 5 were waited for; matrix products, arithmetic and copies ran while one was open for 3% of the time, Pallas kernels for 25%

profile of v4, /device:TPU:4, one launch (start us, length us, event | category | flops | bytes accessed | tf_op | source)
XLA Modules:
  0.0 115.1 jit_solution(8570553392738116200)
XLA Ops:
  0.7 0.8 pad_maximum_fusion.rest_0_
  1.5 1.7 %collective-permute-start.1 = (f32[17,1024]{1,0:T(8,128)S(1)}, f32[17,1024]{1,0:T(8,128)S(1)}, u32[]{:S(2)}, u32[]{:S(2)}) collective-permute-start(f32[17,1024]{1,0:T(8,128)S(1)} %pad_maximum_fusion.rest_0_), channel_id=1, source_target_pairs={{0,8},{4,12},{8,16},{12,20},{16,24},{20,28},{24,0},{28,4},{1,9},{5... | collective-permute-start | bytes 208904 | tf_op jit(solution)/shard_map/ppermute | solution.py:407
  3.2 2.2 %collective-permute-start.2 = (f32[17,1024]{1,0:T(8,128)S(1)}, f32[17,1024]{1,0:T(8,128)S(1)}, u32[]{:S(2)}, u32[]{:S(2)}) collective-permute-start(f32[17,1024]{1,0:T(8,128)S(1)} %pad_maximum_fusion.rest_0_), channel_id=1, source_target_pairs={{0,12},{4,16},{8,20},{12,24},{16,28},{20,0},{24,4},{28,8},{1,13},{... | collective-permute-start | bytes 208904 | tf_op jit(solution)/shard_map/ppermute | solution.py:407
  5.4 1.8 %collective-permute-start.3 = (f32[17,1024]{1,0:T(8,128)S(1)}, f32[17,1024]{1,0:T(8,128)S(1)}, u32[]{:S(2)}, u32[]{:S(2)}) collective-permute-start(f32[17,1024]{1,0:T(8,128)S(1)} %pad_maximum_fusion.rest_0_), channel_id=1, source_target_pairs={{0,16},{4,20},{8,24},{12,28},{16,0},{20,4},{24,8},{28,12},{1,17},{... | collective-permute-start | bytes 208904 | tf_op jit(solution)/shard_map/ppermute | solution.py:407
  7.3 1.8 %collective-permute-start.4 = (f32[17,1024]{1,0:T(8,128)S(1)}, f32[17,1024]{1,0:T(8,128)S(1)}, u32[]{:S(2)}, u32[]{:S(2)}) collective-permute-start(f32[17,1024]{1,0:T(8,128)S(1)} %pad_maximum_fusion.rest_0_), channel_id=1, source_target_pairs={{0,20},{4,24},{8,28},{12,0},{16,4},{20,8},{24,12},{28,16},{1,21},{... | collective-permute-start | bytes 208904 | tf_op jit(solution)/shard_map/ppermute | solution.py:407
  11.1 0.8 copy-done.2
  11.9 0.8 copy-done.4
  12.7 0.9 copy-done.7
  14.4 3.0 %window_conv.1 = (f32[128,1024]{1,0:T(8,128)S(1)}, f32[16,1024]{1,0:T(8,128)S(1)}) custom-call(bf16[128,1024]{1,0:T(8,128)(2,1)S(1)} %copy-done.7, f32[16,1024]{1,0:T(8,128)S(1)} %bitcast.31, f32[16,1024]{1,0:T(8,128)S(1)} %bitcast.35, f32[1,1024]{1,0:T(1,128)S(1)} %bitcast.37), custom_call_target="tpu_custom_call" | custom-call | flops 25165824 | bytes 786432 | tf_op jit(solution)/shard_map/window_conv/pallas_call | solution.py:296
  17.4 1.4 %collective-permute-start.5 = (f32[17,1024]{1,0:T(8,128)S(1)}, f32[17,1024]{1,0:T(8,128)S(1)}, u32[]{:S(2)}, u32[]{:S(2)}) collective-permute-start(f32[17,1024]{1,0:T(8,128)S(1)} %pad_maximum_fusion.rest_0_), channel_id=1, source_target_pairs={{0,24},{4,28},{8,0},{12,4},{16,8},{20,12},{24,16},{28,20},{1,25},{... | collective-permute-start | bytes 208904 | tf_op jit(solution)/shard_map/ppermute | solution.py:407
  19.5 3.8 %collective-permute-start.7 = (f32[16,1024]{1,0:T(8,128)S(1)}, f32[16,1024]{1,0:T(8,128)S(1)}, u32[]{:S(2)}, u32[]{:S(2)}) collective-permute-start(f32[16,1024]{1,0:T(8,128)S(1)} %get-tuple-element.8), channel_id=1, source_target_pairs={{0,32},{32,64},{64,96},{96,128},{128,160},{160,192},{192,224},{1,3... | collective-permute-start | bytes 196616 | tf_op jit(solution)/shard_map/ppermute | solution.py:396
  23.3 1.6 %copy-done = bf16[16,8,8192]{2,1,0:T(8,128)(2,1)S(1)} copy-done((bf16[16,8,8192]{2,1,0:T(8,128)(2,1)S(1)}, bf16[16,8,8192]{2,1,0:T(8,128)(2,1)}, u32[]{:S(2)}) %copy-start) | copy-done | bytes 2097176
  24.9 2.8 %select_pages.1.rest_8_ = bf16[64,6,8,128]{3,2,1,0:T(8,128)(2,1)} custom-call(s32[1]{0:T(128)} %bitcast.place_ref, s32[16]{0:T(128)S(1)} %reshape.102.slots_ref, bf16[16,8,8192]{2,1,0:T(8,128)(2,1)S(1)} %copy-done, f32[17,1024]{1,0:T(8,128)S(1)} %pad_maximum_fusion.rest_0_, f32[17,1024]{1,0:T(8,128)S(1)} %collective-permute-done.rest_1_, ...), custom_call_target="tpu_custom_call" | custom-call | tf_op jit(solution)/shard_map/select_pages/pallas_call | solution.py:337
  27.8 16.6 %page_states.1 = f32[8,16,1024]{2,1,0:T(8,128)S(1)} custom-call(s32[1]{0:T(128)} %bitcast.place_ref, s32[1]{0:T(128)} %bitcast.10.count_ref, s32[16]{0:T(128)S(1)} %get-tuple-element.12.slots_ref, s32[16]{0:T(128)S(1)} %broadcast_add_fusion.where_ref, bf16[16,8,8192]{2,1,0:T(8,128)(2,1)S(1)} %copy-done.1, f32[17,1024]{1,0:T(8,128)S(1)} %pad_maximum_fusion.rest_0_, ...), custom_call_target="tpu_custom_call" | custom-call | flops 67108864 | bytes 2097152 | tf_op jit(solution)/shard_map/page_states/pallas_call | solution.py:350
  44.7 11.3 %all-to-all-start = ((bf16[64,6,8,128]{3,2,1,0:T(8,128)(2,1)}), bf16[64,6,8,128]{3,2,1,0:T(8,128)(2,1)S(1)}, u32[]{:S(2)}, u32[]{:S(2)}) async-start(bf16[64,6,8,128]{3,2,1,0:T(8,128)(2,1)} %select_pages.1.rest_8_), calls=%async_computation | async-start | bytes 1572864 | tf_op jit(solution)/shard_map/all_to_all | solution.py:478
  56.2 1.7 %collective-permute-start.12 = (f32[2,16,1024]{2,1,0:T(8,128)S(1)}, f32[2,16,1024]{2,1,0:T(8,128)S(1)}, u32[]{:S(2)}, u32[]{:S(2)}) collective-permute-start(f32[2,16,1024]{2,1,0:T(8,128)S(1)} %dynamic-slice_bitcast_fusion.1), channel_id=1, source_target_pairs={{0,8},{4,12},{8,0},{12,4},{16,24},{20,28},{24,16},{28,20},{1,9},{5... | collective-permute-start | bytes 393224 | tf_op jit(solution)/shard_map/ppermute | solution.py:419
  57.9 3.4 %collective-permute-start.8 = (f32[16,1024]{1,0:T(8,128)S(1)}, f32[16,1024]{1,0:T(8,128)S(1)}, u32[]{:S(2)}, u32[]{:S(2)}) collective-permute-start(f32[16,1024]{1,0:T(8,128)S(1)} %collective-permute-done.7), channel_id=1, source_target_pairs={{0,32},{32,64},{64,96},{96,128},{128,160},{160,192},{192,224},{1,3... | collective-permute-start | bytes 196616 | tf_op jit(solution)/shard_map/ppermute | solution.py:399
  61.3 3.0 %collective-permute-done.12 = f32[2,16,1024]{2,1,0:T(8,128)S(1)} collective-permute-done((f32[2,16,1024]{2,1,0:T(8,128)S(1)}, f32[2,16,1024]{2,1,0:T(8,128)S(1)}, u32[]{:S(2)}, u32[]{:S(2)}) %collective-permute-start.12) | collective-permute-done | bytes 131104 | tf_op jit(solution)/shard_map/ppermute | solution.py:419
  64.4 3.0 %collective-permute-start.13 = (f32[1,16,1024]{2,1,0:T(8,128)S(1)}, f32[1,16,1024]{2,1,0:T(8,128)S(1)}, u32[]{:S(2)}, u32[]{:S(2)}) collective-permute-start(f32[1,16,1024]{2,1,0:T(8,128)S(1)} %constant_dynamic-slice_fusion), channel_id=1, source_target_pairs={{0,16},{4,20},{8,24},{12,28},{16,0},{20,4},{24,8},{28,12},{1,17},{... | collective-permute-start | bytes 196616 | tf_op jit(solution)/shard_map/ppermute | solution.py:419
  67.4 6.5 %collective-permute-done.8 = f32[16,1024]{1,0:T(8,128)S(1)} collective-permute-done((f32[16,1024]{1,0:T(8,128)S(1)}, f32[16,1024]{1,0:T(8,128)S(1)}, u32[]{:S(2)}, u32[]{:S(2)}) %collective-permute-start.8) | collective-permute-done | bytes 65568 | tf_op jit(solution)/shard_map/ppermute | solution.py:399
  73.9 6.0 %collective-permute-start.9 = (f32[16,1024]{1,0:T(8,128)S(1)}, f32[16,1024]{1,0:T(8,128)S(1)}, u32[]{:S(2)}, u32[]{:S(2)}) collective-permute-start(f32[16,1024]{1,0:T(8,128)S(1)} %multiply_add_fusion.2), channel_id=1, source_target_pairs={{0,64},{32,96},{64,128},{96,160},{128,192},{160,224},{1,65},{33,97... | collective-permute-start | bytes 196616 | tf_op jit(solution)/shard_map/ppermute | solution.py:399
  80.0 1.7 %collective-permute-start.14 = (f32[16,1024]{1,0:T(8,128)S(1)}, f32[16,1024]{1,0:T(8,128)S(1)}, u32[]{:S(2)}, u32[]{:S(2)}) collective-permute-start(f32[16,1024]{1,0:T(8,128)S(1)} %add_bitcast_fusion), channel_id=1, source_target_pairs={{0,32},{32,0},{64,96},{96,64},{128,160},{160,128},{192,224},{224,1... | collective-permute-start | bytes 196616 | tf_op jit(solution)/shard_map/ppermute | solution.py:427
  81.7 0.8 dynamic-slice_bitcast_fusion.4.length_ref
  82.5 1.8 %collective-permute-done.14 = f32[16,1024]{1,0:T(8,128)S(1)} collective-permute-done((f32[16,1024]{1,0:T(8,128)S(1)}, f32[16,1024]{1,0:T(8,128)S(1)}, u32[]{:S(2)}, u32[]{:S(2)}) %collective-permute-start.14) | collective-permute-done | bytes 65568 | tf_op jit(solution)/shard_map/ppermute | solution.py:427
  84.3 3.9 %collective-permute-start.15 = (f32[16,1024]{1,0:T(8,128)S(1)}, f32[16,1024]{1,0:T(8,128)S(1)}, u32[]{:S(2)}, u32[]{:S(2)}) collective-permute-start(f32[16,1024]{1,0:T(8,128)S(1)} %add.184), channel_id=1, source_target_pairs={{0,64},{32,96},{64,0},{96,32},{128,192},{160,224},{192,128},{224,1... | collective-permute-start | bytes 196616 | tf_op jit(solution)/shard_map/ppermute | solution.py:427
  88.2 5.8 %tail_conv.1 = bf16[1024,128]{1,0:T(8,128)(2,1)} custom-call(s32[512]{0:T(512)S(1)} %fusion.7.order_ref, bf16[384,8,128]{2,1,0:T(8,128)(2,1)S(1)} %bitcast.29, s32[1,128]{1,0:T(1,128)S(1)} %dynamic-slice_bitcast_fusion.4.length_ref, f32[16,128]{1,0:T(8,128)S(1)} %dynamic-slice_bitcast_fusion.3.decay_ref, f32[16,128]{1,0:T(8,128)S(1)} %dynamic-slice_bitcast_fusion.2.weight_ref), custom_call_target="tpu_custom_call" | custom-call | flops 25165824 | bytes 1048576 | tf_op jit(solution)/shard_map/tail_conv/pallas_call | solution.py:367
  94.0 3.4 %all-to-all-start.1 = ((bf16[8,128,128]{2,1,0:T(8,128)(2,1)}), bf16[8,128,128]{2,1,0:T(8,128)(2,1)S(1)}, u32[]{:S(2)}, u32[]{:S(2)}) async-start(bf16[8,128,128]{2,1,0:T(8,128)(2,1)} %bitcast.7), calls=%async_computation.1 | async-start | bytes 524288 | tf_op jit(solution)/shard_map/all_to_all | solution.py:494
  97.5 7.7 %collective-permute-start.10 = (f32[16,1024]{1,0:T(8,128)S(1)}, f32[16,1024]{1,0:T(8,128)S(1)}, u32[]{:S(2)}, u32[]{:S(2)}) collective-permute-start(f32[16,1024]{1,0:T(8,128)S(1)} %multiply_add_fusion.1), channel_id=1, source_target_pairs={{0,128},{32,160},{64,192},{96,224},{1,129},{33,161},{65,193},{97,2... | collective-permute-start | bytes 196616 | tf_op jit(solution)/shard_map/ppermute | solution.py:399
  105.3 1.8 %collective-permute-done.10 = f32[16,1024]{1,0:T(8,128)S(1)} collective-permute-done((f32[16,1024]{1,0:T(8,128)S(1)}, f32[16,1024]{1,0:T(8,128)S(1)}, u32[]{:S(2)}, u32[]{:S(2)}) %collective-permute-start.10) | collective-permute-done | bytes 65568 | tf_op jit(solution)/shard_map/ppermute | solution.py:399
  107.1 6.4 %collective-permute-done.16 = f32[16,1024]{1,0:T(8,128)S(1)} collective-permute-done((f32[16,1024]{1,0:T(8,128)S(1)}, f32[16,1024]{1,0:T(8,128)S(1)}, u32[]{:S(2)}, u32[]{:S(2)}) %collective-permute-start.16) | collective-permute-done | bytes 65568 | tf_op jit(solution)/shard_map/ppermute | solution.py:427
  113.5 0.8 add_carry.1.base_ref
  114.3 0.8 gate_out.1
  (68 shorter events, 4.7 us)
Async XLA Ops:
  1.5 15.9 %collective-permute-start = (f32[17,1024]{1,0:T(8,128)S(1)}, f32[17,1024]{1,0:T(8,128)S(1)}, u32[]{:S(2)}, u32[]{:S(2)}) collective-permute-start(f32[17,1024]{1,0:T(8,128)S(1)} %pad_maximum_fusion.rest_0_), channel_id=1, source_target_pairs={{0,4},{4,8},{8,12},{12,16},{16,20},{20,24},{24,28},{28,0},{1,5},{5... | collective-permute-start | bytes 208904 | tf_op jit(solution)/shard_map/ppermute | solution.py:407
  1.5 17.3 %collective-permute-start.1 = (f32[17,1024]{1,0:T(8,128)S(1)}, f32[17,1024]{1,0:T(8,128)S(1)}, u32[]{:S(2)}, u32[]{:S(2)}) collective-permute-start(f32[17,1024]{1,0:T(8,128)S(1)} %pad_maximum_fusion.rest_0_), channel_id=1, source_target_pairs={{0,8},{4,12},{8,16},{12,20},{16,24},{20,28},{24,0},{28,4},{1,9},{5... | collective-permute-start | bytes 208904 | tf_op jit(solution)/shard_map/ppermute | solution.py:407
  3.2 16.3 %collective-permute-start.2 = (f32[17,1024]{1,0:T(8,128)S(1)}, f32[17,1024]{1,0:T(8,128)S(1)}, u32[]{:S(2)}, u32[]{:S(2)}) collective-permute-start(f32[17,1024]{1,0:T(8,128)S(1)} %pad_maximum_fusion.rest_0_), channel_id=1, source_target_pairs={{0,12},{4,16},{8,20},{12,24},{16,28},{20,0},{24,4},{28,8},{1,13},{... | collective-permute-start | bytes 208904 | tf_op jit(solution)/shard_map/ppermute | solution.py:407
  5.4 17.9 %collective-permute-start.3 = (f32[17,1024]{1,0:T(8,128)S(1)}, f32[17,1024]{1,0:T(8,128)S(1)}, u32[]{:S(2)}, u32[]{:S(2)}) collective-permute-start(f32[17,1024]{1,0:T(8,128)S(1)} %pad_maximum_fusion.rest_0_), channel_id=1, source_target_pairs={{0,16},{4,20},{8,24},{12,28},{16,0},{20,4},{24,8},{28,12},{1,17},{... | collective-permute-start | bytes 208904 | tf_op jit(solution)/shard_map/ppermute | solution.py:407
  7.3 16.1 %collective-permute-start.4 = (f32[17,1024]{1,0:T(8,128)S(1)}, f32[17,1024]{1,0:T(8,128)S(1)}, u32[]{:S(2)}, u32[]{:S(2)}) collective-permute-start(f32[17,1024]{1,0:T(8,128)S(1)} %pad_maximum_fusion.rest_0_), channel_id=1, source_target_pairs={{0,20},{4,24},{8,28},{12,0},{16,4},{20,8},{24,12},{28,16},{1,21},{... | collective-permute-start | bytes 208904 | tf_op jit(solution)/shard_map/ppermute | solution.py:407
  11.1 0.8 copy-start.2
  11.9 0.8 copy-start.4
  12.7 0.9 copy-start.7
  13.7 0.7 copy-start.8
  17.4 5.9 %collective-permute-start.5 = (f32[17,1024]{1,0:T(8,128)S(1)}, f32[17,1024]{1,0:T(8,128)S(1)}, u32[]{:S(2)}, u32[]{:S(2)}) collective-permute-start(f32[17,1024]{1,0:T(8,128)S(1)} %pad_maximum_fusion.rest_0_), channel_id=1, source_target_pairs={{0,24},{4,28},{8,0},{12,4},{16,8},{20,12},{24,16},{28,20},{1,25},{... | collective-permute-start | bytes 208904 | tf_op jit(solution)/shard_map/ppermute | solution.py:407
  18.8 4.5 %collective-permute-start.6 = (f32[17,1024]{1,0:T(8,128)S(1)}, f32[17,1024]{1,0:T(8,128)S(1)}, u32[]{:S(2)}, u32[]{:S(2)}) collective-permute-start(f32[17,1024]{1,0:T(8,128)S(1)} %pad_maximum_fusion.rest_0_), channel_id=1, source_target_pairs={{0,28},{4,0},{8,4},{12,8},{16,12},{20,16},{24,20},{28,24},{1,29},{... | collective-permute-start | bytes 208904 | tf_op jit(solution)/shard_map/ppermute | solution.py:407
  19.5 38.4 %collective-permute-start.7 = (f32[16,1024]{1,0:T(8,128)S(1)}, f32[16,1024]{1,0:T(8,128)S(1)}, u32[]{:S(2)}, u32[]{:S(2)}) collective-permute-start(f32[16,1024]{1,0:T(8,128)S(1)} %get-tuple-element.8), channel_id=1, source_target_pairs={{0,32},{32,64},{64,96},{96,128},{128,160},{160,192},{192,224},{1,3... | collective-permute-start | bytes 196616 | tf_op jit(solution)/shard_map/ppermute | solution.py:396
  23.3 1.6 %copy-start = (bf16[16,8,8192]{2,1,0:T(8,128)(2,1)S(1)}, bf16[16,8,8192]{2,1,0:T(8,128)(2,1)}, u32[]{:S(2)}) copy-start(bf16[16,8,8192]{2,1,0:T(8,128)(2,1)} %pool_ref.3) | copy-start | bytes 6291460
  24.9 2.8 %copy-start.1 = (bf16[16,8,8192]{2,1,0:T(8,128)(2,1)S(1)}, bf16[16,8,8192]{2,1,0:T(8,128)(2,1)}, u32[]{:S(2)}) copy-start(bf16[16,8,8192]{2,1,0:T(8,128)(2,1)} %pool_ref.3) | copy-start | bytes 6291460
  44.3 13.5 %copy-start.5 = (f32[1024,16]{0,1:T(8,128)S(1)}, f32[1024,16]{0,1:T(8,128)}, u32[]{:S(2)}) copy-start(f32[1024,16]{0,1:T(8,128)} %param.13) | copy-start | bytes 196612
  44.3 13.5 %copy-start.3 = (f32[1024,16]{0,1:T(8,128)S(1)}, f32[1024,16]{0,1:T(8,128)}, u32[]{:S(2)}) copy-start(f32[1024,16]{0,1:T(8,128)} %param.14) | copy-start | bytes 196612
  44.4 11.7 %collective-permute-start.11 = (f32[4,16,1024]{2,1,0:T(8,128)S(1)}, f32[4,16,1024]{2,1,0:T(8,128)S(1)}, u32[]{:S(2)}, u32[]{:S(2)}) collective-permute-start(f32[4,16,1024]{2,1,0:T(8,128)S(1)} %dynamic-slice_bitcast_fusion), channel_id=1, source_target_pairs={{0,4},{4,0},{8,12},{12,8},{16,20},{20,16},{24,28},{28,24},{1,5},{5... | collective-permute-start | bytes 786440 | tf_op jit(solution)/shard_map/ppermute | solution.py:419
  44.7 43.5 %all-to-all-start = ((bf16[64,6,8,128]{3,2,1,0:T(8,128)(2,1)}), bf16[64,6,8,128]{3,2,1,0:T(8,128)(2,1)S(1)}, u32[]{:S(2)}, u32[]{:S(2)}) async-start(bf16[64,6,8,128]{3,2,1,0:T(8,128)(2,1)} %select_pages.1.rest_8_), calls=%async_computation | async-start | bytes 1572864 | tf_op jit(solution)/shard_map/all_to_all | solution.py:478
  56.2 8.1 %collective-permute-start.12 = (f32[2,16,1024]{2,1,0:T(8,128)S(1)}, f32[2,16,1024]{2,1,0:T(8,128)S(1)}, u32[]{:S(2)}, u32[]{:S(2)}) collective-permute-start(f32[2,16,1024]{2,1,0:T(8,128)S(1)} %dynamic-slice_bitcast_fusion.1), channel_id=1, source_target_pairs={{0,8},{4,12},{8,0},{12,4},{16,24},{20,28},{24,16},{28,20},{1,9},{5... | collective-permute-start | bytes 393224 | tf_op jit(solution)/shard_map/ppermute | solution.py:419
  57.9 16.0 %collective-permute-start.8 = (f32[16,1024]{1,0:T(8,128)S(1)}, f32[16,1024]{1,0:T(8,128)S(1)}, u32[]{:S(2)}, u32[]{:S(2)}) collective-permute-start(f32[16,1024]{1,0:T(8,128)S(1)} %collective-permute-done.7), channel_id=1, source_target_pairs={{0,32},{32,64},{64,96},{96,128},{128,160},{160,192},{192,224},{1,3... | collective-permute-start | bytes 196616 | tf_op jit(solution)/shard_map/ppermute | solution.py:399
  64.4 15.6 %collective-permute-start.13 = (f32[1,16,1024]{2,1,0:T(8,128)S(1)}, f32[1,16,1024]{2,1,0:T(8,128)S(1)}, u32[]{:S(2)}, u32[]{:S(2)}) collective-permute-start(f32[1,16,1024]{2,1,0:T(8,128)S(1)} %constant_dynamic-slice_fusion), channel_id=1, source_target_pairs={{0,16},{4,20},{8,24},{12,28},{16,0},{20,4},{24,8},{28,12},{1,17},{... | collective-permute-start | bytes 196616 | tf_op jit(solution)/shard_map/ppermute | solution.py:419
  73.9 40.4 %copy-start.6 = (bf16[128,1024]{1,0:T(8,128)(2,1)S(1)}, bf16[128,1024]{1,0:T(8,128)(2,1)}, u32[]{:S(2)}) copy-start(bf16[128,1024]{1,0:T(8,128)(2,1)} %gate_ref.1) | copy-start | bytes 786436
  73.9 23.5 %collective-permute-start.9 = (f32[16,1024]{1,0:T(8,128)S(1)}, f32[16,1024]{1,0:T(8,128)S(1)}, u32[]{:S(2)}, u32[]{:S(2)}) collective-permute-start(f32[16,1024]{1,0:T(8,128)S(1)} %multiply_add_fusion.2), channel_id=1, source_target_pairs={{0,64},{32,96},{64,128},{96,160},{128,192},{160,224},{1,65},{33,97... | collective-permute-start | bytes 196616 | tf_op jit(solution)/shard_map/ppermute | solution.py:399
  80.0 4.4 %collective-permute-start.14 = (f32[16,1024]{1,0:T(8,128)S(1)}, f32[16,1024]{1,0:T(8,128)S(1)}, u32[]{:S(2)}, u32[]{:S(2)}) collective-permute-start(f32[16,1024]{1,0:T(8,128)S(1)} %add_bitcast_fusion), channel_id=1, source_target_pairs={{0,32},{32,0},{64,96},{96,64},{128,160},{160,128},{192,224},{224,1... | collective-permute-start | bytes 196616 | tf_op jit(solution)/shard_map/ppermute | solution.py:427
  84.3 20.9 %collective-permute-start.15 = (f32[16,1024]{1,0:T(8,128)S(1)}, f32[16,1024]{1,0:T(8,128)S(1)}, u32[]{:S(2)}, u32[]{:S(2)}) collective-permute-start(f32[16,1024]{1,0:T(8,128)S(1)} %add.184), channel_id=1, source_target_pairs={{0,64},{32,96},{64,0},{96,32},{128,192},{160,224},{192,128},{224,1... | collective-permute-start | bytes 196616 | tf_op jit(solution)/shard_map/ppermute | solution.py:427
  94.0 20.3 %all-to-all-start.1 = ((bf16[8,128,128]{2,1,0:T(8,128)(2,1)}), bf16[8,128,128]{2,1,0:T(8,128)(2,1)S(1)}, u32[]{:S(2)}, u32[]{:S(2)}) async-start(bf16[8,128,128]{2,1,0:T(8,128)(2,1)} %bitcast.7), calls=%async_computation.1 | async-start | bytes 524288 | tf_op jit(solution)/shard_map/all_to_all | solution.py:494
  97.5 9.6 %collective-permute-start.10 = (f32[16,1024]{1,0:T(8,128)S(1)}, f32[16,1024]{1,0:T(8,128)S(1)}, u32[]{:S(2)}, u32[]{:S(2)}) collective-permute-start(f32[16,1024]{1,0:T(8,128)S(1)} %multiply_add_fusion.1), channel_id=1, source_target_pairs={{0,128},{32,160},{64,192},{96,224},{1,129},{33,161},{65,193},{97,2... | collective-permute-start | bytes 196616 | tf_op jit(solution)/shard_map/ppermute | solution.py:399
  105.2 8.3 %collective-permute-start.16 = (f32[16,1024]{1,0:T(8,128)S(1)}, f32[16,1024]{1,0:T(8,128)S(1)}, u32[]{:S(2)}, u32[]{:S(2)}) collective-permute-start(f32[16,1024]{1,0:T(8,128)S(1)} %add.185), channel_id=1, source_target_pairs={{0,128},{32,160},{64,192},{96,224},{128,0},{160,32},{192,64},{224,... | collective-permute-start | bytes 196616 | tf_op jit(solution)/shard_map/ppermute | solution.py:427

commit v5 on v3

--- a/solution.py
+++ b/solution.py
@@ -9,7 +9,10 @@
 
 LANES = 128
 SUBS = 8
-VMEM_LIMIT = 32 * 1024 * 1024
+CHUNK = 128
+PIECES = 4
+VMEM_LIMIT = 12 * 1024 * 1024
+WHOLE_VMEM = 60 * 1024 * 1024
 
 
 def row(ref, index):
@@ -85,20 +88,8 @@
 
 
 def cache_kernel(
-    modes,
-    steps,
-    place_ref,
-    slots_ref,
-    pages_ref,
-    length_ref,
-    decay_ref,
-    weight_ref,
-    *rest,
+    modes, steps, slots_ref, pages_ref, length_ref, decay_ref, weight_ref, tail_ref, begin_ref, signal
 ):
-    end_refs, (out_ref, signal, result, before) = rest[:SUBS], rest[SUBS:]
-    for hop, end_ref in enumerate(end_refs):
-        segment = lax.rem(place_ref[0] + (SUBS - hop), SUBS)
-        before[pl.ds(segment, modes, stride=SUBS), :] = end_ref[...]
     page_count = slots_ref.shape[0]
     cached = page_count * SUBS
     rows = lax.broadcasted_iota(jnp.int32, (SUBS, LANES), 0)
@@ -115,59 +106,87 @@
         return tuple(s * l + value for s, l in zip(states, lam_page))
 
     zero = jnp.zeros((SUBS, LANES), jnp.float32)
-    states = lax.fori_loop(0, page_count, scan_page, tuple(zero for _ in range(modes)), unroll=4)
+    states = lax.fori_loop(0, page_count, scan_page, tuple(zero for _ in range(modes)), unroll=16)
     rows_float = rows.astype(jnp.float32)
-    history = []
     for r in range(modes):
         decay = row(decay_ref, r)
         weighted = states[r] * jnp.exp(-decay * (float(SUBS - 1) - rows_float))
-        total = jnp.sum(weighted, axis=0, keepdims=True)
-        history.append(jnp.broadcast_to(total, (SUBS, LANES)) * row(weight_ref, r))
+        total = jnp.broadcast_to(jnp.sum(weighted, axis=0, keepdims=True), (SUBS, LANES))
+        ahead = jnp.exp(-decay * (float(steps) * rows_float))
+        begin_ref[r * SUBS : (r + 1) * SUBS, :] = row(weight_ref, r) * total * ahead
 
     window = steps * SUBS
     shift = cached // 2
-    reach = cached - window
     while shift >= 1:
-        keep = window + min(shift - 1, reach) if shift > 1 else window
-        keep = min(keep, cached - shift)
-        size = 128 if shift >= 128 else 64 if shift >= 64 else 32 if shift >= 32 else 16 if shift >= 16 else 8
-        chunk = min(size, 64)
-        count = -(-keep // chunk)
-        wide = (jnp.broadcast_to(first[0:1, :], (chunk, LANES)) & shift) != 0
-
-        def move(index, carry, chunk=chunk, wide=wide, shift=shift):
-            start = pl.multiple_of(index * chunk, chunk)
-            near = signal[pl.ds(start, chunk), :]
-            far = signal[pl.ds(start + shift, chunk), :]
-            signal[pl.ds(start, chunk), :] = jnp.where(wide, far, near)
+        keep = min(window + shift - 1, cached - shift)
+        wide = (jnp.broadcast_to(first[0:1, :], (CHUNK, LANES)) & shift) != 0
+        into = tail_ref if shift == 1 else signal
+
+        def move(index, carry, wide=wide, shift=shift, into=into):
+            start = pl.multiple_of(index * CHUNK, CHUNK)
+            near = signal[pl.ds(start, CHUNK), :]
+            far = signal[pl.ds(start + shift, CHUNK), :]
+            into[pl.ds(start, CHUNK), :] = jnp.where(wide, far, near)
             return carry
 
-        lax.fori_loop(0, count, move, 0)
+        lax.fori_loop(0, -(-keep // CHUNK), move, 0)
         shift //= 2
-    signal[0:SUBS, :] = jnp.where(rows > 0, signal[0:SUBS, :], 0.0)
-
-    lam = [jnp.exp(-row(decay_ref, r)) for r in range(modes)]
+    tail_ref[0:SUBS, :] = jnp.where(rows > 0, tail_ref[0:SUBS, :], 0.0)
 
     def read(step):
-        return signal[pl.ds(step, SUBS, stride=steps), :]
+        return tail_ref[pl.ds(step, SUBS, stride=steps), :]
+
+    ends = segment_states(read, steps, [jnp.exp(-row(decay_ref, r)) for r in range(modes)])
+    length_float = length.astype(jnp.float32)
+    for r in range(modes):
+        decay = row(decay_ref, r)
+        prior = shift_down(inclusive_scan(ends[r], decay, steps), 1)
+        gone = row(weight_ref, r) * jnp.exp(-decay * length_float) * prior
+        here = slice(r * SUBS, (r + 1) * SUBS)
+        begin_ref[here, :] = begin_ref[here, :] - gone
+
+
+def output_kernel(
+    modes, steps, place_ref, length_ref, decay_ref, weight_ref, tail_ref, begin_ref, *rest
+):
+    end_refs, (out_ref, result, before) = rest[:SUBS], rest[SUBS:]
+    for hop, end_ref in enumerate(end_refs):
+        segment = lax.rem(place_ref[0] + (SUBS - hop), SUBS)
+        before[pl.ds(segment, modes, stride=SUBS), :] = end_ref[...]
+    length_float = jnp.broadcast_to(length_ref[...], (SUBS, LANES)).astype(jnp.float32)
+    begin, lam, gain = [], [], []
+    for r in range(modes):
+        decay = row(decay_ref, r)
+        here = slice(r * SUBS, (r + 1) * SUBS)
+        prior = shift_down(inclusive_scan(before[here, :], decay, steps), 1)
+        begin.append(begin_ref[here, :] + row(weight_ref, r) * prior)
+        lam.append(jnp.exp(-decay))
+        gain.append(-row(weight_ref, r) * jnp.exp(-decay * length_float))
+
+    def read(step):
+        return tail_ref[pl.ds(step, SUBS, stride=steps), :]
 
     def write(step, value):
         result[pl.ds(step, SUBS, stride=steps), :] = value
 
-    ends = segment_states(read, steps, lam)
-    length_float = length.astype(jnp.float32)
-    gain = [
-        -row(weight_ref, r) * jnp.exp(-row(decay_ref, r) * length_float) for r in range(modes)
-    ]
-    begin = []
-    for r in range(modes):
-        decay = row(decay_ref, r)
-        from_cache = history[r] * jnp.exp(-decay * (float(steps) * rows_float))
-        prior = inclusive_scan(before[r * SUBS : (r + 1) * SUBS, :], decay, steps)
-        from_cache = from_cache + row(weight_ref, r) * shift_down(prior, 1)
-        begin.append(from_cache + gain[r] * shift_down(inclusive_scan(ends[r], decay, steps), 1))
     segment_outputs(read, write, steps, lam, gain, begin)
     out_ref[...] = result[...].astype(jnp.bfloat16)
+
+
+def parcel_kernel(pool_ref, parcel_ref):
+    pages, page_len, _ = pool_ref.shape
+    each = parcel_ref.shape[0] // PIECES
+
+    def piece(from_ref, to_ref):
+        for block in range(each):
+            to_ref[block] = from_ref[:, :, block * LANES : (block + 1) * LANES]
+
+    pltpu.emit_pipeline(
+        piece,
+        grid=(PIECES,),
+        in_specs=[pl.BlockSpec((pages, page_len, each * LANES), lambda i: (0, 0, i))],
+        out_specs=[pl.BlockSpec((each, pages, page_len, LANES), lambda i: (i, 0, 0, 0))],
+    )(pool_ref, parcel_ref)
 
 
 def gate_kernel(conv_ref, base_ref, gate_ref, out_ref):
@@ -181,8 +200,8 @@
     return [pl.BlockSpec(memory_space=pltpu.VMEM) for _ in range(count)]
 
 
-def params():
-    return pltpu.CompilerParams(vmem_limit_bytes=VMEM_LIMIT)
+def params(limit=VMEM_LIMIT):
+    return pltpu.CompilerParams(vmem_limit_bytes=limit)
 
 
 def window_conv(window, decay, weight, skip):
@@ -205,25 +224,53 @@
     )(window, decay, weight, skip)
 
 
-def cache_conv(place, slots, pages, length, decay, weight, ends, window):
+def cache_conv(slots, pages, length, decay, weight, window):
     modes = decay.shape[0]
     cached = slots.shape[0] * SUBS
     return pl.pallas_call(
         functools.partial(cache_kernel, modes, window // SUBS),
+        out_shape=(
+            jax.ShapeDtypeStruct((window, LANES), jnp.float32),
+            jax.ShapeDtypeStruct((modes * SUBS, LANES), jnp.float32),
+        ),
+        in_specs=[pl.BlockSpec(memory_space=pltpu.SMEM)] + vmem(4),
+        out_specs=tuple(vmem(2)),
+        scratch_shapes=[pltpu.VMEM((cached + CHUNK, LANES), jnp.float32)],
+        compiler_params=params(),
+        cost_estimate=pl.CostEstimate(
+            flops=40 * cached * LANES * modes, bytes_accessed=4 * cached * LANES, transcendentals=0
+        ),
+        name="cache_conv",
+    )(slots, pages, length, decay, weight)
+
+
+def output_conv(place, length, decay, weight, tail, begin, ends):
+    modes = decay.shape[0]
+    window = tail.shape[0]
+    return pl.pallas_call(
+        functools.partial(output_kernel, modes, window // SUBS),
         out_shape=jax.ShapeDtypeStruct((window, LANES), jnp.bfloat16),
-        in_specs=[pl.BlockSpec(memory_space=pltpu.SMEM)] * 2 + vmem(4 + len(ends)),
+        in_specs=[pl.BlockSpec(memory_space=pltpu.SMEM)] + vmem(5 + len(ends)),
         out_specs=pl.BlockSpec(memory_space=pltpu.VMEM),
         scratch_shapes=[
-            pltpu.VMEM((cached + 64, LANES), jnp.float32),
             pltpu.VMEM((window, LANES), jnp.float32),
             pltpu.VMEM((modes * SUBS, LANES), jnp.float32),
         ],
         compiler_params=params(),
-        cost_estimate=pl.CostEstimate(
-            flops=4 * cached * LANES * modes, bytes_accessed=4 * cached * LANES, transcendentals=0
-        ),
-        name="cache_conv",
-    )(place, slots, pages, length, decay, weight, *ends)
+        name="output_conv",
+    )(place, length, decay, weight, tail, begin, *ends)
+
+
+def parcel_of(pool):
+    pages, page_len, width = pool.shape
+    return pl.pallas_call(
+        parcel_kernel,
+        out_shape=jax.ShapeDtypeStruct((width // LANES, pages, page_len, LANES), pool.dtype),
+        in_specs=[pl.BlockSpec(memory_space=pl.ANY)],
+        out_specs=pl.BlockSpec(memory_space=pl.ANY),
+        compiler_params=params(WHOLE_VMEM),
+        name="parcel_of",
+    )(pool)
 
 
 def gate_out(conv_home, base, gate_values):
@@ -258,8 +305,9 @@
     pool_pages, page_len, width = page_pool.shape
     rows = window_input.shape[0]
     pencil = window_input.shape[1] // ctx_count
-    parcel = jnp.transpose(page_pool.reshape(pool_pages, page_len, -1, pencil), (2, 0, 1, 3))
-    arrived = lax.all_to_all(parcel, ("chan", "ctx"), split_axis=0, concat_axis=0, tiled=True)
+    arrived = lax.all_to_all(
+        parcel_of(page_pool), ("chan", "ctx"), split_axis=0, concat_axis=0, tiled=True
+    )
     arrived = arrived.reshape(-1, page_len, pencil)
     owners = page_table // pool_pages
     source = (owners % chan_count) * ctx_count + owners // chan_count
@@ -270,9 +318,8 @@
     length = lax.dynamic_slice_in_dim(filter_len, start, pencil, 0)[None, :]
     base, ends = window_conv(window_input, decays.T, residues.T, skip_gain[None, :])
     ends = end_states(ends, ctx_pos, ctx_count)
-    convolved = cache_conv(
-        ctx_pos[None], slots, arrived, length, decay, weight, ends, rows * ctx_count
-    )
+    tail, begin = cache_conv(slots, arrived, length, decay, weight, rows * ctx_count)
+    convolved = output_conv(ctx_pos[None], length, decay, weight, tail, begin, ends)
     conv_home = lax.all_to_all(
         convolved.reshape(ctx_count, -1, pencil), "ctx", split_axis=0, concat_axis=0, tiled=True
     )

time: 99 us -> 93.1 us (0.940)
  local copies, waits for them, and re-layouts: 4.34 us -> 0.14 us
  Pallas kernels: 16.2 us -> 15.2 us
    pallas_call x1, Pallas kernels: 12.3 us -> 5.59 us  [cache_conv(): pl.pallas_call(functools.partial(cache_kernel, modes, window // SUBS), ou...]
    pallas_call x0 -> x2, Pallas kernels: none -> 5.75 us  [the longest x1 3.94 us: parcel_of(): pl.pallas_call(parcel_kernel, out_shape=jax.ShapeDtypeStruct((width // LA...]
    transpose x1 -> x0, local copies, waits for them, and re-layouts: 1.91 us -> none  [local(): jnp.transpose(page_pool.reshape(pool_pages, page_len, -1, pencil), (2, 0,...]
    unnamed x14, local copies, waits for them, and re-layouts: 1.62 us -> 0.03 us
  transfers between devices with their start and end apart: 8 -> 8, of which waited for: 2 -> 1; matrix products, arithmetic and copies ran while one was open for 1% -> 0% of each run, Pallas kernels for 3% -> 9%
where the time goes in v5:
time: 93.1 us; the launch traced here: 92.5 us
  waiting for transfers between devices  33.9 us (36%)
  starting transfers between devices  28.4 us (31%)
  Pallas kernels  15.2 us (16%)
  blocking collectives  14.7 us (16%)
    ppermute x7, waiting for transfers between devices, end_states(): lax.ppermute(block(hop), 'ctx', [(i, (i + hop) % count) for i in range(co...  33.9 us
    ppermute x7, starting transfers between devices, end_states(): lax.ppermute(block(hop), 'ctx', [(i, (i + hop) % count) for i in range(co...  16.1 us
    all_to_all x1, blocking collectives, local(): lax.all_to_all(convolved.reshape(ctx_count, -1, pencil), 'ctx', split_axi...  14.7 us
    all_to_all x1, starting transfers between devices, local(): lax.all_to_all(parcel_of(page_pool), ('chan', 'ctx'), split_axis=0, conca...  12.2 us
    pallas_call x1, Pallas kernels, cache_conv(): pl.pallas_call(functools.partial(cache_kernel, modes, window // SUBS), ou...  5.59 us
    pallas_call x1, Pallas kernels, parcel_of(): pl.pallas_call(parcel_kernel, out_shape=jax.ShapeDtypeStruct((width // LA...  3.94 us
    pallas_call x1, Pallas kernels, window_conv(): pl.pallas_call(functools.partial(window_kernel, modes, rows // SUBS), out...  3.02 us
  transfers between devices with their start and end apart: 8, of which 1 were waited for; matrix products, arithmetic and copies ran while one was open for 0% of the time, Pallas kernels for 9%

profile of v5, /device:TPU:4, one launch (start us, length us, event | category | flops | bytes accessed | tf_op | source)
XLA Modules:
  0.0 92.5 jit_solution(16704663704138446655)
XLA Ops:
  0.0 0.0 copy-start
  0.0 3.9 %parcel_of.1 = bf16[64,16,8,128]{3,2,1,0:T(8,128)(2,1)} custom-call(bf16[16,8,8192]{2,1,0:T(8,128)(2,1)} %pool_ref.1), custom_call_target="tpu_custom_call" | custom-call | tf_op jit(solution)/shard_map/parcel_of/pallas_call | solution.py:266
  4.0 12.2 %all-to-all-start = ((bf16[64,16,8,128]{3,2,1,0:T(8,128)(2,1)}), bf16[64,16,8,128]{3,2,1,0:T(8,128)(2,1)S(1)}, u32[]{:S(2)}, u32[]{:S(2)}) async-start(bf16[64,16,8,128]{3,2,1,0:T(8,128)(2,1)} %parcel_of.1), calls=%async_computation | async-start | bytes 4194304 | tf_op jit(solution)/shard_map/all_to_all | solution.py:308
  16.3 0.0 copy-start.1
  16.3 0.0 copy-done.2
  16.4 0.0 copy-done.3
  16.4 0.0 copy-done.4
  16.4 0.0 copy-done.5
  16.4 3.0 %window_conv.1 = (f32[128,1024]{1,0:T(8,128)S(1)}, f32[16,1024]{1,0:T(8,128)S(1)}) custom-call(bf16[128,1024]{1,0:T(8,128)(2,1)S(1)} %copy-done.2, f32[16,1024]{1,0:T(8,128)S(1)} %bitcast.15, f32[16,1024]{1,0:T(8,128)S(1)} %bitcast.14, f32[1,1024]{1,0:T(1,128)S(1)} %bitcast.16), custom_call_target="tpu_custom_call" | custom-call | flops 25165824 | bytes 786432 | tf_op jit(solution)/shard_map/window_conv/pallas_call | solution.py:210
  19.4 1.6 %collective-permute-start = (f32[16,128]{1,0:T(8,128)S(1)}, f32[16,128]{1,0:T(8,128)S(1)}, u32[]{:S(2)}, u32[]{:S(2)}) collective-permute-start(f32[16,128]{1,0:T(8,128)S(1)} %get-tuple-element.19), channel_id=1, source_target_pairs={{0,32},{32,64},{64,96},{96,128},{128,160},{160,192},{192,224},{224... | collective-permute-start | bytes 24584 | tf_op jit(solution)/shard_map/ppermute | solution.py:294
  21.1 2.4 %collective-permute-start.1 = (f32[16,128]{1,0:T(8,128)S(1)}, f32[16,128]{1,0:T(8,128)S(1)}, u32[]{:S(2)}, u32[]{:S(2)}) collective-permute-start(f32[16,128]{1,0:T(8,128)S(1)} %get-tuple-element.18), channel_id=1, source_target_pairs={{0,64},{32,96},{64,128},{96,160},{128,192},{160,224},{192,0},{224,... | collective-permute-start | bytes 24584 | tf_op jit(solution)/shard_map/ppermute | solution.py:294
  23.5 2.7 %collective-permute-start.2 = (f32[16,128]{1,0:T(8,128)S(1)}, f32[16,128]{1,0:T(8,128)S(1)}, u32[]{:S(2)}, u32[]{:S(2)}) collective-permute-start(f32[16,128]{1,0:T(8,128)S(1)} %get-tuple-element.17), channel_id=1, source_target_pairs={{0,96},{32,128},{64,160},{96,192},{128,224},{160,0},{192,32},{224,... | collective-permute-start | bytes 24584 | tf_op jit(solution)/shard_map/ppermute | solution.py:294
  26.1 2.4 %collective-permute-start.3 = (f32[16,128]{1,0:T(8,128)S(1)}, f32[16,128]{1,0:T(8,128)S(1)}, u32[]{:S(2)}, u32[]{:S(2)}) collective-permute-start(f32[16,128]{1,0:T(8,128)S(1)} %get-tuple-element.16), channel_id=1, source_target_pairs={{0,128},{32,160},{64,192},{96,224},{128,0},{160,32},{192,64},{224,... | collective-permute-start | bytes 24584 | tf_op jit(solution)/shard_map/ppermute | solution.py:294
  28.5 2.7 %collective-permute-start.4 = (f32[16,128]{1,0:T(8,128)S(1)}, f32[16,128]{1,0:T(8,128)S(1)}, u32[]{:S(2)}, u32[]{:S(2)}) collective-permute-start(f32[16,128]{1,0:T(8,128)S(1)} %get-tuple-element.15), channel_id=1, source_target_pairs={{0,160},{32,192},{64,224},{96,0},{128,32},{160,64},{192,96},{224,1... | collective-permute-start | bytes 24584 | tf_op jit(solution)/shard_map/ppermute | solution.py:294
  31.2 0.0 copy-done.6
  31.2 0.0 copy-done
  31.2 0.1 dynamic-slice_bitcast_fusion.2.length_ref
  31.3 33.8 %collective-permute-done.rest_1_ = f32[16,128]{1,0:T(8,128)S(1)} collective-permute-done((f32[16,128]{1,0:T(8,128)S(1)}, f32[16,128]{1,0:T(8,128)S(1)}, u32[]{:S(2)}, u32[]{:S(2)}) %collective-permute-start) | collective-permute-done | bytes 8224 | tf_op jit(solution)/shard_map/ppermute | solution.py:294
  65.1 2.4 %collective-permute-start.5 = (f32[16,128]{1,0:T(8,128)S(1)}, f32[16,128]{1,0:T(8,128)S(1)}, u32[]{:S(2)}, u32[]{:S(2)}) collective-permute-start(f32[16,128]{1,0:T(8,128)S(1)} %get-tuple-element.14), channel_id=1, source_target_pairs={{0,192},{32,224},{64,0},{96,32},{128,64},{160,96},{192,128},{224,1... | collective-permute-start | bytes 24584 | tf_op jit(solution)/shard_map/ppermute | solution.py:294
  67.5 0.0 collective-permute-done.1.rest_2_
  67.5 2.1 %collective-permute-start.6 = (f32[16,128]{1,0:T(8,128)S(1)}, f32[16,128]{1,0:T(8,128)S(1)}, u32[]{:S(2)}, u32[]{:S(2)}) collective-permute-start(f32[16,128]{1,0:T(8,128)S(1)} %get-tuple-element.13), channel_id=1, source_target_pairs={{0,224},{32,0},{64,32},{96,64},{128,96},{160,128},{192,160},{224,1... | collective-permute-start | bytes 24584 | tf_op jit(solution)/shard_map/ppermute | solution.py:294
  69.5 0.0 all-to-all-done
  69.6 5.6 %cache_conv.1 = (f32[1024,128]{1,0:T(8,128)S(1)}, f32[128,128]{1,0:T(8,128)S(1)}) custom-call(s32[512]{0:T(512)S(1)} %fusion.3.slots_ref, bf16[1024,8,128]{2,1,0:T(8,128)(2,1)S(1)} %bitcast.12, s32[1,128]{1,0:T(1,128)S(1)} %dynamic-slice_bitcast_fusion.2.length_ref, f32[16,128]{1,0:T(8,128)S(1)} %get-tuple-element.22.decay_ref, ...), custom_call_target="tpu_custom_call" | custom-call | flops 335544320 | bytes 2097152 | tf_op jit(solution)/shard_map/cache_conv/pallas_call | solution.py:230
  75.2 0.0 collective-permute-done.2.rest_3_
  75.2 0.0 collective-permute-done.3.rest_4_
  75.2 0.0 collective-permute-done.4.rest_5_
  75.2 0.0 collective-permute-done.5.rest_6_
  75.2 0.0 collective-permute-done.6.rest_7_
  75.2 1.8 %output_conv.1 = bf16[1024,128]{1,0:T(8,128)(2,1)S(1)} custom-call(s32[1]{0:T(128)} %bitcast.place_ref, s32[1,128]{1,0:T(1,128)S(1)} %dynamic-slice_bitcast_fusion.2.length_ref, f32[16,128]{1,0:T(8,128)S(1)} %get-tuple-element.22.decay_ref, f32[16,128]{1,0:T(8,128)S(1)} %get-tuple-element.21.weight_ref, f32[1024,128]{1,0:T(8,128)S(1)} %get-tuple-element.9.tail_ref, ...), custom_call_target="tpu_custom_call" | custom-call | tf_op jit(solution)/shard_map/output_conv/pallas_call | solution.py:250
  77.0 14.7 %all_to_all.10.conv_ref = bf16[8,128,128]{2,1,0:T(8,128)(2,1)S(1)} all-to-all(bf16[8,128,128]{2,1,0:T(8,128)(2,1)S(1)} %bitcast.13), channel_id=1, replica_groups=mesh['ctx'=8,'chan'=8,'req'=4] {'ctx'}, dimensions={0} | all-to-all | bytes 524288 | tf_op jit(solution)/shard_map/all_to_all | solution.py:323
  91.7 0.0 copy-done.1
  91.7 0.8 gate_out.1
  (8 shorter events, 0.1 us)
Async XLA Ops:
  0.0 31.2 %copy-start = (s32[1024]{0:T(1024)S(1)}, s32[1024]{0:T(1024)}, u32[]{:S(2)}) copy-start(s32[1024]{0:T(1024)} %param.12) | copy-start | bytes 12292
  3.9 12.4 %copy-start.2 = (bf16[128,1024]{1,0:T(8,128)(2,1)S(1)}, bf16[128,1024]{1,0:T(8,128)(2,1)}, u32[]{:S(2)}) copy-start(bf16[128,1024]{1,0:T(8,128)(2,1)} %window_ref.1) | copy-start | bytes 786436
  3.9 12.4 %copy-start.3 = (f32[1024,16]{0,1:T(8,128)S(1)}, f32[1024,16]{0,1:T(8,128)}, u32[]{:S(2)}) copy-start(f32[1024,16]{0,1:T(8,128)} %param.13) | copy-start | bytes 196612
  3.9 12.4 %copy-start.4 = (f32[1024,16]{0,1:T(8,128)S(1)}, f32[1024,16]{0,1:T(8,128)}, u32[]{:S(2)}) copy-start(f32[1024,16]{0,1:T(8,128)} %param.14) | copy-start | bytes 196612
  4.0 12.4 %copy-start.5 = (f32[1024]{0:T(1024)S(1)}, f32[1024]{0:T(1024)}, u32[]{:S(2)}) copy-start(f32[1024]{0:T(1024)} %param.15) | copy-start | bytes 12292
  4.0 27.2 %copy-start.6 = (s32[512]{0:T(512)S(1)}, s32[512]{0:T(512)}, u32[]{:S(2)}) copy-start(s32[512]{0:T(512)} %param.11) | copy-start | bytes 6148
  4.0 65.6 %all-to-all-start = ((bf16[64,16,8,128]{3,2,1,0:T(8,128)(2,1)}), bf16[64,16,8,128]{3,2,1,0:T(8,128)(2,1)S(1)}, u32[]{:S(2)}, u32[]{:S(2)}) async-start(bf16[64,16,8,128]{3,2,1,0:T(8,128)(2,1)} %parcel_of.1), calls=%async_computation | async-start | bytes 4194304 | tf_op jit(solution)/shard_map/all_to_all | solution.py:308
  16.3 75.4 %copy-start.1 = (bf16[128,1024]{1,0:T(8,128)(2,1)S(1)}, bf16[128,1024]{1,0:T(8,128)(2,1)}, u32[]{:S(2)}) copy-start(bf16[128,1024]{1,0:T(8,128)(2,1)} %gate_ref.1) | copy-start | bytes 786436
  19.4 45.7 %collective-permute-start = (f32[16,128]{1,0:T(8,128)S(1)}, f32[16,128]{1,0:T(8,128)S(1)}, u32[]{:S(2)}, u32[]{:S(2)}) collective-permute-start(f32[16,128]{1,0:T(8,128)S(1)} %get-tuple-element.19), channel_id=1, source_target_pairs={{0,32},{32,64},{64,96},{96,128},{128,160},{160,192},{192,224},{224... | collective-permute-start | bytes 24584 | tf_op jit(solution)/shard_map/ppermute | solution.py:294
  21.1 46.4 %collective-permute-start.1 = (f32[16,128]{1,0:T(8,128)S(1)}, f32[16,128]{1,0:T(8,128)S(1)}, u32[]{:S(2)}, u32[]{:S(2)}) collective-permute-start(f32[16,128]{1,0:T(8,128)S(1)} %get-tuple-element.18), channel_id=1, source_target_pairs={{0,64},{32,96},{64,128},{96,160},{128,192},{160,224},{192,0},{224,... | collective-permute-start | bytes 24584 | tf_op jit(solution)/shard_map/ppermute | solution.py:294
  23.5 51.7 %collective-permute-start.2 = (f32[16,128]{1,0:T(8,128)S(1)}, f32[16,128]{1,0:T(8,128)S(1)}, u32[]{:S(2)}, u32[]{:S(2)}) collective-permute-start(f32[16,128]{1,0:T(8,128)S(1)} %get-tuple-element.17), channel_id=1, source_target_pairs={{0,96},{32,128},{64,160},{96,192},{128,224},{160,0},{192,32},{224,... | collective-permute-start | bytes 24584 | tf_op jit(solution)/shard_map/ppermute | solution.py:294
  26.1 49.0 %collective-permute-start.3 = (f32[16,128]{1,0:T(8,128)S(1)}, f32[16,128]{1,0:T(8,128)S(1)}, u32[]{:S(2)}, u32[]{:S(2)}) collective-permute-start(f32[16,128]{1,0:T(8,128)S(1)} %get-tuple-element.16), channel_id=1, source_target_pairs={{0,128},{32,160},{64,192},{96,224},{128,0},{160,32},{192,64},{224,... | collective-permute-start | bytes 24584 | tf_op jit(solution)/shard_map/ppermute | solution.py:294
  28.5 46.7 %collective-permute-start.4 = (f32[16,128]{1,0:T(8,128)S(1)}, f32[16,128]{1,0:T(8,128)S(1)}, u32[]{:S(2)}, u32[]{:S(2)}) collective-permute-start(f32[16,128]{1,0:T(8,128)S(1)} %get-tuple-element.15), channel_id=1, source_target_pairs={{0,160},{32,192},{64,224},{96,0},{128,32},{160,64},{192,96},{224,1... | collective-permute-start | bytes 24584 | tf_op jit(solution)/shard_map/ppermute | solution.py:294
  65.1 10.0 %collective-permute-start.5 = (f32[16,128]{1,0:T(8,128)S(1)}, f32[16,128]{1,0:T(8,128)S(1)}, u32[]{:S(2)}, u32[]{:S(2)}) collective-permute-start(f32[16,128]{1,0:T(8,128)S(1)} %get-tuple-element.14), channel_id=1, source_target_pairs={{0,192},{32,224},{64,0},{96,32},{128,64},{160,96},{192,128},{224,1... | collective-permute-start | bytes 24584 | tf_op jit(solution)/shard_map/ppermute | solution.py:294
  67.5 7.7 %collective-permute-start.6 = (f32[16,128]{1,0:T(8,128)S(1)}, f32[16,128]{1,0:T(8,128)S(1)}, u32[]{:S(2)}, u32[]{:S(2)}) collective-permute-start(f32[16,128]{1,0:T(8,128)S(1)} %get-tuple-element.13), channel_id=1, source_target_pairs={{0,224},{32,0},{64,32},{96,64},{128,96},{160,128},{192,160},{224,1... | collective-permute-start | bytes 24584 | tf_op jit(solution)/shard_map/ppermute | solution.py:294

commit v6 on v5

--- a/solution.py
+++ b/solution.py
@@ -10,7 +10,7 @@
 LANES = 128
 SUBS = 8
 CHUNK = 128
-PIECES = 4
+PIECES = 8
 VMEM_LIMIT = 12 * 1024 * 1024
 WHOLE_VMEM = 60 * 1024 * 1024
 
@@ -96,26 +96,32 @@
     length = jnp.broadcast_to(length_ref[...], (SUBS, LANES))
     first = cached - length
 
+    window = steps * SUBS
     lam_page = [jnp.exp(-float(SUBS) * row(decay_ref, r)) for r in range(modes)]
 
+    def take_page(page):
+        value = pages_ref[slots_ref[page]].astype(jnp.float32)
+        signal[pl.ds(pl.multiple_of(page * SUBS, SUBS), SUBS), :] = value
+        return value
+
+    def copy_page(page, carry):
+        take_page(page)
+        return carry
+
     def scan_page(page, states):
-        value = pages_ref[slots_ref[page]].astype(jnp.float32)
-        start = pl.multiple_of(page * SUBS, SUBS)
-        signal[pl.ds(start, SUBS), :] = value
-        value = jnp.where(rows + page * SUBS > first, value, 0.0)
+        value = jnp.where(rows + page * SUBS >= first + window, take_page(page), 0.0)
         return tuple(s * l + value for s, l in zip(states, lam_page))
 
-    zero = jnp.zeros((SUBS, LANES), jnp.float32)
-    states = lax.fori_loop(0, page_count, scan_page, tuple(zero for _ in range(modes)), unroll=16)
+    lax.fori_loop(0, window // SUBS, copy_page, 0, unroll=16)
+    zero = tuple(jnp.zeros((SUBS, LANES), jnp.float32) for _ in range(modes))
+    states = lax.fori_loop(window // SUBS, page_count, scan_page, zero, unroll=16)
     rows_float = rows.astype(jnp.float32)
     for r in range(modes):
         decay = row(decay_ref, r)
         weighted = states[r] * jnp.exp(-decay * (float(SUBS - 1) - rows_float))
         total = jnp.broadcast_to(jnp.sum(weighted, axis=0, keepdims=True), (SUBS, LANES))
-        ahead = jnp.exp(-decay * (float(steps) * rows_float))
-        begin_ref[r * SUBS : (r + 1) * SUBS, :] = row(weight_ref, r) * total * ahead
-
-    window = steps * SUBS
+        begin_ref[r * SUBS : (r + 1) * SUBS, :] = total
+
     shift = cached // 2
     while shift >= 1:
         keep = min(window + shift - 1, cached - shift)
@@ -140,10 +146,14 @@
     length_float = length.astype(jnp.float32)
     for r in range(modes):
         decay = row(decay_ref, r)
-        prior = shift_down(inclusive_scan(ends[r], decay, steps), 1)
-        gone = row(weight_ref, r) * jnp.exp(-decay * length_float) * prior
+        weight = row(weight_ref, r)
         here = slice(r * SUBS, (r + 1) * SUBS)
-        begin_ref[here, :] = begin_ref[here, :] - gone
+        total = inclusive_scan(ends[r], decay, steps)
+        near = jnp.broadcast_to(total[SUBS - 1 : SUBS, :], (SUBS, LANES))
+        cache = begin_ref[here, :] + jnp.exp(-decay * (length_float - float(window))) * near
+        ahead = jnp.exp(-decay * (float(steps) * rows_float))
+        gone = jnp.exp(-decay * length_float) * shift_down(total, 1)
+        begin_ref[here, :] = weight * (cache * ahead - gone)
 
 
 def output_kernel(
@@ -173,20 +183,30 @@
     out_ref[...] = result[...].astype(jnp.bfloat16)
 
 
-def parcel_kernel(pool_ref, parcel_ref):
-    pages, page_len, _ = pool_ref.shape
-    each = parcel_ref.shape[0] // PIECES
-
-    def piece(from_ref, to_ref):
-        for block in range(each):
-            to_ref[block] = from_ref[:, :, block * LANES : (block + 1) * LANES]
-
-    pltpu.emit_pipeline(
-        piece,
-        grid=(PIECES,),
-        in_specs=[pl.BlockSpec((pages, page_len, each * LANES), lambda i: (0, 0, i))],
-        out_specs=[pl.BlockSpec((each, pages, page_len, LANES), lambda i: (i, 0, 0, 0))],
-    )(pool_ref, parcel_ref)
+def parcel_kernel(inner, pool_ref, parcel_ref, held, in_sems, out_sems):
+    tiles = parcel_ref.shape[0]
+    each = tiles // PIECES
+    fetches = [
+        pltpu.make_async_copy(
+            pool_ref.at[:, :, pl.ds(piece * each * LANES, each * LANES)],
+            held.at[:, :, pl.ds(piece * each * LANES, each * LANES)],
+            in_sems.at[piece],
+        )
+        for piece in range(PIECES)
+    ]
+    for fetch in fetches:
+        fetch.start()
+    sends = []
+    for piece, fetch in enumerate(fetches):
+        fetch.wait()
+        for block in range(piece * each, (piece + 1) * each):
+            send = pltpu.make_async_copy(
+                held.at[:, :, pl.ds(block * LANES, LANES)], parcel_ref.at[block % inner * (tiles // inner) + block // inner], out_sems.at[block]
+            )
+            send.start()
+            sends.append(send)
+    for send in sends:
+        send.wait()
 
 
 def gate_kernel(conv_ref, base_ref, gate_ref, out_ref):
@@ -261,13 +281,18 @@
     )(place, length, decay, weight, tail, begin, *ends)
 
 
-def parcel_of(pool):
+def parcel_of(pool, inner):
     pages, page_len, width = pool.shape
     return pl.pallas_call(
-        parcel_kernel,
+        functools.partial(parcel_kernel, inner),
         out_shape=jax.ShapeDtypeStruct((width // LANES, pages, page_len, LANES), pool.dtype),
         in_specs=[pl.BlockSpec(memory_space=pl.ANY)],
         out_specs=pl.BlockSpec(memory_space=pl.ANY),
+        scratch_shapes=[
+            pltpu.VMEM(pool.shape, pool.dtype),
+            pltpu.SemaphoreType.DMA((PIECES,)),
+            pltpu.SemaphoreType.DMA((width // LANES,)),
+        ],
         compiler_params=params(WHOLE_VMEM),
         name="parcel_of",
     )(pool)
@@ -300,25 +325,21 @@
     window_input, gate_values, page_pool, page_table, filter_len, residues, decays, skip_gain
 ):
     ctx_count = lax.axis_size("ctx")
-    chan_count = lax.axis_size("chan")
     ctx_pos = lax.axis_index("ctx")
     pool_pages, page_len, width = page_pool.shape
     rows = window_input.shape[0]
     pencil = window_input.shape[1] // ctx_count
     arrived = lax.all_to_all(
-        parcel_of(page_pool), ("chan", "ctx"), split_axis=0, concat_axis=0, tiled=True
+        parcel_of(page_pool, ctx_count), ("ctx", "chan"), split_axis=0, concat_axis=0, tiled=True
     )
     arrived = arrived.reshape(-1, page_len, pencil)
-    owners = page_table // pool_pages
-    source = (owners % chan_count) * ctx_count + owners // chan_count
-    slots = source * pool_pages + page_table % pool_pages
     start = ctx_pos * pencil
     decay = lax.dynamic_slice_in_dim(decays, start, pencil, 0).T
     weight = lax.dynamic_slice_in_dim(residues, start, pencil, 0).T
     length = lax.dynamic_slice_in_dim(filter_len, start, pencil, 0)[None, :]
     base, ends = window_conv(window_input, decays.T, residues.T, skip_gain[None, :])
     ends = end_states(ends, ctx_pos, ctx_count)
-    tail, begin = cache_conv(slots, arrived, length, decay, weight, rows * ctx_count)
+    tail, begin = cache_conv(page_table, arrived, length, decay, weight, rows * ctx_count)
     convolved = output_conv(ctx_pos[None], length, decay, weight, tail, begin, ends)
     conv_home = lax.all_to_all(
         convolved.reshape(ctx_count, -1, pencil), "ctx", split_axis=0, concat_axis=0, tiled=True

time: 93.1 us -> 90.6 us (0.973)
  Pallas kernels: 15.2 us -> 13.7 us
  waiting for transfers between devices: 33.9 us -> 32.7 us
    ppermute x7, waiting for transfers between devices: 33.9 us -> 32.7 us  [end_states(): lax.ppermute(block(hop), 'ctx', [(i, (i + hop) % count) for i in range(co...]
    pallas_call x1, Pallas kernels: 3.94 us -> 2.95 us  [parcel_of(): pl.pallas_call(functools.partial(parcel_kernel, inner), out_shape=jax.Sha...]
  transfers between devices with their start and end apart: 8 -> 8, of which waited for: 1 -> 2; matrix products, arithmetic and copies ran while one was open for 0% -> 0% of each run, Pallas kernels for 9% -> 9%
where the time goes in v6:
time: 90.6 us; the launch traced here: 90.4 us
  waiting for transfers between devices  32.7 us (36%)
  starting transfers between devices  29.1 us (32%)
  blocking collectives  14.4 us (16%)
  Pallas kernels  13.7 us (15%)
    ppermute x7, waiting for transfers between devices, end_states(): lax.ppermute(block(hop), 'ctx', [(i, (i + hop) % count) for i in range(co...  32.7 us
    ppermute x7, starting transfers between devices, end_states(): lax.ppermute(block(hop), 'ctx', [(i, (i + hop) % count) for i in range(co...  16.9 us
    all_to_all x1, blocking collectives, local(): lax.all_to_all(convolved.reshape(ctx_count, -1, pencil), 'ctx', split_axi...  14.4 us
    all_to_all x1, starting transfers between devices, local(): lax.all_to_all(parcel_of(page_pool, ctx_count), ('ctx', 'chan'), split_ax...  12.2 us
    pallas_call x1, Pallas kernels, cache_conv(): pl.pallas_call(functools.partial(cache_kernel, modes, window // SUBS), ou...  5.1 us
    pallas_call x1, Pallas kernels, window_conv(): pl.pallas_call(functools.partial(window_kernel, modes, rows // SUBS), out...  3.02 us
    pallas_call x1, Pallas kernels, parcel_of(): pl.pallas_call(functools.partial(parcel_kernel, inner), out_shape=jax.Sha...  2.95 us
  transfers between devices with their start and end apart: 8, of which 2 were waited for; matrix products, arithmetic and copies ran while one was open for 0% of the time, Pallas kernels for 9%

profile of v6, /device:TPU:4, one launch (start us, length us, event | category | flops | bytes accessed | tf_op | source)
XLA Modules:
  0.0 90.4 jit_solution(978472043139535539)
XLA Ops:
  0.0 2.9 %parcel_of.1 = bf16[64,16,8,128]{3,2,1,0:T(8,128)(2,1)} custom-call(bf16[16,8,8192]{2,1,0:T(8,128)(2,1)} %pool_ref.1), custom_call_target="tpu_custom_call" | custom-call | tf_op jit(solution)/shard_map/parcel_of/pallas_call | solution.py:286
  3.0 0.0 copy-start.2
  3.0 0.0 copy-start.3
  3.0 0.0 copy-start.4
  3.0 0.0 copy-start.5
  3.0 0.0 copy-start.6
  3.0 12.2 %all-to-all-start = ((bf16[64,16,8,128]{3,2,1,0:T(8,128)(2,1)}), bf16[64,16,8,128]{3,2,1,0:T(8,128)(2,1)S(1)}, u32[]{:S(2)}, u32[]{:S(2)}) async-start(bf16[64,16,8,128]{3,2,1,0:T(8,128)(2,1)} %parcel_of.1), calls=%async_computation | async-start | bytes 4194304 | tf_op jit(solution)/shard_map/all_to_all | solution.py:332
  15.4 0.0 copy-start.1
  15.4 0.0 copy-done.2
  15.4 0.0 copy-done.3
  15.4 0.0 copy-done.4
  15.4 3.0 %window_conv.1 = (f32[128,1024]{1,0:T(8,128)S(1)}, f32[16,1024]{1,0:T(8,128)S(1)}) custom-call(bf16[128,1024]{1,0:T(8,128)(2,1)S(1)} %copy-done.2, f32[16,1024]{1,0:T(8,128)S(1)} %bitcast.15, f32[16,1024]{1,0:T(8,128)S(1)} %bitcast.14, f32[1,1024]{1,0:T(1,128)S(1)} %bitcast.16), custom_call_target="tpu_custom_call" | custom-call | flops 25165824 | bytes 786432 | tf_op jit(solution)/shard_map/window_conv/pallas_call | solution.py:230
  18.5 1.7 %collective-permute-start = (f32[16,128]{1,0:T(8,128)S(1)}, f32[16,128]{1,0:T(8,128)S(1)}, u32[]{:S(2)}, u32[]{:S(2)}) collective-permute-start(f32[16,128]{1,0:T(8,128)S(1)} %get-tuple-element.19), channel_id=1, source_target_pairs={{0,32},{32,64},{64,96},{96,128},{128,160},{160,192},{192,224},{224... | collective-permute-start | bytes 24584 | tf_op jit(solution)/shard_map/ppermute | solution.py:319
  20.2 2.4 %collective-permute-start.1 = (f32[16,128]{1,0:T(8,128)S(1)}, f32[16,128]{1,0:T(8,128)S(1)}, u32[]{:S(2)}, u32[]{:S(2)}) collective-permute-start(f32[16,128]{1,0:T(8,128)S(1)} %get-tuple-element.18), channel_id=1, source_target_pairs={{0,64},{32,96},{64,128},{96,160},{128,192},{160,224},{192,0},{224,... | collective-permute-start | bytes 24584 | tf_op jit(solution)/shard_map/ppermute | solution.py:319
  22.6 2.8 %collective-permute-start.2 = (f32[16,128]{1,0:T(8,128)S(1)}, f32[16,128]{1,0:T(8,128)S(1)}, u32[]{:S(2)}, u32[]{:S(2)}) collective-permute-start(f32[16,128]{1,0:T(8,128)S(1)} %get-tuple-element.17), channel_id=1, source_target_pairs={{0,96},{32,128},{64,160},{96,192},{128,224},{160,0},{192,32},{224,... | collective-permute-start | bytes 24584 | tf_op jit(solution)/shard_map/ppermute | solution.py:319
  25.4 2.2 %collective-permute-start.3 = (f32[16,128]{1,0:T(8,128)S(1)}, f32[16,128]{1,0:T(8,128)S(1)}, u32[]{:S(2)}, u32[]{:S(2)}) collective-permute-start(f32[16,128]{1,0:T(8,128)S(1)} %get-tuple-element.16), channel_id=1, source_target_pairs={{0,128},{32,160},{64,192},{96,224},{128,0},{160,32},{192,64},{224,... | collective-permute-start | bytes 24584 | tf_op jit(solution)/shard_map/ppermute | solution.py:319
  27.6 2.9 %collective-permute-start.4 = (f32[16,128]{1,0:T(8,128)S(1)}, f32[16,128]{1,0:T(8,128)S(1)}, u32[]{:S(2)}, u32[]{:S(2)}) collective-permute-start(f32[16,128]{1,0:T(8,128)S(1)} %get-tuple-element.15), channel_id=1, source_target_pairs={{0,160},{32,192},{64,224},{96,0},{128,32},{160,64},{192,96},{224,1... | collective-permute-start | bytes 24584 | tf_op jit(solution)/shard_map/ppermute | solution.py:319
  30.5 0.1 dynamic-slice_bitcast_fusion.2.length_ref
  30.6 32.4 %collective-permute-done.rest_1_ = f32[16,128]{1,0:T(8,128)S(1)} collective-permute-done((f32[16,128]{1,0:T(8,128)S(1)}, f32[16,128]{1,0:T(8,128)S(1)}, u32[]{:S(2)}, u32[]{:S(2)}) %collective-permute-start) | collective-permute-done | bytes 8224 | tf_op jit(solution)/shard_map/ppermute | solution.py:319
  63.0 2.2 %collective-permute-start.5 = (f32[16,128]{1,0:T(8,128)S(1)}, f32[16,128]{1,0:T(8,128)S(1)}, u32[]{:S(2)}, u32[]{:S(2)}) collective-permute-start(f32[16,128]{1,0:T(8,128)S(1)} %get-tuple-element.14), channel_id=1, source_target_pairs={{0,192},{32,224},{64,0},{96,32},{128,64},{160,96},{192,128},{224,1... | collective-permute-start | bytes 24584 | tf_op jit(solution)/shard_map/ppermute | solution.py:319
  65.2 0.2 collective-permute-done.1.rest_2_
  65.5 2.7 %collective-permute-start.6 = (f32[16,128]{1,0:T(8,128)S(1)}, f32[16,128]{1,0:T(8,128)S(1)}, u32[]{:S(2)}, u32[]{:S(2)}) collective-permute-start(f32[16,128]{1,0:T(8,128)S(1)} %get-tuple-element.13), channel_id=1, source_target_pairs={{0,224},{32,0},{64,32},{96,64},{128,96},{160,128},{192,160},{224,1... | collective-permute-start | bytes 24584 | tf_op jit(solution)/shard_map/ppermute | solution.py:319
  68.1 0.0 all-to-all-done
  68.1 5.1 %cache_conv.1 = (f32[1024,128]{1,0:T(8,128)S(1)}, f32[128,128]{1,0:T(8,128)S(1)}) custom-call(s32[512]{0:T(512)S(1)} %copy-done.6, bf16[1024,8,128]{2,1,0:T(8,128)(2,1)S(1)} %bitcast.12, s32[1,128]{1,0:T(1,128)S(1)} %dynamic-slice_bitcast_fusion.2.length_ref, f32[16,128]{1,0:T(8,128)S(1)} %get-tuple-element.22.decay_ref, ...), custom_call_target="tpu_custom_call" | custom-call | flops 335544320 | bytes 2097152 | tf_op jit(solution)/shard_map/cache_conv/pallas_call | solution.py:250
  73.2 0.0 collective-permute-done.2.rest_3_
  73.2 0.0 collective-permute-done.3.rest_4_
  73.3 0.0 collective-permute-done.4.rest_5_
  73.3 0.0 collective-permute-done.5.rest_6_
  73.3 0.0 collective-permute-done.6.rest_7_
  73.3 1.8 %output_conv.1 = bf16[1024,128]{1,0:T(8,128)(2,1)S(1)} custom-call(s32[1]{0:T(128)} %bitcast.place_ref, s32[1,128]{1,0:T(1,128)S(1)} %dynamic-slice_bitcast_fusion.2.length_ref, f32[16,128]{1,0:T(8,128)S(1)} %get-tuple-element.22.decay_ref, f32[16,128]{1,0:T(8,128)S(1)} %get-tuple-element.21.weight_ref, f32[1024,128]{1,0:T(8,128)S(1)} %get-tuple-element.9.tail_ref, ...), custom_call_target="tpu_custom_call" | custom-call | tf_op jit(solution)/shard_map/output_conv/pallas_call | solution.py:270
  75.1 14.4 %all_to_all.10.conv_ref = bf16[8,128,128]{2,1,0:T(8,128)(2,1)S(1)} all-to-all(bf16[8,128,128]{2,1,0:T(8,128)(2,1)S(1)} %bitcast.13), channel_id=1, replica_groups=mesh['ctx'=8,'chan'=8,'req'=4] {'ctx'}, dimensions={0} | all-to-all | bytes 524288 | tf_op jit(solution)/shard_map/all_to_all | solution.py:344
  89.5 0.8 gate_out.1
  (7 shorter events, 0.0 us)
Async XLA Ops:
  0.0 30.5 %copy-start = (s32[1024]{0:T(1024)S(1)}, s32[1024]{0:T(1024)}, u32[]{:S(2)}) copy-start(s32[1024]{0:T(1024)} %param.12) | copy-start | bytes 12292
  3.0 12.4 %copy-start.2 = (bf16[128,1024]{1,0:T(8,128)(2,1)S(1)}, bf16[128,1024]{1,0:T(8,128)(2,1)}, u32[]{:S(2)}) copy-start(bf16[128,1024]{1,0:T(8,128)(2,1)} %window_ref.1) | copy-start | bytes 786436
  3.0 12.4 %copy-start.3 = (f32[1024,16]{0,1:T(8,128)S(1)}, f32[1024,16]{0,1:T(8,128)}, u32[]{:S(2)}) copy-start(f32[1024,16]{0,1:T(8,128)} %param.13) | copy-start | bytes 196612
  3.0 12.4 %copy-start.4 = (f32[1024,16]{0,1:T(8,128)S(1)}, f32[1024,16]{0,1:T(8,128)}, u32[]{:S(2)}) copy-start(f32[1024,16]{0,1:T(8,128)} %param.14) | copy-start | bytes 196612
  3.0 12.4 %copy-start.5 = (f32[1024]{0:T(1024)S(1)}, f32[1024]{0:T(1024)}, u32[]{:S(2)}) copy-start(f32[1024]{0:T(1024)} %param.15) | copy-start | bytes 12292
  3.0 65.1 %copy-start.6 = (s32[512]{0:T(512)S(1)}, s32[512]{0:T(512)}, u32[]{:S(2)}) copy-start(s32[512]{0:T(512)} %slots_ref.1) | copy-start | bytes 6148
  3.0 65.1 %all-to-all-start = ((bf16[64,16,8,128]{3,2,1,0:T(8,128)(2,1)}), bf16[64,16,8,128]{3,2,1,0:T(8,128)(2,1)S(1)}, u32[]{:S(2)}, u32[]{:S(2)}) async-start(bf16[64,16,8,128]{3,2,1,0:T(8,128)(2,1)} %parcel_of.1), calls=%async_computation | async-start | bytes 4194304 | tf_op jit(solution)/shard_map/all_to_all | solution.py:332
  15.4 74.2 %copy-start.1 = (bf16[128,1024]{1,0:T(8,128)(2,1)S(1)}, bf16[128,1024]{1,0:T(8,128)(2,1)}, u32[]{:S(2)}) copy-start(bf16[128,1024]{1,0:T(8,128)(2,1)} %gate_ref.1) | copy-start | bytes 786436
  18.5 44.5 %collective-permute-start = (f32[16,128]{1,0:T(8,128)S(1)}, f32[16,128]{1,0:T(8,128)S(1)}, u32[]{:S(2)}, u32[]{:S(2)}) collective-permute-start(f32[16,128]{1,0:T(8,128)S(1)} %get-tuple-element.19), channel_id=1, source_target_pairs={{0,32},{32,64},{64,96},{96,128},{128,160},{160,192},{192,224},{224... | collective-permute-start | bytes 24584 | tf_op jit(solution)/shard_map/ppermute | solution.py:319
  20.2 45.3 %collective-permute-start.1 = (f32[16,128]{1,0:T(8,128)S(1)}, f32[16,128]{1,0:T(8,128)S(1)}, u32[]{:S(2)}, u32[]{:S(2)}) collective-permute-start(f32[16,128]{1,0:T(8,128)S(1)} %get-tuple-element.18), channel_id=1, source_target_pairs={{0,64},{32,96},{64,128},{96,160},{128,192},{160,224},{192,0},{224,... | collective-permute-start | bytes 24584 | tf_op jit(solution)/shard_map/ppermute | solution.py:319
  22.6 50.7 %collective-permute-start.2 = (f32[16,128]{1,0:T(8,128)S(1)}, f32[16,128]{1,0:T(8,128)S(1)}, u32[]{:S(2)}, u32[]{:S(2)}) collective-permute-start(f32[16,128]{1,0:T(8,128)S(1)} %get-tuple-element.17), channel_id=1, source_target_pairs={{0,96},{32,128},{64,160},{96,192},{128,224},{160,0},{192,32},{224,... | collective-permute-start | bytes 24584 | tf_op jit(solution)/shard_map/ppermute | solution.py:319
  25.4 47.9 %collective-permute-start.3 = (f32[16,128]{1,0:T(8,128)S(1)}, f32[16,128]{1,0:T(8,128)S(1)}, u32[]{:S(2)}, u32[]{:S(2)}) collective-permute-start(f32[16,128]{1,0:T(8,128)S(1)} %get-tuple-element.16), channel_id=1, source_target_pairs={{0,128},{32,160},{64,192},{96,224},{128,0},{160,32},{192,64},{224,... | collective-permute-start | bytes 24584 | tf_op jit(solution)/shard_map/ppermute | solution.py:319
  27.6 45.7 %collective-permute-start.4 = (f32[16,128]{1,0:T(8,128)S(1)}, f32[16,128]{1,0:T(8,128)S(1)}, u32[]{:S(2)}, u32[]{:S(2)}) collective-permute-start(f32[16,128]{1,0:T(8,128)S(1)} %get-tuple-element.15), channel_id=1, source_target_pairs={{0,160},{32,192},{64,224},{96,0},{128,32},{160,64},{192,96},{224,1... | collective-permute-start | bytes 24584 | tf_op jit(solution)/shard_map/ppermute | solution.py:319
  63.0 10.3 %collective-permute-start.5 = (f32[16,128]{1,0:T(8,128)S(1)}, f32[16,128]{1,0:T(8,128)S(1)}, u32[]{:S(2)}, u32[]{:S(2)}) collective-permute-start(f32[16,128]{1,0:T(8,128)S(1)} %get-tuple-element.14), channel_id=1, source_target_pairs={{0,192},{32,224},{64,0},{96,32},{128,64},{160,96},{192,128},{224,1... | collective-permute-start | bytes 24584 | tf_op jit(solution)/shard_map/ppermute | solution.py:319
  65.5 7.8 %collective-permute-start.6 = (f32[16,128]{1,0:T(8,128)S(1)}, f32[16,128]{1,0:T(8,128)S(1)}, u32[]{:S(2)}, u32[]{:S(2)}) collective-permute-start(f32[16,128]{1,0:T(8,128)S(1)} %get-tuple-element.13), channel_id=1, source_target_pairs={{0,224},{32,0},{64,32},{96,64},{128,96},{160,128},{192,160},{224,1... | collective-permute-start | bytes 24584 | tf_op jit(solution)/shard_map/ppermute | solution.py:319

commit v7 on v6

--- a/solution.py
+++ b/solution.py
@@ -10,7 +10,8 @@
 LANES = 128
 SUBS = 8
 CHUNK = 128
-PIECES = 8
+PIECES = 2
+COUNTS = (13, 14, 15)
 VMEM_LIMIT = 12 * 1024 * 1024
 WHOLE_VMEM = 60 * 1024 * 1024
 
@@ -183,25 +184,51 @@
     out_ref[...] = result[...].astype(jnp.bfloat16)
 
 
-def parcel_kernel(inner, pool_ref, parcel_ref, held, in_sems, out_sems):
-    tiles = parcel_ref.shape[0]
+def plan_kernel(pool_pages, owner_count, counts, self_ref, table_ref, which_ref, list_ref):
+    bits = pool_pages.bit_length() - 1
+    table = table_ref[...]
+    shape = (owner_count, table.shape[1])
+    same = lax.shift_right_logical(table, bits) == lax.broadcasted_iota(jnp.int32, shape, 0)
+    most = jnp.max(jnp.sum(jnp.where(same, 1.0, 0.0), axis=1, keepdims=True))
+    which = jnp.int32(0)
+    for count in counts:
+        which = which + jnp.where(most > float(count), 1, 0)
+    which_ref[0] = which
+    mine = lax.broadcasted_iota(jnp.int32, (pool_pages, table.shape[1]), 0) + self_ref[0] * pool_pages
+    used = jnp.sum(jnp.where(table == mine, 1.0, 0.0), axis=1, keepdims=True)
+    slot = lax.broadcasted_iota(jnp.int32, (pool_pages, LANES), 0)
+    lane = lax.broadcasted_iota(jnp.int32, (pool_pages, LANES), 1)
+    across = jnp.sum(jnp.where(slot == lane, used, 0.0), axis=0, keepdims=True)
+    rank = jnp.sum(jnp.where(lane < slot, across, 0.0), axis=1, keepdims=True)
+    here = (used > 0.5) & (rank == lane.astype(jnp.float32))
+    chosen = jnp.sum(jnp.where(here, slot.astype(jnp.float32), 0.0), axis=0, keepdims=True)
+    list_ref[...] = chosen.astype(jnp.int32)
+
+
+def parcel_kernel(inner, list_ref, pool_ref, parcel_ref, held, in_sems, out_sems):
+    tiles, count = parcel_ref.shape[:2]
     each = tiles // PIECES
-    fetches = [
-        pltpu.make_async_copy(
-            pool_ref.at[:, :, pl.ds(piece * each * LANES, each * LANES)],
-            held.at[:, :, pl.ds(piece * each * LANES, each * LANES)],
-            in_sems.at[piece],
-        )
-        for piece in range(PIECES)
-    ]
-    for fetch in fetches:
-        fetch.start()
+    fetches = []
+    for piece in range(PIECES):
+        lanes = pl.ds(piece * each * LANES, each * LANES)
+        for page in range(count):
+            fetches.append(
+                pltpu.make_async_copy(
+                    pool_ref.at[list_ref[0, page], :, lanes],
+                    held.at[page, :, lanes],
+                    in_sems.at[piece, page],
+                )
+            )
+            fetches[-1].start()
     sends = []
-    for piece, fetch in enumerate(fetches):
-        fetch.wait()
+    for piece in range(PIECES):
+        for fetch in fetches[piece * count : (piece + 1) * count]:
+            fetch.wait()
         for block in range(piece * each, (piece + 1) * each):
             send = pltpu.make_async_copy(
-                held.at[:, :, pl.ds(block * LANES, LANES)], parcel_ref.at[block % inner * (tiles // inner) + block // inner], out_sems.at[block]
+                held.at[:, :, pl.ds(block * LANES, LANES)],
+                parcel_ref.at[block % inner * (tiles // inner) + block // inner],
+                out_sems.at[block],
             )
             send.start()
             sends.append(send)
@@ -281,21 +308,35 @@
     )(place, length, decay, weight, tail, begin, *ends)
 
 
-def parcel_of(pool, inner):
-    pages, page_len, width = pool.shape
+def plan_of(self_owner, table, pool_pages, owner_count, counts):
+    return pl.pallas_call(
+        functools.partial(plan_kernel, pool_pages, owner_count, counts),
+        out_shape=(
+            jax.ShapeDtypeStruct((1,), jnp.int32),
+            jax.ShapeDtypeStruct((1, LANES), jnp.int32),
+        ),
+        in_specs=[pl.BlockSpec(memory_space=pltpu.SMEM)] + vmem(1),
+        out_specs=(pl.BlockSpec(memory_space=pltpu.SMEM), pl.BlockSpec(memory_space=pltpu.VMEM)),
+        compiler_params=params(),
+        name="plan_of",
+    )(self_owner, table)
+
+
+def parcel_of(chosen, pool, inner, count):
+    _, page_len, width = pool.shape
     return pl.pallas_call(
         functools.partial(parcel_kernel, inner),
-        out_shape=jax.ShapeDtypeStruct((width // LANES, pages, page_len, LANES), pool.dtype),
-        in_specs=[pl.BlockSpec(memory_space=pl.ANY)],
+        out_shape=jax.ShapeDtypeStruct((width // LANES, count, page_len, LANES), pool.dtype),
+        in_specs=[pl.BlockSpec(memory_space=pltpu.SMEM), pl.BlockSpec(memory_space=pl.ANY)],
         out_specs=pl.BlockSpec(memory_space=pl.ANY),
         scratch_shapes=[
-            pltpu.VMEM(pool.shape, pool.dtype),
-            pltpu.SemaphoreType.DMA((PIECES,)),
+            pltpu.VMEM((count, page_len, width), pool.dtype),
+            pltpu.SemaphoreType.DMA((PIECES, count)),
             pltpu.SemaphoreType.DMA((width // LANES,)),
         ],
         compiler_params=params(WHOLE_VMEM),
         name="parcel_of",
-    )(pool)
+    )(chosen, pool)
 
 
 def gate_out(conv_home, base, gate_values):
@@ -321,30 +362,59 @@
     ]
 
 
-def local(
-    window_input, gate_values, page_pool, page_table, filter_len, residues, decays, skip_gain
+def with_count(
+    count, window_input, gate_values, page_pool, page_table, chosen, filter_len, residues, decays, skip_gain
 ):
     ctx_count = lax.axis_size("ctx")
     ctx_pos = lax.axis_index("ctx")
-    pool_pages, page_len, width = page_pool.shape
+    page_len = page_pool.shape[1]
     rows = window_input.shape[0]
     pencil = window_input.shape[1] // ctx_count
-    arrived = lax.all_to_all(
-        parcel_of(page_pool, ctx_count), ("ctx", "chan"), split_axis=0, concat_axis=0, tiled=True
-    )
+    parcel = parcel_of(chosen, page_pool, ctx_count, count)
+    arrived = lax.all_to_all(parcel, ("ctx", "chan"), split_axis=0, concat_axis=0, tiled=True)
     arrived = arrived.reshape(-1, page_len, pencil)
+    owners = page_table // page_pool.shape[0]
+    lower = (owners[:, None] == owners[None, :]) & (page_table[None, :] < page_table[:, None])
+    slots = owners * count + jnp.sum(lower.astype(jnp.int32), axis=1)
     start = ctx_pos * pencil
     decay = lax.dynamic_slice_in_dim(decays, start, pencil, 0).T
     weight = lax.dynamic_slice_in_dim(residues, start, pencil, 0).T
     length = lax.dynamic_slice_in_dim(filter_len, start, pencil, 0)[None, :]
     base, ends = window_conv(window_input, decays.T, residues.T, skip_gain[None, :])
     ends = end_states(ends, ctx_pos, ctx_count)
-    tail, begin = cache_conv(page_table, arrived, length, decay, weight, rows * ctx_count)
+    tail, begin = cache_conv(slots, arrived, length, decay, weight, rows * ctx_count)
     convolved = output_conv(ctx_pos[None], length, decay, weight, tail, begin, ends)
     conv_home = lax.all_to_all(
         convolved.reshape(ctx_count, -1, pencil), "ctx", split_axis=0, concat_axis=0, tiled=True
     )
     return gate_out(conv_home, base, gate_values)
+
+
+def local(
+    window_input, gate_values, page_pool, page_table, filter_len, residues, decays, skip_gain
+):
+    chan_count = lax.axis_size("chan")
+    pool_pages = page_pool.shape[0]
+    self_owner = lax.axis_index("ctx") * chan_count + lax.axis_index("chan")
+    owner_count = lax.axis_size("ctx") * chan_count
+    counts = [c for c in COUNTS if c < pool_pages]
+    which, chosen = plan_of(
+        self_owner[None], page_table[None, :], pool_pages, owner_count, counts
+    )
+    counts.append(pool_pages)
+    return lax.switch(
+        which[0],
+        [functools.partial(with_count, c) for c in counts],
+        window_input,
+        gate_values,
+        page_pool,
+        page_table,
+        chosen,
+        filter_len,
+        residues,
+        decays,
+        skip_gain,
+    )
 
 
 def solution(mesh):

time: 90.6 us -> 87.2 us (0.962); the launches traced: 90.4 us -> 88.2 us
  waiting for transfers between devices: 32.7 us -> 26.1 us
  Pallas kernels: 13.7 us -> 16.3 us
    ppermute x7, waiting for transfers between devices: 32.7 us -> 26.1 us  [end_states(): lax.ppermute(block(hop), 'ctx', [(i, (i + hop) % count) for i in range(co...]
    pallas_call x0 -> x1, Pallas kernels: none -> 1.34 us  [plan_of(): pl.pallas_call(functools.partial(plan_kernel, pool_pages, owner_count, co...]
    pallas_call x1, Pallas kernels: 2.95 us -> 4.23 us  [parcel_of(): pl.pallas_call(functools.partial(parcel_kernel, inner), out_shape=jax.Sha...]
  transfers between devices with their start and end apart: 8 -> 8, of which waited for: 2 -> 1; matrix products, arithmetic and copies ran while one was open for 0% -> 1% of each run, Pallas kernels for 9% -> 9%
where the time goes in v7:
time: 87.2 us; the launch traced here: 88.2 us
  starting transfers between devices  29.3 us (34%)
  waiting for transfers between devices  26.1 us (30%)
  Pallas kernels  16.3 us (19%)
  blocking collectives  14.4 us (17%)
    ppermute x7, waiting for transfers between devices, end_states(): lax.ppermute(block(hop), 'ctx', [(i, (i + hop) % count) for i in range(co...  26.1 us
    ppermute x7, starting transfers between devices, end_states(): lax.ppermute(block(hop), 'ctx', [(i, (i + hop) % count) for i in range(co...  16.8 us
    all_to_all x1, blocking collectives, with_count(): lax.all_to_all(convolved.reshape(ctx_count, -1, pencil), 'ctx', split_axi...  14.4 us
    all_to_all x1, starting transfers between devices, with_count(): lax.all_to_all(parcel, ('ctx', 'chan'), split_axis=0, concat_axis=0, tile...  12.4 us
    pallas_call x1, Pallas kernels, cache_conv(): pl.pallas_call(functools.partial(cache_kernel, modes, window // SUBS), ou...  5.1 us
    pallas_call x1, Pallas kernels, parcel_of(): pl.pallas_call(functools.partial(parcel_kernel, inner), out_shape=jax.Sha...  4.23 us
    pallas_call x1, Pallas kernels, window_conv(): pl.pallas_call(functools.partial(window_kernel, modes, rows // SUBS), out...  3.02 us
    pallas_call x1, Pallas kernels, output_conv(): pl.pallas_call(functools.partial(output_kernel, modes, window // SUBS), o...  1.81 us
  transfers between devices with their start and end apart: 8, of which 1 were waited for; matrix products, arithmetic and copies ran while one was open for 1% of the time, Pallas kernels for 9%

profile of v7, /device:TPU:4, one launch (start us, length us, event | category | flops | bytes accessed | tf_op | source)
XLA Modules:
  0.0 88.2 jit_solution(6071360139184361661)
XLA Ops:
  0.0 1.3 %plan_of.1 = (s32[1]{0:T(128)}, s32[1,128]{1,0:T(1,128)S(1)}) custom-call(s32[1]{0:T(128)} %bitcast.36.self_ref, s32[1,512]{1,0:T(1,128)} %bitcast.67), custom_call_target="tpu_custom_call" | custom-call | tf_op jit(solution)/shard_map/plan_of/pallas_call | solution.py:312
  1.9 86.3 %conditional.1 = (bf16[128,1024]{1,0:T(8,128)(2,1)}) conditional(s32[]{:T(128)} %bitcast.38, (s32[1024]{0:T(1024)}, f32[1024,16]{0,1:T(8,128)}, f32[1024,16]{0,1:T(8,128)}, s32[512]{0:T(512)}, s32[1,128]{1,0:T(1,128)S(1)}, /*index=5*/bf16[16,8,8192]{2,1,0:T(8,128)(2,1)}, f32[1024]{0:T(1024)}, ...), branch_computations={%region_0.2_spmd, %region_2.4_spmd, %region_4.6_spmd, %region_6.8_... | conditional | flops 362036736 | bytes 12757898 | solution.py:405
  1.9 4.2 %parcel_of.5 = bf16[64,14,8,128]{3,2,1,0:T(8,128)(2,1)} custom-call(s32[1,128]{1,0:T(1,128)S(1)} %get-tuple-element.99.list_ref, bf16[16,8,8192]{2,1,0:T(8,128)(2,1)} %get-tuple-element.100.pool_ref), custom_call_target="tpu_custom_call" | custom-call | tf_op jit(solution)/shard_map/cond/branch_1_fun/parcel_of/pallas_call | solution.py:327
  6.2 0.0 copy-start.5
  6.2 0.0 copy-start.9
  6.2 0.0 copy-start.13
  6.2 0.0 copy-start.21
  6.2 0.0 copy-start.17
  6.2 12.4 %all-to-all-start.2 = ((bf16[64,14,8,128]{3,2,1,0:T(8,128)(2,1)}), bf16[64,14,8,128]{3,2,1,0:T(8,128)(2,1)S(1)}, u32[]{:S(2)}, u32[]{:S(2)}) async-start(bf16[64,14,8,128]{3,2,1,0:T(8,128)(2,1)} %parcel_of.5), calls=%async_computation.2 | async-start | bytes 3670016 | tf_op jit(solution)/shard_map/cond/branch_1_fun/all_to_all | solution.py:374
  18.8 0.0 copy-start.1
  18.9 3.0 %window_conv.5 = (f32[128,1024]{1,0:T(8,128)S(1)}, f32[16,1024]{1,0:T(8,128)S(1)}) custom-call(bf16[128,1024]{1,0:T(8,128)(2,1)S(1)} %copy-done.5, f32[16,1024]{1,0:T(8,128)S(1)} %bitcast.60, f32[16,1024]{1,0:T(8,128)S(1)} %bitcast.64, f32[1,1024]{1,0:T(1,128)S(1)} %bitcast.69), custom_call_target="tpu_custom_call" | custom-call | flops 25165824 | bytes 786432 | tf_op jit(solution)/shard_map/cond/branch_1_fun/window_conv/pallas_call | solution.py:257
  21.9 1.7 %collective-permute-start.7 = (f32[16,128]{1,0:T(8,128)S(1)}, f32[16,128]{1,0:T(8,128)S(1)}, u32[]{:S(2)}, u32[]{:S(2)}) collective-permute-start(f32[16,128]{1,0:T(8,128)S(1)} %get-tuple-element.155), channel_id=1, source_target_pairs={{0,32},{32,64},{64,96},{96,128},{128,160},{160,192},{192,224},{224... | collective-permute-start | bytes 24584 | tf_op jit(solution)/shard_map/cond/branch_1_fun/ppermute | solution.py:360
  23.6 2.4 %collective-permute-start.8 = (f32[16,128]{1,0:T(8,128)S(1)}, f32[16,128]{1,0:T(8,128)S(1)}, u32[]{:S(2)}, u32[]{:S(2)}) collective-permute-start(f32[16,128]{1,0:T(8,128)S(1)} %get-tuple-element.154), channel_id=1, source_target_pairs={{0,64},{32,96},{64,128},{96,160},{128,192},{160,224},{192,0},{224,... | collective-permute-start | bytes 24584 | tf_op jit(solution)/shard_map/cond/branch_1_fun/ppermute | solution.py:360
  26.0 2.8 %collective-permute-start.9 = (f32[16,128]{1,0:T(8,128)S(1)}, f32[16,128]{1,0:T(8,128)S(1)}, u32[]{:S(2)}, u32[]{:S(2)}) collective-permute-start(f32[16,128]{1,0:T(8,128)S(1)} %get-tuple-element.153), channel_id=1, source_target_pairs={{0,96},{32,128},{64,160},{96,192},{128,224},{160,0},{192,32},{224,... | collective-permute-start | bytes 24584 | tf_op jit(solution)/shard_map/cond/branch_1_fun/ppermute | solution.py:360
  28.8 2.2 %collective-permute-start.10 = (f32[16,128]{1,0:T(8,128)S(1)}, f32[16,128]{1,0:T(8,128)S(1)}, u32[]{:S(2)}, u32[]{:S(2)}) collective-permute-start(f32[16,128]{1,0:T(8,128)S(1)} %get-tuple-element.152), channel_id=1, source_target_pairs={{0,128},{32,160},{64,192},{96,224},{128,0},{160,32},{192,64},{224,... | collective-permute-start | bytes 24584 | tf_op jit(solution)/shard_map/cond/branch_1_fun/ppermute | solution.py:360
  31.0 2.9 %collective-permute-start.11 = (f32[16,128]{1,0:T(8,128)S(1)}, f32[16,128]{1,0:T(8,128)S(1)}, u32[]{:S(2)}, u32[]{:S(2)}) collective-permute-start(f32[16,128]{1,0:T(8,128)S(1)} %get-tuple-element.151), channel_id=1, source_target_pairs={{0,160},{32,192},{64,224},{96,0},{128,32},{160,64},{192,96},{224,1... | collective-permute-start | bytes 24584 | tf_op jit(solution)/shard_map/cond/branch_1_fun/ppermute | solution.py:360
  33.9 0.3 convert_reduce_fusion.1
  34.3 0.8 dynamic-slice_bitcast_fusion.5.length_ref
  35.0 26.1 %collective-permute-done.7.rest_1_ = f32[16,128]{1,0:T(8,128)S(1)} collective-permute-done((f32[16,128]{1,0:T(8,128)S(1)}, f32[16,128]{1,0:T(8,128)S(1)}, u32[]{:S(2)}, u32[]{:S(2)}) %collective-permute-start.7) | collective-permute-done | bytes 8224 | tf_op jit(solution)/shard_map/cond/branch_1_fun/ppermute | solution.py:360
  61.1 2.3 %collective-permute-start.12 = (f32[16,128]{1,0:T(8,128)S(1)}, f32[16,128]{1,0:T(8,128)S(1)}, u32[]{:S(2)}, u32[]{:S(2)}) collective-permute-start(f32[16,128]{1,0:T(8,128)S(1)} %get-tuple-element.150), channel_id=1, source_target_pairs={{0,192},{32,224},{64,0},{96,32},{128,64},{160,96},{192,128},{224,1... | collective-permute-start | bytes 24584 | tf_op jit(solution)/shard_map/cond/branch_1_fun/ppermute | solution.py:360
  63.4 0.0 collective-permute-done.8.rest_2_
  63.4 2.5 %collective-permute-start.13 = (f32[16,128]{1,0:T(8,128)S(1)}, f32[16,128]{1,0:T(8,128)S(1)}, u32[]{:S(2)}, u32[]{:S(2)}) collective-permute-start(f32[16,128]{1,0:T(8,128)S(1)} %get-tuple-element.149), channel_id=1, source_target_pairs={{0,224},{32,0},{64,32},{96,64},{128,96},{160,128},{192,160},{224,1... | collective-permute-start | bytes 24584 | tf_op jit(solution)/shard_map/cond/branch_1_fun/ppermute | solution.py:360
  66.0 0.0 all-to-all-done.2
  66.0 5.1 %cache_conv.5 = (f32[1024,128]{1,0:T(8,128)S(1)}, f32[128,128]{1,0:T(8,128)S(1)}) custom-call(s32[512]{0:T(512)S(1)} %multiply_add_fusion.1.slots_ref, bf16[896,8,128]{2,1,0:T(8,128)(2,1)S(1)} %bitcast.53, s32[1,128]{1,0:T(1,128)S(1)} %dynamic-slice_bitcast_fusion.5.length_ref, f32[16,128]{1,0:T(8,128)S(1)} %get-tuple-element.158.decay_ref, ...), custom_call_target="tpu_custom_call" | custom-call | flops 335544320 | bytes 2097152 | tf_op jit(solution)/shard_map/cond/branch_1_fun/cache_conv/pallas_call | solution.py:277
  71.1 0.0 collective-permute-done.9.rest_3_
  71.1 0.0 collective-permute-done.10.rest_4_
  71.1 0.0 collective-permute-done.11.rest_5_
  71.1 0.0 collective-permute-done.12.rest_6_
  71.1 0.0 collective-permute-done.13.rest_7_
  71.1 1.8 %output_conv.5 = bf16[1024,128]{1,0:T(8,128)(2,1)S(1)} custom-call(s32[1]{0:T(128)} %bitcast.9.place_ref, s32[1,128]{1,0:T(1,128)S(1)} %dynamic-slice_bitcast_fusion.5.length_ref, f32[16,128]{1,0:T(8,128)S(1)} %get-tuple-element.158.decay_ref, f32[16,128]{1,0:T(8,128)S(1)} %get-tuple-element.157.weight_ref, f32[1024,128]{1,0:T(8,128)S(1)} %get-tuple-element.101.tail_ref, ...), custom_call_target="tpu_custom_call" | custom-call | tf_op jit(solution)/shard_map/cond/branch_1_fun/output_conv/pallas_call | solution.py:297
  73.0 14.4 %all_to_all.33.conv_ref = bf16[8,128,128]{2,1,0:T(8,128)(2,1)S(1)} all-to-all(bf16[8,128,128]{2,1,0:T(8,128)(2,1)S(1)} %bitcast.56), channel_id=1, replica_groups=mesh['ctx'=8,'chan'=8,'req'=4] {'ctx'}, dimensions={0} | all-to-all | bytes 524288 | tf_op jit(solution)/shard_map/cond/branch_1_fun/all_to_all | solution.py:387
  87.4 0.8 gate_out.5
  (10 shorter events, 0.1 us)
Async XLA Ops:
  6.2 12.6 %copy-start.5 = (bf16[128,1024]{1,0:T(8,128)(2,1)S(1)}, bf16[128,1024]{1,0:T(8,128)(2,1)}, u32[]{:S(2)}) copy-start(bf16[128,1024]{1,0:T(8,128)(2,1)} %get-tuple-element.103.window_ref) | copy-start | bytes 786436 | tf_op jit(solution)/shard_map/cond
  6.2 12.6 %copy-start.9 = (f32[1024,16]{0,1:T(8,128)S(1)}, f32[1024,16]{0,1:T(8,128)}, u32[]{:S(2)}) copy-start(f32[1024,16]{0,1:T(8,128)} %get-tuple-element.96) | copy-start | bytes 196612 | tf_op jit(solution)/shard_map/cond
  6.2 12.6 %copy-start.13 = (f32[1024,16]{0,1:T(8,128)S(1)}, f32[1024,16]{0,1:T(8,128)}, u32[]{:S(2)}) copy-start(f32[1024,16]{0,1:T(8,128)} %get-tuple-element.97) | copy-start | bytes 196612 | tf_op jit(solution)/shard_map/cond
  6.2 12.6 %copy-start.21 = (f32[1024]{0:T(1024)S(1)}, f32[1024]{0:T(1024)}, u32[]{:S(2)}) copy-start(f32[1024]{0:T(1024)} %get-tuple-element.104) | copy-start | bytes 12292 | tf_op jit(solution)/shard_map/cond
  6.2 27.7 %copy-start.17 = (s32[512]{0:T(512)S(1)}, s32[512]{0:T(512)}, u32[]{:S(2)}) copy-start(s32[512]{0:T(512)} %get-tuple-element.98) | copy-start | bytes 6148 | tf_op jit(solution)/shard_map/cond
  6.2 59.7 %all-to-all-start.2 = ((bf16[64,14,8,128]{3,2,1,0:T(8,128)(2,1)}), bf16[64,14,8,128]{3,2,1,0:T(8,128)(2,1)S(1)}, u32[]{:S(2)}, u32[]{:S(2)}) async-start(bf16[64,14,8,128]{3,2,1,0:T(8,128)(2,1)} %parcel_of.5), calls=%async_computation.2 | async-start | bytes 3670016 | tf_op jit(solution)/shard_map/cond/branch_1_fun/all_to_all | solution.py:374
  18.8 68.5 %copy-start.1 = (bf16[128,1024]{1,0:T(8,128)(2,1)S(1)}, bf16[128,1024]{1,0:T(8,128)(2,1)}, u32[]{:S(2)}) copy-start(bf16[128,1024]{1,0:T(8,128)(2,1)} %get-tuple-element.107.gate_ref) | copy-start | bytes 786436 | tf_op jit(solution)/shard_map/cond
  21.9 39.2 %collective-permute-start.7 = (f32[16,128]{1,0:T(8,128)S(1)}, f32[16,128]{1,0:T(8,128)S(1)}, u32[]{:S(2)}, u32[]{:S(2)}) collective-permute-start(f32[16,128]{1,0:T(8,128)S(1)} %get-tuple-element.155), channel_id=1, source_target_pairs={{0,32},{32,64},{64,96},{96,128},{128,160},{160,192},{192,224},{224... | collective-permute-start | bytes 24584 | tf_op jit(solution)/shard_map/cond/branch_1_fun/ppermute | solution.py:360
  23.6 39.9 %collective-permute-start.8 = (f32[16,128]{1,0:T(8,128)S(1)}, f32[16,128]{1,0:T(8,128)S(1)}, u32[]{:S(2)}, u32[]{:S(2)}) collective-permute-start(f32[16,128]{1,0:T(8,128)S(1)} %get-tuple-element.154), channel_id=1, source_target_pairs={{0,64},{32,96},{64,128},{96,160},{128,192},{160,224},{192,0},{224,... | collective-permute-start | bytes 24584 | tf_op jit(solution)/shard_map/cond/branch_1_fun/ppermute | solution.py:360
  26.0 45.1 %collective-permute-start.9 = (f32[16,128]{1,0:T(8,128)S(1)}, f32[16,128]{1,0:T(8,128)S(1)}, u32[]{:S(2)}, u32[]{:S(2)}) collective-permute-start(f32[16,128]{1,0:T(8,128)S(1)} %get-tuple-element.153), channel_id=1, source_target_pairs={{0,96},{32,128},{64,160},{96,192},{128,224},{160,0},{192,32},{224,... | collective-permute-start | bytes 24584 | tf_op jit(solution)/shard_map/cond/branch_1_fun/ppermute | solution.py:360
  28.8 42.3 %collective-permute-start.10 = (f32[16,128]{1,0:T(8,128)S(1)}, f32[16,128]{1,0:T(8,128)S(1)}, u32[]{:S(2)}, u32[]{:S(2)}) collective-permute-start(f32[16,128]{1,0:T(8,128)S(1)} %get-tuple-element.152), channel_id=1, source_target_pairs={{0,128},{32,160},{64,192},{96,224},{128,0},{160,32},{192,64},{224,... | collective-permute-start | bytes 24584 | tf_op jit(solution)/shard_map/cond/branch_1_fun/ppermute | solution.py:360
  31.0 40.1 %collective-permute-start.11 = (f32[16,128]{1,0:T(8,128)S(1)}, f32[16,128]{1,0:T(8,128)S(1)}, u32[]{:S(2)}, u32[]{:S(2)}) collective-permute-start(f32[16,128]{1,0:T(8,128)S(1)} %get-tuple-element.151), channel_id=1, source_target_pairs={{0,160},{32,192},{64,224},{96,0},{128,32},{160,64},{192,96},{224,1... | collective-permute-start | bytes 24584 | tf_op jit(solution)/shard_map/cond/branch_1_fun/ppermute | solution.py:360
  61.1 10.0 %collective-permute-start.12 = (f32[16,128]{1,0:T(8,128)S(1)}, f32[16,128]{1,0:T(8,128)S(1)}, u32[]{:S(2)}, u32[]{:S(2)}) collective-permute-start(f32[16,128]{1,0:T(8,128)S(1)} %get-tuple-element.150), channel_id=1, source_target_pairs={{0,192},{32,224},{64,0},{96,32},{128,64},{160,96},{192,128},{224,1... | collective-permute-start | bytes 24584 | tf_op jit(solution)/shard_map/cond/branch_1_fun/ppermute | solution.py:360
  63.4 7.7 %collective-permute-start.13 = (f32[16,128]{1,0:T(8,128)S(1)}, f32[16,128]{1,0:T(8,128)S(1)}, u32[]{:S(2)}, u32[]{:S(2)}) collective-permute-start(f32[16,128]{1,0:T(8,128)S(1)} %get-tuple-element.149), channel_id=1, source_target_pairs={{0,224},{32,0},{64,32},{96,64},{128,96},{160,128},{192,160},{224,1... | collective-permute-start | bytes 24584 | tf_op jit(solution)/shard_map/cond/branch_1_fun/ppermute | solution.py:360

commit v8 on v7

--- a/solution.py
+++ b/solution.py
@@ -10,10 +10,11 @@
 LANES = 128
 SUBS = 8
 CHUNK = 128
-PIECES = 2
+PIECES = 4
 COUNTS = (13, 14, 15)
 VMEM_LIMIT = 12 * 1024 * 1024
-WHOLE_VMEM = 60 * 1024 * 1024
+PLAN_VMEM = 57 * 1024 * 1024
+PARCEL_VMEM = 56 * 1024 * 1024
 
 
 def row(ref, index):
@@ -184,7 +185,7 @@
     out_ref[...] = result[...].astype(jnp.bfloat16)
 
 
-def plan_kernel(pool_pages, owner_count, counts, self_ref, table_ref, which_ref, list_ref):
+def plan_kernel(pool_pages, owner_count, counts, self_ref, table_ref, _, which_ref, list_ref):
     bits = pool_pages.bit_length() - 1
     table = table_ref[...]
     shape = (owner_count, table.shape[1])
@@ -205,33 +206,26 @@
     list_ref[...] = chosen.astype(jnp.int32)
 
 
-def parcel_kernel(inner, list_ref, pool_ref, parcel_ref, held, in_sems, out_sems):
+def parcel_kernel(inner, list_ref, pool_ref, parcel_ref, staged, sems):
     tiles, count = parcel_ref.shape[:2]
+    outer = tiles // inner
     each = tiles // PIECES
-    fetches = []
-    for piece in range(PIECES):
-        lanes = pl.ds(piece * each * LANES, each * LANES)
-        for page in range(count):
-            fetches.append(
-                pltpu.make_async_copy(
-                    pool_ref.at[list_ref[0, page], :, lanes],
-                    held.at[page, :, lanes],
-                    in_sems.at[piece, page],
-                )
-            )
-            fetches[-1].start()
+    pages = [list_ref[0, page] for page in range(count)]
     sends = []
     for piece in range(PIECES):
-        for fetch in fetches[piece * count : (piece + 1) * count]:
-            fetch.wait()
-        for block in range(piece * each, (piece + 1) * each):
-            send = pltpu.make_async_copy(
-                held.at[:, :, pl.ds(block * LANES, LANES)],
-                parcel_ref.at[block % inner * (tiles // inner) + block // inner],
-                out_sems.at[block],
-            )
-            send.start()
-            sends.append(send)
+
+        def cut(index, carry, piece=piece):
+            dest = piece * each + index
+            tile = lax.rem(dest, outer) * inner + lax.div(dest, outer)
+            lanes = pl.ds(pl.multiple_of(tile * LANES, LANES), LANES)
+            for page in range(count):
+                staged[dest, page] = pool_ref[pages[page], :, lanes]
+            return carry
+
+        lax.fori_loop(0, each, cut, 0, unroll=2)
+        part = pl.ds(piece * each, each)
+        sends.append(pltpu.make_async_copy(staged.at[part], parcel_ref.at[part], sems.at[piece]))
+        sends[-1].start()
     for send in sends:
         send.wait()
 
@@ -308,33 +302,30 @@
     )(place, length, decay, weight, tail, begin, *ends)
 
 
-def plan_of(self_owner, table, pool_pages, owner_count, counts):
+def plan_of(self_owner, table, pool, pool_pages, owner_count, counts):
     return pl.pallas_call(
         functools.partial(plan_kernel, pool_pages, owner_count, counts),
         out_shape=(
             jax.ShapeDtypeStruct((1,), jnp.int32),
             jax.ShapeDtypeStruct((1, LANES), jnp.int32),
         ),
-        in_specs=[pl.BlockSpec(memory_space=pltpu.SMEM)] + vmem(1),
+        in_specs=[pl.BlockSpec(memory_space=pltpu.SMEM)] + vmem(1) + [pl.BlockSpec(memory_space=pl.ANY)],
         out_specs=(pl.BlockSpec(memory_space=pltpu.SMEM), pl.BlockSpec(memory_space=pltpu.VMEM)),
         compiler_params=params(),
         name="plan_of",
-    )(self_owner, table)
+    )(self_owner, table, pool)
 
 
 def parcel_of(chosen, pool, inner, count):
     _, page_len, width = pool.shape
+    shape = (width // LANES, count, page_len, LANES)
     return pl.pallas_call(
         functools.partial(parcel_kernel, inner),
-        out_shape=jax.ShapeDtypeStruct((width // LANES, count, page_len, LANES), pool.dtype),
-        in_specs=[pl.BlockSpec(memory_space=pltpu.SMEM), pl.BlockSpec(memory_space=pl.ANY)],
+        out_shape=jax.ShapeDtypeStruct(shape, pool.dtype),
+        in_specs=[pl.BlockSpec(memory_space=pltpu.SMEM)] + vmem(1),
         out_specs=pl.BlockSpec(memory_space=pl.ANY),
-        scratch_shapes=[
-            pltpu.VMEM((count, page_len, width), pool.dtype),
-            pltpu.SemaphoreType.DMA((PIECES, count)),
-            pltpu.SemaphoreType.DMA((width // LANES,)),
-        ],
-        compiler_params=params(WHOLE_VMEM),
+        scratch_shapes=[pltpu.VMEM(shape, pool.dtype), pltpu.SemaphoreType.DMA((PIECES,))],
+        compiler_params=params(PARCEL_VMEM),
         name="parcel_of",
     )(chosen, pool)
 
@@ -399,7 +390,7 @@
     owner_count = lax.axis_size("ctx") * chan_count
     counts = [c for c in COUNTS if c < pool_pages]
     which, chosen = plan_of(
-        self_owner[None], page_table[None, :], pool_pages, owner_count, counts
+        self_owner[None], page_table[None, :], page_pool, pool_pages, owner_count, counts
     )
     counts.append(pool_pages)
     return lax.switch(

time: 87.2 us -> 84.6 us (0.970); the launches traced: 88.2 us -> 84.3 us
  Pallas kernels: 16.3 us -> 14.2 us
  waiting for transfers between devices: 26.1 us -> 24 us
    ppermute x7, waiting for transfers between devices: 26.1 us -> 24 us  [end_states(): lax.ppermute(block(hop), 'ctx', [(i, (i + hop) % count) for i in range(co...]
    pallas_call x1, Pallas kernels: 4.23 us -> 2.63 us  [parcel_of(): pl.pallas_call(functools.partial(parcel_kernel, inner), out_shape=jax.Sha...]
  transfers between devices with their start and end apart: 8 -> 8, of which waited for: 1 -> 1; matrix products, arithmetic and copies ran while one was open for 1% -> 1% of each run, Pallas kernels for 9% -> 10%
where the time goes in v8:
time: 84.6 us; the launch traced here: 84.3 us
  starting transfers between devices  29 us (34%)
  waiting for transfers between devices  24 us (28%)
  blocking collectives  14.5 us (17%)
  Pallas kernels  14.2 us (17%)
  local copies, waits for them, and re-layouts  0.85 us (1%)
    ppermute x7, waiting for transfers between devices, end_states(): lax.ppermute(block(hop), 'ctx', [(i, (i + hop) % count) for i in range(co...  24 us
    ppermute x7, starting transfers between devices, end_states(): lax.ppermute(block(hop), 'ctx', [(i, (i + hop) % count) for i in range(co...  16.7 us
    all_to_all x1, blocking collectives, with_count(): lax.all_to_all(convolved.reshape(ctx_count, -1, pencil), 'ctx', split_axi...  14.5 us
    all_to_all x1, starting transfers between devices, with_count(): lax.all_to_all(parcel, ('ctx', 'chan'), split_axis=0, concat_axis=0, tile...  12.2 us
    pallas_call x1, Pallas kernels, cache_conv(): pl.pallas_call(functools.partial(cache_kernel, modes, window // SUBS), ou...  5.1 us
    pallas_call x1, Pallas kernels, window_conv(): pl.pallas_call(functools.partial(window_kernel, modes, rows // SUBS), out...  3.02 us
    pallas_call x1, Pallas kernels, parcel_of(): pl.pallas_call(functools.partial(parcel_kernel, inner), out_shape=jax.Sha...  2.63 us
    pallas_call x1, Pallas kernels, output_conv(): pl.pallas_call(functools.partial(output_kernel, modes, window // SUBS), o...  1.81 us
  transfers between devices with their start and end apart: 8, of which 1 were waited for; matrix products, arithmetic and copies ran while one was open for 1% of the time, Pallas kernels for 10%

profile of v8, /device:TPU:4, one launch (start us, length us, event | category | flops | bytes accessed | tf_op | source)
XLA Modules:
  0.0 84.3 jit_solution(14133335889706535640)
XLA Ops:
  0.0 1.5 %plan_of.1 = (s32[1]{0:T(128)}, s32[1,128]{1,0:T(1,128)S(1)}) custom-call(s32[1]{0:T(128)} %bitcast.36.self_ref, s32[1,512]{1,0:T(1,128)} %bitcast.67, bf16[16,8,8192]{2,1,0:T(8,128)(2,1)} %_.1), custom_call_target="tpu_custom_call" | custom-call | tf_op jit(solution)/shard_map/plan_of/pallas_call | solution.py:306
  2.1 81.5 %conditional.1 = (bf16[128,1024]{1,0:T(8,128)(2,1)S(1)}) conditional(s32[]{:T(128)} %bitcast.38, (s32[1024]{0:T(1024)S(1)}, f32[1024,16]{0,1:T(8,128)}, f32[1024,16]{0,1:T(8,128)}, s32[512]{0:T(512)S(1)}, s32[1,128]{1,0:T(1,128)S(1)}, /*index=5*/bf16[16,8,8192]{2,1,0:T(8,128)(2,1)S(1)}, f32[1024]{0:T(1024)S(1)}, ...), branch_computations={%region_0.2_spmd, %region_2.4_spmd, %region_4.6_spmd, %region_6.8_... | conditional | flops 362036736 | bytes 12733266 | solution.py:396
  2.1 2.6 %parcel_of.4 = bf16[64,13,8,128]{3,2,1,0:T(8,128)(2,1)} custom-call(s32[1,128]{1,0:T(1,128)S(1)} %get-tuple-element.86.list_ref, bf16[16,8,8192]{2,1,0:T(8,128)(2,1)S(1)} %get-tuple-element.87.pool_ref), custom_call_target="tpu_custom_call" | custom-call | tf_op jit(solution)/shard_map/cond/branch_0_fun/parcel_of/pallas_call | solution.py:322
  4.8 0.0 copy-start.5
  4.8 0.0 copy-start.9
  4.8 0.0 copy-start.13
  4.8 12.2 %all-to-all-start = ((bf16[64,13,8,128]{3,2,1,0:T(8,128)(2,1)}), bf16[64,13,8,128]{3,2,1,0:T(8,128)(2,1)S(1)}, u32[]{:S(2)}, u32[]{:S(2)}) async-start(bf16[64,13,8,128]{3,2,1,0:T(8,128)(2,1)} %parcel_of.4), calls=%async_computation | async-start | bytes 3407872 | tf_op jit(solution)/shard_map/cond/branch_0_fun/all_to_all | solution.py:365
  17.1 0.0 copy-start.1
  17.2 3.0 %window_conv.4 = (f32[128,1024]{1,0:T(8,128)S(1)}, f32[16,1024]{1,0:T(8,128)S(1)}) custom-call(bf16[128,1024]{1,0:T(8,128)(2,1)S(1)} %copy-done.5, f32[16,1024]{1,0:T(8,128)S(1)} %bitcast.59, f32[16,1024]{1,0:T(8,128)S(1)} %bitcast.63, f32[1,1024]{1,0:T(1,128)S(1)} %bitcast.68), custom_call_target="tpu_custom_call" | custom-call | flops 25165824 | bytes 786432 | tf_op jit(solution)/shard_map/cond/branch_0_fun/window_conv/pallas_call | solution.py:251
  20.3 1.7 %collective-permute-start = (f32[16,128]{1,0:T(8,128)S(1)}, f32[16,128]{1,0:T(8,128)S(1)}, u32[]{:S(2)}, u32[]{:S(2)}) collective-permute-start(f32[16,128]{1,0:T(8,128)S(1)} %get-tuple-element.145), channel_id=1, source_target_pairs={{0,32},{32,64},{64,96},{96,128},{128,160},{160,192},{192,224},{224... | collective-permute-start | bytes 24584 | tf_op jit(solution)/shard_map/cond/branch_0_fun/ppermute | solution.py:351
  21.9 2.4 %collective-permute-start.1 = (f32[16,128]{1,0:T(8,128)S(1)}, f32[16,128]{1,0:T(8,128)S(1)}, u32[]{:S(2)}, u32[]{:S(2)}) collective-permute-start(f32[16,128]{1,0:T(8,128)S(1)} %get-tuple-element.144), channel_id=1, source_target_pairs={{0,64},{32,96},{64,128},{96,160},{128,192},{160,224},{192,0},{224,... | collective-permute-start | bytes 24584 | tf_op jit(solution)/shard_map/cond/branch_0_fun/ppermute | solution.py:351
  24.4 2.8 %collective-permute-start.2 = (f32[16,128]{1,0:T(8,128)S(1)}, f32[16,128]{1,0:T(8,128)S(1)}, u32[]{:S(2)}, u32[]{:S(2)}) collective-permute-start(f32[16,128]{1,0:T(8,128)S(1)} %get-tuple-element.143), channel_id=1, source_target_pairs={{0,96},{32,128},{64,160},{96,192},{128,224},{160,0},{192,32},{224,... | collective-permute-start | bytes 24584 | tf_op jit(solution)/shard_map/cond/branch_0_fun/ppermute | solution.py:351
  27.2 2.2 %collective-permute-start.3 = (f32[16,128]{1,0:T(8,128)S(1)}, f32[16,128]{1,0:T(8,128)S(1)}, u32[]{:S(2)}, u32[]{:S(2)}) collective-permute-start(f32[16,128]{1,0:T(8,128)S(1)} %get-tuple-element.142), channel_id=1, source_target_pairs={{0,128},{32,160},{64,192},{96,224},{128,0},{160,32},{192,64},{224,... | collective-permute-start | bytes 24584 | tf_op jit(solution)/shard_map/cond/branch_0_fun/ppermute | solution.py:351
  29.4 2.9 %collective-permute-start.4 = (f32[16,128]{1,0:T(8,128)S(1)}, f32[16,128]{1,0:T(8,128)S(1)}, u32[]{:S(2)}, u32[]{:S(2)}) collective-permute-start(f32[16,128]{1,0:T(8,128)S(1)} %get-tuple-element.141), channel_id=1, source_target_pairs={{0,160},{32,192},{64,224},{96,0},{128,32},{160,64},{192,96},{224,1... | collective-permute-start | bytes 24584 | tf_op jit(solution)/shard_map/cond/branch_0_fun/ppermute | solution.py:351
  32.3 0.3 convert_reduce_fusion
  32.7 0.1 dynamic-slice_bitcast_fusion.2.length_ref
  32.7 24.0 %collective-permute-done.rest_1_ = f32[16,128]{1,0:T(8,128)S(1)} collective-permute-done((f32[16,128]{1,0:T(8,128)S(1)}, f32[16,128]{1,0:T(8,128)S(1)}, u32[]{:S(2)}, u32[]{:S(2)}) %collective-permute-start) | collective-permute-done | bytes 8224 | tf_op jit(solution)/shard_map/cond/branch_0_fun/ppermute | solution.py:351
  56.7 2.3 %collective-permute-start.5 = (f32[16,128]{1,0:T(8,128)S(1)}, f32[16,128]{1,0:T(8,128)S(1)}, u32[]{:S(2)}, u32[]{:S(2)}) collective-permute-start(f32[16,128]{1,0:T(8,128)S(1)} %get-tuple-element.140), channel_id=1, source_target_pairs={{0,192},{32,224},{64,0},{96,32},{128,64},{160,96},{192,128},{224,1... | collective-permute-start | bytes 24584 | tf_op jit(solution)/shard_map/cond/branch_0_fun/ppermute | solution.py:351
  59.1 0.0 collective-permute-done.1.rest_2_
  59.1 2.4 %collective-permute-start.6 = (f32[16,128]{1,0:T(8,128)S(1)}, f32[16,128]{1,0:T(8,128)S(1)}, u32[]{:S(2)}, u32[]{:S(2)}) collective-permute-start(f32[16,128]{1,0:T(8,128)S(1)} %get-tuple-element.139), channel_id=1, source_target_pairs={{0,224},{32,0},{64,32},{96,64},{128,96},{160,128},{192,160},{224,1... | collective-permute-start | bytes 24584 | tf_op jit(solution)/shard_map/cond/branch_0_fun/ppermute | solution.py:351
  61.5 0.0 all-to-all-done
  61.5 5.1 %cache_conv.4 = (f32[1024,128]{1,0:T(8,128)S(1)}, f32[128,128]{1,0:T(8,128)S(1)}) custom-call(s32[512]{0:T(512)S(1)} %multiply_add_fusion.slots_ref, bf16[832,8,128]{2,1,0:T(8,128)(2,1)S(1)} %bitcast.54, s32[1,128]{1,0:T(1,128)S(1)} %dynamic-slice_bitcast_fusion.2.length_ref, f32[16,128]{1,0:T(8,128)S(1)} %get-tuple-element.148.decay_ref, ...), custom_call_target="tpu_custom_call" | custom-call | flops 335544320 | bytes 2097152 | tf_op jit(solution)/shard_map/cond/branch_0_fun/cache_conv/pallas_call | solution.py:271
  66.6 0.0 collective-permute-done.2.rest_3_
  66.6 0.0 collective-permute-done.3.rest_4_
  66.6 0.0 collective-permute-done.4.rest_5_
  66.6 0.0 collective-permute-done.5.rest_6_
  66.6 0.0 collective-permute-done.6.rest_7_
  66.7 1.8 %output_conv.4 = bf16[1024,128]{1,0:T(8,128)(2,1)S(1)} custom-call(s32[1]{0:T(128)} %bitcast.place_ref, s32[1,128]{1,0:T(1,128)S(1)} %dynamic-slice_bitcast_fusion.2.length_ref, f32[16,128]{1,0:T(8,128)S(1)} %get-tuple-element.148.decay_ref, f32[16,128]{1,0:T(8,128)S(1)} %get-tuple-element.147.weight_ref, f32[1024,128]{1,0:T(8,128)S(1)} %get-tuple-element.88.tail_ref, ...), custom_call_target="tpu_custom_call" | custom-call | tf_op jit(solution)/shard_map/cond/branch_0_fun/output_conv/pallas_call | solution.py:291
  68.5 14.5 %all_to_all.32.conv_ref = bf16[8,128,128]{2,1,0:T(8,128)(2,1)S(1)} all-to-all(bf16[8,128,128]{2,1,0:T(8,128)(2,1)S(1)} %bitcast.55), channel_id=1, replica_groups=mesh['ctx'=8,'chan'=8,'req'=4] {'ctx'}, dimensions={0} | all-to-all | bytes 524288 | tf_op jit(solution)/shard_map/cond/branch_0_fun/all_to_all | solution.py:378
  83.0 0.1 gate_out.4
  83.6 0.0 copy-start.18
  83.6 0.7 copy-done.18
  (16 shorter events, 0.1 us)
Async XLA Ops:
  0.0 2.1 %copy-start.17 = (s32[512]{0:T(512)S(1)}, s32[512]{0:T(512)}, u32[]{:S(2)}) copy-start(s32[512]{0:T(512)} %param.15) | copy-start | bytes 6148
  0.0 2.1 %copy-start = (bf16[16,8,8192]{2,1,0:T(8,128)(2,1)S(1)}, bf16[16,8,8192]{2,1,0:T(8,128)(2,1)}, u32[]{:S(2)}) copy-start(bf16[16,8,8192]{2,1,0:T(8,128)(2,1)} %_.1) | copy-start | bytes 6291460
  0.0 2.1 %copy-start.20 = (s32[1024]{0:T(1024)S(1)}, s32[1024]{0:T(1024)}, u32[]{:S(2)}) copy-start(s32[1024]{0:T(1024)} %param.16) | copy-start | bytes 12292
  0.0 2.1 %copy-start.19 = (f32[1024]{0:T(1024)S(1)}, f32[1024]{0:T(1024)}, u32[]{:S(2)}) copy-start(f32[1024]{0:T(1024)} %param.19) | copy-start | bytes 12292
  4.8 12.4 %copy-start.5 = (bf16[128,1024]{1,0:T(8,128)(2,1)S(1)}, bf16[128,1024]{1,0:T(8,128)(2,1)}, u32[]{:S(2)}) copy-start(bf16[128,1024]{1,0:T(8,128)(2,1)} %get-tuple-element.90.window_ref) | copy-start | bytes 786436 | tf_op jit(solution)/shard_map/cond
  4.8 12.4 %copy-start.9 = (f32[1024,16]{0,1:T(8,128)S(1)}, f32[1024,16]{0,1:T(8,128)}, u32[]{:S(2)}) copy-start(f32[1024,16]{0,1:T(8,128)} %get-tuple-element.82) | copy-start | bytes 196612 | tf_op jit(solution)/shard_map/cond
  4.8 12.4 %copy-start.13 = (f32[1024,16]{0,1:T(8,128)S(1)}, f32[1024,16]{0,1:T(8,128)}, u32[]{:S(2)}) copy-start(f32[1024,16]{0,1:T(8,128)} %get-tuple-element.84) | copy-start | bytes 196612 | tf_op jit(solution)/shard_map/cond
  4.8 56.7 %all-to-all-start = ((bf16[64,13,8,128]{3,2,1,0:T(8,128)(2,1)}), bf16[64,13,8,128]{3,2,1,0:T(8,128)(2,1)S(1)}, u32[]{:S(2)}, u32[]{:S(2)}) async-start(bf16[64,13,8,128]{3,2,1,0:T(8,128)(2,1)} %parcel_of.4), calls=%async_computation | async-start | bytes 3407872 | tf_op jit(solution)/shard_map/cond/branch_0_fun/all_to_all | solution.py:365
  17.1 65.8 %copy-start.1 = (bf16[128,1024]{1,0:T(8,128)(2,1)S(1)}, bf16[128,1024]{1,0:T(8,128)(2,1)}, u32[]{:S(2)}) copy-start(bf16[128,1024]{1,0:T(8,128)(2,1)} %get-tuple-element.94.gate_ref) | copy-start | bytes 786436 | tf_op jit(solution)/shard_map/cond
  20.3 36.5 %collective-permute-start = (f32[16,128]{1,0:T(8,128)S(1)}, f32[16,128]{1,0:T(8,128)S(1)}, u32[]{:S(2)}, u32[]{:S(2)}) collective-permute-start(f32[16,128]{1,0:T(8,128)S(1)} %get-tuple-element.145), channel_id=1, source_target_pairs={{0,32},{32,64},{64,96},{96,128},{128,160},{160,192},{192,224},{224... | collective-permute-start | bytes 24584 | tf_op jit(solution)/shard_map/cond/branch_0_fun/ppermute | solution.py:351
  21.9 37.1 %collective-permute-start.1 = (f32[16,128]{1,0:T(8,128)S(1)}, f32[16,128]{1,0:T(8,128)S(1)}, u32[]{:S(2)}, u32[]{:S(2)}) collective-permute-start(f32[16,128]{1,0:T(8,128)S(1)} %get-tuple-element.144), channel_id=1, source_target_pairs={{0,64},{32,96},{64,128},{96,160},{128,192},{160,224},{192,0},{224,... | collective-permute-start | bytes 24584 | tf_op jit(solution)/shard_map/cond/branch_0_fun/ppermute | solution.py:351
  24.4 42.3 %collective-permute-start.2 = (f32[16,128]{1,0:T(8,128)S(1)}, f32[16,128]{1,0:T(8,128)S(1)}, u32[]{:S(2)}, u32[]{:S(2)}) collective-permute-start(f32[16,128]{1,0:T(8,128)S(1)} %get-tuple-element.143), channel_id=1, source_target_pairs={{0,96},{32,128},{64,160},{96,192},{128,224},{160,0},{192,32},{224,... | collective-permute-start | bytes 24584 | tf_op jit(solution)/shard_map/cond/branch_0_fun/ppermute | solution.py:351
  27.2 39.4 %collective-permute-start.3 = (f32[16,128]{1,0:T(8,128)S(1)}, f32[16,128]{1,0:T(8,128)S(1)}, u32[]{:S(2)}, u32[]{:S(2)}) collective-permute-start(f32[16,128]{1,0:T(8,128)S(1)} %get-tuple-element.142), channel_id=1, source_target_pairs={{0,128},{32,160},{64,192},{96,224},{128,0},{160,32},{192,64},{224,... | collective-permute-start | bytes 24584 | tf_op jit(solution)/shard_map/cond/branch_0_fun/ppermute | solution.py:351
  29.4 37.3 %collective-permute-start.4 = (f32[16,128]{1,0:T(8,128)S(1)}, f32[16,128]{1,0:T(8,128)S(1)}, u32[]{:S(2)}, u32[]{:S(2)}) collective-permute-start(f32[16,128]{1,0:T(8,128)S(1)} %get-tuple-element.141), channel_id=1, source_target_pairs={{0,160},{32,192},{64,224},{96,0},{128,32},{160,64},{192,96},{224,1... | collective-permute-start | bytes 24584 | tf_op jit(solution)/shard_map/cond/branch_0_fun/ppermute | solution.py:351
  56.7 9.9 %collective-permute-start.5 = (f32[16,128]{1,0:T(8,128)S(1)}, f32[16,128]{1,0:T(8,128)S(1)}, u32[]{:S(2)}, u32[]{:S(2)}) collective-permute-start(f32[16,128]{1,0:T(8,128)S(1)} %get-tuple-element.140), channel_id=1, source_target_pairs={{0,192},{32,224},{64,0},{96,32},{128,64},{160,96},{192,128},{224,1... | collective-permute-start | bytes 24584 | tf_op jit(solution)/shard_map/cond/branch_0_fun/ppermute | solution.py:351
  59.1 7.6 %collective-permute-start.6 = (f32[16,128]{1,0:T(8,128)S(1)}, f32[16,128]{1,0:T(8,128)S(1)}, u32[]{:S(2)}, u32[]{:S(2)}) collective-permute-start(f32[16,128]{1,0:T(8,128)S(1)} %get-tuple-element.139), channel_id=1, source_target_pairs={{0,224},{32,0},{64,32},{96,64},{128,96},{160,128},{192,160},{224,1... | collective-permute-start | bytes 24584 | tf_op jit(solution)/shard_map/cond/branch_0_fun/ppermute | solution.py:351
  83.6 0.7 copy-start.18

commit v9 on v8

--- a/solution.py
+++ b/solution.py
@@ -10,7 +10,7 @@
 LANES = 128
 SUBS = 8
 CHUNK = 128
-PIECES = 4
+PIECES = 8
 COUNTS = (13, 14, 15)
 VMEM_LIMIT = 12 * 1024 * 1024
 PLAN_VMEM = 57 * 1024 * 1024
@@ -33,7 +33,7 @@
         return tuple(s * l + value for s, l in zip(states, lam))
 
     zero = jnp.zeros((SUBS, LANES), jnp.float32)
-    return lax.fori_loop(0, steps, body, tuple(zero for _ in lam), unroll=4)
+    return lax.fori_loop(0, steps, body, tuple(zero for _ in lam), unroll=8)
 
 
 def inclusive_scan(end, decay, steps):
@@ -53,7 +53,7 @@
         write(step, parts[0])
         return new
 
-    lax.fori_loop(0, steps, body, tuple(begin), unroll=4)
+    lax.fori_loop(0, steps, body, tuple(begin), unroll=8)
 
 
 def window_kernel(modes, steps, window_ref, decay_ref, weight_ref, skip_ref, base_ref, end_ref, signal, result):
@@ -222,7 +222,7 @@
                 staged[dest, page] = pool_ref[pages[page], :, lanes]
             return carry
 
-        lax.fori_loop(0, each, cut, 0, unroll=2)
+        lax.fori_loop(0, each, cut, 0, unroll=4)
         part = pl.ds(piece * each, each)
         sends.append(pltpu.make_async_copy(staged.at[part], parcel_ref.at[part], sems.at[piece]))
         sends[-1].start()

time: 84.6 us -> 84.1 us (level)
  transfers between devices with their start and end apart: 8 -> 8, of which waited for: 1 -> 1; matrix products, arithmetic and copies ran while one was open for 1% -> 1% of each run, Pallas kernels for 10% -> 9%
where the time goes in v9:
time: 84.1 us; the launch traced here: 83.9 us
  starting transfers between devices  29 us (34%)
  waiting for transfers between devices  24.2 us (29%)
  blocking collectives  14.5 us (17%)
  Pallas kernels  13.6 us (16%)
  local copies, waits for them, and re-layouts  0.85 us (1%)
    ppermute x7, waiting for transfers between devices, end_states(): lax.ppermute(block(hop), 'ctx', [(i, (i + hop) % count) for i in range(co...  24.2 us
    ppermute x7, starting transfers between devices, end_states(): lax.ppermute(block(hop), 'ctx', [(i, (i + hop) % count) for i in range(co...  16.7 us
    all_to_all x1, blocking collectives, with_count(): lax.all_to_all(convolved.reshape(ctx_count, -1, pencil), 'ctx', split_axi...  14.5 us
    all_to_all x1, starting transfers between devices, with_count(): lax.all_to_all(parcel, ('ctx', 'chan'), split_axis=0, concat_axis=0, tile...  12.2 us
    pallas_call x1, Pallas kernels, cache_conv(): pl.pallas_call(functools.partial(cache_kernel, modes, window // SUBS), ou...  4.98 us
    pallas_call x1, Pallas kernels, window_conv(): pl.pallas_call(functools.partial(window_kernel, modes, rows // SUBS), out...  2.88 us
    pallas_call x1, Pallas kernels, parcel_of(): pl.pallas_call(functools.partial(parcel_kernel, inner), out_shape=jax.Sha...  2.43 us
  transfers between devices with their start and end apart: 8, of which 1 were waited for; matrix products, arithmetic and copies ran while one was open for 1% of the time, Pallas kernels for 9%

profile of v9, /device:TPU:4, one launch (start us, length us, event | category | flops | bytes accessed | tf_op | source)
XLA Modules:
  0.0 83.9 jit_solution(4660592947011852399)
XLA Ops:
  0.0 1.5 %plan_of.1 = (s32[1]{0:T(128)}, s32[1,128]{1,0:T(1,128)S(1)}) custom-call(s32[1]{0:T(128)} %bitcast.36.self_ref, s32[1,512]{1,0:T(1,128)} %bitcast.67, bf16[16,8,8192]{2,1,0:T(8,128)(2,1)} %_.1), custom_call_target="tpu_custom_call" | custom-call | tf_op jit(solution)/shard_map/plan_of/pallas_call | solution.py:306
  2.1 81.0 %conditional.1 = (bf16[128,1024]{1,0:T(8,128)(2,1)S(1)}) conditional(s32[]{:T(128)} %bitcast.38, (s32[1024]{0:T(1024)S(1)}, f32[1024,16]{0,1:T(8,128)}, f32[1024,16]{0,1:T(8,128)}, s32[512]{0:T(512)S(1)}, s32[1,128]{1,0:T(1,128)S(1)}, /*index=5*/bf16[16,8,8192]{2,1,0:T(8,128)(2,1)S(1)}, f32[1024]{0:T(1024)S(1)}, ...), branch_computations={%region_0.2_spmd, %region_2.4_spmd, %region_4.6_spmd, %region_6.8_... | conditional | flops 362036736 | bytes 12733266 | solution.py:396
  2.1 2.4 %parcel_of.4 = bf16[64,13,8,128]{3,2,1,0:T(8,128)(2,1)} custom-call(s32[1,128]{1,0:T(1,128)S(1)} %get-tuple-element.86.list_ref, bf16[16,8,8192]{2,1,0:T(8,128)(2,1)S(1)} %get-tuple-element.87.pool_ref), custom_call_target="tpu_custom_call" | custom-call | tf_op jit(solution)/shard_map/cond/branch_0_fun/parcel_of/pallas_call | solution.py:322
  4.6 0.0 copy-start.5
  4.6 0.0 copy-start.9
  4.6 0.0 copy-start.13
  4.6 12.2 %all-to-all-start = ((bf16[64,13,8,128]{3,2,1,0:T(8,128)(2,1)}), bf16[64,13,8,128]{3,2,1,0:T(8,128)(2,1)S(1)}, u32[]{:S(2)}, u32[]{:S(2)}) async-start(bf16[64,13,8,128]{3,2,1,0:T(8,128)(2,1)} %parcel_of.4), calls=%async_computation | async-start | bytes 3407872 | tf_op jit(solution)/shard_map/cond/branch_0_fun/all_to_all | solution.py:365
  16.9 0.0 copy-start.1
  17.0 2.9 %window_conv.4 = (f32[128,1024]{1,0:T(8,128)S(1)}, f32[16,1024]{1,0:T(8,128)S(1)}) custom-call(bf16[128,1024]{1,0:T(8,128)(2,1)S(1)} %copy-done.5, f32[16,1024]{1,0:T(8,128)S(1)} %bitcast.59, f32[16,1024]{1,0:T(8,128)S(1)} %bitcast.63, f32[1,1024]{1,0:T(1,128)S(1)} %bitcast.68), custom_call_target="tpu_custom_call" | custom-call | flops 25165824 | bytes 786432 | tf_op jit(solution)/shard_map/cond/branch_0_fun/window_conv/pallas_call | solution.py:251
  20.0 1.7 %collective-permute-start = (f32[16,128]{1,0:T(8,128)S(1)}, f32[16,128]{1,0:T(8,128)S(1)}, u32[]{:S(2)}, u32[]{:S(2)}) collective-permute-start(f32[16,128]{1,0:T(8,128)S(1)} %get-tuple-element.145), channel_id=1, source_target_pairs={{0,32},{32,64},{64,96},{96,128},{128,160},{160,192},{192,224},{224... | collective-permute-start | bytes 24584 | tf_op jit(solution)/shard_map/cond/branch_0_fun/ppermute | solution.py:351
  21.6 2.4 %collective-permute-start.1 = (f32[16,128]{1,0:T(8,128)S(1)}, f32[16,128]{1,0:T(8,128)S(1)}, u32[]{:S(2)}, u32[]{:S(2)}) collective-permute-start(f32[16,128]{1,0:T(8,128)S(1)} %get-tuple-element.144), channel_id=1, source_target_pairs={{0,64},{32,96},{64,128},{96,160},{128,192},{160,224},{192,0},{224,... | collective-permute-start | bytes 24584 | tf_op jit(solution)/shard_map/cond/branch_0_fun/ppermute | solution.py:351
  24.0 2.8 %collective-permute-start.2 = (f32[16,128]{1,0:T(8,128)S(1)}, f32[16,128]{1,0:T(8,128)S(1)}, u32[]{:S(2)}, u32[]{:S(2)}) collective-permute-start(f32[16,128]{1,0:T(8,128)S(1)} %get-tuple-element.143), channel_id=1, source_target_pairs={{0,96},{32,128},{64,160},{96,192},{128,224},{160,0},{192,32},{224,... | collective-permute-start | bytes 24584 | tf_op jit(solution)/shard_map/cond/branch_0_fun/ppermute | solution.py:351
  26.9 2.2 %collective-permute-start.3 = (f32[16,128]{1,0:T(8,128)S(1)}, f32[16,128]{1,0:T(8,128)S(1)}, u32[]{:S(2)}, u32[]{:S(2)}) collective-permute-start(f32[16,128]{1,0:T(8,128)S(1)} %get-tuple-element.142), channel_id=1, source_target_pairs={{0,128},{32,160},{64,192},{96,224},{128,0},{160,32},{192,64},{224,... | collective-permute-start | bytes 24584 | tf_op jit(solution)/shard_map/cond/branch_0_fun/ppermute | solution.py:351
  29.0 2.9 %collective-permute-start.4 = (f32[16,128]{1,0:T(8,128)S(1)}, f32[16,128]{1,0:T(8,128)S(1)}, u32[]{:S(2)}, u32[]{:S(2)}) collective-permute-start(f32[16,128]{1,0:T(8,128)S(1)} %get-tuple-element.141), channel_id=1, source_target_pairs={{0,160},{32,192},{64,224},{96,0},{128,32},{160,64},{192,96},{224,1... | collective-permute-start | bytes 24584 | tf_op jit(solution)/shard_map/cond/branch_0_fun/ppermute | solution.py:351
  32.0 0.3 convert_reduce_fusion
  32.3 0.1 dynamic-slice_bitcast_fusion.2.length_ref
  32.4 24.2 %collective-permute-done.rest_1_ = f32[16,128]{1,0:T(8,128)S(1)} collective-permute-done((f32[16,128]{1,0:T(8,128)S(1)}, f32[16,128]{1,0:T(8,128)S(1)}, u32[]{:S(2)}, u32[]{:S(2)}) %collective-permute-start) | collective-permute-done | bytes 8224 | tf_op jit(solution)/shard_map/cond/branch_0_fun/ppermute | solution.py:351
  56.6 2.3 %collective-permute-start.5 = (f32[16,128]{1,0:T(8,128)S(1)}, f32[16,128]{1,0:T(8,128)S(1)}, u32[]{:S(2)}, u32[]{:S(2)}) collective-permute-start(f32[16,128]{1,0:T(8,128)S(1)} %get-tuple-element.140), channel_id=1, source_target_pairs={{0,192},{32,224},{64,0},{96,32},{128,64},{160,96},{192,128},{224,1... | collective-permute-start | bytes 24584 | tf_op jit(solution)/shard_map/cond/branch_0_fun/ppermute | solution.py:351
  58.9 0.0 collective-permute-done.1.rest_2_
  58.9 2.4 %collective-permute-start.6 = (f32[16,128]{1,0:T(8,128)S(1)}, f32[16,128]{1,0:T(8,128)S(1)}, u32[]{:S(2)}, u32[]{:S(2)}) collective-permute-start(f32[16,128]{1,0:T(8,128)S(1)} %get-tuple-element.139), channel_id=1, source_target_pairs={{0,224},{32,0},{64,32},{96,64},{128,96},{160,128},{192,160},{224,1... | collective-permute-start | bytes 24584 | tf_op jit(solution)/shard_map/cond/branch_0_fun/ppermute | solution.py:351
  61.3 0.0 all-to-all-done
  61.3 5.0 %cache_conv.4 = (f32[1024,128]{1,0:T(8,128)S(1)}, f32[128,128]{1,0:T(8,128)S(1)}) custom-call(s32[512]{0:T(512)S(1)} %multiply_add_fusion.slots_ref, bf16[832,8,128]{2,1,0:T(8,128)(2,1)S(1)} %bitcast.54, s32[1,128]{1,0:T(1,128)S(1)} %dynamic-slice_bitcast_fusion.2.length_ref, f32[16,128]{1,0:T(8,128)S(1)} %get-tuple-element.148.decay_ref, ...), custom_call_target="tpu_custom_call" | custom-call | flops 335544320 | bytes 2097152 | tf_op jit(solution)/shard_map/cond/branch_0_fun/cache_conv/pallas_call | solution.py:271
  66.3 0.0 collective-permute-done.2.rest_3_
  66.3 0.0 collective-permute-done.3.rest_4_
  66.3 0.0 collective-permute-done.4.rest_5_
  66.3 0.0 collective-permute-done.5.rest_6_
  66.3 0.0 collective-permute-done.6.rest_7_
  66.3 1.7 %output_conv.4 = bf16[1024,128]{1,0:T(8,128)(2,1)S(1)} custom-call(s32[1]{0:T(128)} %bitcast.place_ref, s32[1,128]{1,0:T(1,128)S(1)} %dynamic-slice_bitcast_fusion.2.length_ref, f32[16,128]{1,0:T(8,128)S(1)} %get-tuple-element.148.decay_ref, f32[16,128]{1,0:T(8,128)S(1)} %get-tuple-element.147.weight_ref, f32[1024,128]{1,0:T(8,128)S(1)} %get-tuple-element.88.tail_ref, ...), custom_call_target="tpu_custom_call" | custom-call | tf_op jit(solution)/shard_map/cond/branch_0_fun/output_conv/pallas_call | solution.py:291
  68.0 14.5 %all_to_all.32.conv_ref = bf16[8,128,128]{2,1,0:T(8,128)(2,1)S(1)} all-to-all(bf16[8,128,128]{2,1,0:T(8,128)(2,1)S(1)} %bitcast.55), channel_id=1, replica_groups=mesh['ctx'=8,'chan'=8,'req'=4] {'ctx'}, dimensions={0} | all-to-all | bytes 524288 | tf_op jit(solution)/shard_map/cond/branch_0_fun/all_to_all | solution.py:378
  82.5 0.1 gate_out.4
  83.2 0.0 copy-start.18
  83.2 0.7 copy-done.18
  (16 shorter events, 0.1 us)
Async XLA Ops:
  0.0 2.1 %copy-start.17 = (s32[512]{0:T(512)S(1)}, s32[512]{0:T(512)}, u32[]{:S(2)}) copy-start(s32[512]{0:T(512)} %param.15) | copy-start | bytes 6148
  0.0 2.1 %copy-start = (bf16[16,8,8192]{2,1,0:T(8,128)(2,1)S(1)}, bf16[16,8,8192]{2,1,0:T(8,128)(2,1)}, u32[]{:S(2)}) copy-start(bf16[16,8,8192]{2,1,0:T(8,128)(2,1)} %_.1) | copy-start | bytes 6291460
  0.0 2.1 %copy-start.20 = (s32[1024]{0:T(1024)S(1)}, s32[1024]{0:T(1024)}, u32[]{:S(2)}) copy-start(s32[1024]{0:T(1024)} %param.16) | copy-start | bytes 12292
  0.0 2.1 %copy-start.19 = (f32[1024]{0:T(1024)S(1)}, f32[1024]{0:T(1024)}, u32[]{:S(2)}) copy-start(f32[1024]{0:T(1024)} %param.19) | copy-start | bytes 12292
  4.6 12.4 %copy-start.5 = (bf16[128,1024]{1,0:T(8,128)(2,1)S(1)}, bf16[128,1024]{1,0:T(8,128)(2,1)}, u32[]{:S(2)}) copy-start(bf16[128,1024]{1,0:T(8,128)(2,1)} %get-tuple-element.90.window_ref) | copy-start | bytes 786436 | tf_op jit(solution)/shard_map/cond
  4.6 12.4 %copy-start.9 = (f32[1024,16]{0,1:T(8,128)S(1)}, f32[1024,16]{0,1:T(8,128)}, u32[]{:S(2)}) copy-start(f32[1024,16]{0,1:T(8,128)} %get-tuple-element.82) | copy-start | bytes 196612 | tf_op jit(solution)/shard_map/cond
  4.6 12.4 %copy-start.13 = (f32[1024,16]{0,1:T(8,128)S(1)}, f32[1024,16]{0,1:T(8,128)}, u32[]{:S(2)}) copy-start(f32[1024,16]{0,1:T(8,128)} %get-tuple-element.84) | copy-start | bytes 196612 | tf_op jit(solution)/shard_map/cond
  4.6 56.7 %all-to-all-start = ((bf16[64,13,8,128]{3,2,1,0:T(8,128)(2,1)}), bf16[64,13,8,128]{3,2,1,0:T(8,128)(2,1)S(1)}, u32[]{:S(2)}, u32[]{:S(2)}) async-start(bf16[64,13,8,128]{3,2,1,0:T(8,128)(2,1)} %parcel_of.4), calls=%async_computation | async-start | bytes 3407872 | tf_op jit(solution)/shard_map/cond/branch_0_fun/all_to_all | solution.py:365
  16.9 65.6 %copy-start.1 = (bf16[128,1024]{1,0:T(8,128)(2,1)S(1)}, bf16[128,1024]{1,0:T(8,128)(2,1)}, u32[]{:S(2)}) copy-start(bf16[128,1024]{1,0:T(8,128)(2,1)} %get-tuple-element.94.gate_ref) | copy-start | bytes 786436 | tf_op jit(solution)/shard_map/cond
  20.0 36.6 %collective-permute-start = (f32[16,128]{1,0:T(8,128)S(1)}, f32[16,128]{1,0:T(8,128)S(1)}, u32[]{:S(2)}, u32[]{:S(2)}) collective-permute-start(f32[16,128]{1,0:T(8,128)S(1)} %get-tuple-element.145), channel_id=1, source_target_pairs={{0,32},{32,64},{64,96},{96,128},{128,160},{160,192},{192,224},{224... | collective-permute-start | bytes 24584 | tf_op jit(solution)/shard_map/cond/branch_0_fun/ppermute | solution.py:351
  21.6 37.3 %collective-permute-start.1 = (f32[16,128]{1,0:T(8,128)S(1)}, f32[16,128]{1,0:T(8,128)S(1)}, u32[]{:S(2)}, u32[]{:S(2)}) collective-permute-start(f32[16,128]{1,0:T(8,128)S(1)} %get-tuple-element.144), channel_id=1, source_target_pairs={{0,64},{32,96},{64,128},{96,160},{128,192},{160,224},{192,0},{224,... | collective-permute-start | bytes 24584 | tf_op jit(solution)/shard_map/cond/branch_0_fun/ppermute | solution.py:351
  24.0 42.3 %collective-permute-start.2 = (f32[16,128]{1,0:T(8,128)S(1)}, f32[16,128]{1,0:T(8,128)S(1)}, u32[]{:S(2)}, u32[]{:S(2)}) collective-permute-start(f32[16,128]{1,0:T(8,128)S(1)} %get-tuple-element.143), channel_id=1, source_target_pairs={{0,96},{32,128},{64,160},{96,192},{128,224},{160,0},{192,32},{224,... | collective-permute-start | bytes 24584 | tf_op jit(solution)/shard_map/cond/branch_0_fun/ppermute | solution.py:351
  26.9 39.4 %collective-permute-start.3 = (f32[16,128]{1,0:T(8,128)S(1)}, f32[16,128]{1,0:T(8,128)S(1)}, u32[]{:S(2)}, u32[]{:S(2)}) collective-permute-start(f32[16,128]{1,0:T(8,128)S(1)} %get-tuple-element.142), channel_id=1, source_target_pairs={{0,128},{32,160},{64,192},{96,224},{128,0},{160,32},{192,64},{224,... | collective-permute-start | bytes 24584 | tf_op jit(solution)/shard_map/cond/branch_0_fun/ppermute | solution.py:351
  29.0 37.3 %collective-permute-start.4 = (f32[16,128]{1,0:T(8,128)S(1)}, f32[16,128]{1,0:T(8,128)S(1)}, u32[]{:S(2)}, u32[]{:S(2)}) collective-permute-start(f32[16,128]{1,0:T(8,128)S(1)} %get-tuple-element.141), channel_id=1, source_target_pairs={{0,160},{32,192},{64,224},{96,0},{128,32},{160,64},{192,96},{224,1... | collective-permute-start | bytes 24584 | tf_op jit(solution)/shard_map/cond/branch_0_fun/ppermute | solution.py:351
  56.6 9.8 %collective-permute-start.5 = (f32[16,128]{1,0:T(8,128)S(1)}, f32[16,128]{1,0:T(8,128)S(1)}, u32[]{:S(2)}, u32[]{:S(2)}) collective-permute-start(f32[16,128]{1,0:T(8,128)S(1)} %get-tuple-element.140), channel_id=1, source_target_pairs={{0,192},{32,224},{64,0},{96,32},{128,64},{160,96},{192,128},{224,1... | collective-permute-start | bytes 24584 | tf_op jit(solution)/shard_map/cond/branch_0_fun/ppermute | solution.py:351
  58.9 7.5 %collective-permute-start.6 = (f32[16,128]{1,0:T(8,128)S(1)}, f32[16,128]{1,0:T(8,128)S(1)}, u32[]{:S(2)}, u32[]{:S(2)}) collective-permute-start(f32[16,128]{1,0:T(8,128)S(1)} %get-tuple-element.139), channel_id=1, source_target_pairs={{0,224},{32,0},{64,32},{96,64},{128,96},{160,128},{192,160},{224,1... | collective-permute-start | bytes 24584 | tf_op jit(solution)/shard_map/cond/branch_0_fun/ppermute | solution.py:351
  83.2 0.7 copy-start.18

commit v10 on v9

--- a/solution.py
+++ b/solution.py
@@ -11,7 +11,7 @@
 SUBS = 8
 CHUNK = 128
 PIECES = 8
-COUNTS = (13, 14, 15)
+COUNTS = (12, 13, 14, 15)
 VMEM_LIMIT = 12 * 1024 * 1024
 PLAN_VMEM = 57 * 1024 * 1024
 PARCEL_VMEM = 56 * 1024 * 1024

time: 84.1 us -> 85.6 us (1.018); the launches traced: 83.9 us -> 86.8 us
  waiting for transfers between devices: 24.2 us -> 26.9 us
    ppermute x7, waiting for transfers between devices: 24.2 us -> 26.9 us  [end_states(): lax.ppermute(block(hop), 'ctx', [(i, (i + hop) % count) for i in range(co...]
where the time goes in v10:
time: 85.6 us; the launch traced here: 86.8 us
  starting transfers between devices  29.1 us (34%)
  waiting for transfers between devices  26.9 us (31%)
  blocking collectives  14.4 us (17%)
  Pallas kernels  13.6 us (16%)
    ppermute x7, waiting for transfers between devices, end_states(): lax.ppermute(block(hop), 'ctx', [(i, (i + hop) % count) for i in range(co...  26.9 us
    ppermute x7, starting transfers between devices, end_states(): lax.ppermute(block(hop), 'ctx', [(i, (i + hop) % count) for i in range(co...  16.8 us
    all_to_all x1, blocking collectives, with_count(): lax.all_to_all(convolved.reshape(ctx_count, -1, pencil), 'ctx', split_axi...  14.4 us
    all_to_all x1, starting transfers between devices, with_count(): lax.all_to_all(parcel, ('ctx', 'chan'), split_axis=0, concat_axis=0, tile...  12.2 us
    pallas_call x1, Pallas kernels, cache_conv(): pl.pallas_call(functools.partial(cache_kernel, modes, window // SUBS), ou...  4.98 us
    pallas_call x1, Pallas kernels, window_conv(): pl.pallas_call(functools.partial(window_kernel, modes, rows // SUBS), out...  2.88 us
    pallas_call x1, Pallas kernels, parcel_of(): pl.pallas_call(functools.partial(parcel_kernel, inner), out_shape=jax.Sha...  2.53 us
  transfers between devices with their start and end apart: 8, of which 1 were waited for; matrix products, arithmetic and copies ran while one was open for 1% of the time, Pallas kernels for 9%

profile of v10, /device:TPU:4, one launch (start us, length us, event | category | flops | bytes accessed | tf_op | source)
XLA Modules:
  0.0 86.8 jit_solution(2412507788828457188)
XLA Ops:
  0.0 1.5 %plan_of.1 = (s32[1]{0:T(128)}, s32[1,128]{1,0:T(1,128)S(1)}) custom-call(s32[1]{0:T(128)} %bitcast.45.self_ref, s32[1,512]{1,0:T(1,128)} %bitcast.83, bf16[16,8,8192]{2,1,0:T(8,128)(2,1)} %_.1), custom_call_target="tpu_custom_call" | custom-call | tf_op jit(solution)/shard_map/plan_of/pallas_call | solution.py:306
  2.1 83.9 %conditional.1 = (bf16[128,1024]{1,0:T(8,128)(2,1)S(1)}) conditional(s32[]{:T(128)} %bitcast.47, (s32[1024]{0:T(1024)S(1)}, f32[1024,16]{0,1:T(8,128)}, f32[1024,16]{0,1:T(8,128)}, s32[512]{0:T(512)S(1)}, s32[1,128]{1,0:T(1,128)S(1)}, /*index=5*/bf16[16,8,8192]{2,1,0:T(8,128)(2,1)S(1)}, f32[1024]{0:T(1024)S(1)}, ...), branch_computations={%region_0.2_spmd, %region_2.4_spmd, %region_4.6_spmd, %region_6.8_... | conditional | flops 362036736 | bytes 12733266 | solution.py:396
  2.4 2.5 %parcel_of.7 = bf16[64,14,8,128]{3,2,1,0:T(8,128)(2,1)} custom-call(s32[1,128]{1,0:T(1,128)S(1)} %get-tuple-element.131.list_ref, bf16[16,8,8192]{2,1,0:T(8,128)(2,1)S(1)} %get-tuple-element.132.pool_ref), custom_call_target="tpu_custom_call" | custom-call | tf_op jit(solution)/shard_map/cond/branch_2_fun/parcel_of/pallas_call | solution.py:322
  4.9 0.0 copy-start.8
  4.9 0.0 copy-start.13
  4.9 0.0 copy-start.18
  5.0 12.2 %all-to-all-start.4 = ((bf16[64,14,8,128]{3,2,1,0:T(8,128)(2,1)}), bf16[64,14,8,128]{3,2,1,0:T(8,128)(2,1)S(1)}, u32[]{:S(2)}, u32[]{:S(2)}) async-start(bf16[64,14,8,128]{3,2,1,0:T(8,128)(2,1)} %parcel_of.7), calls=%async_computation.4 | async-start | bytes 3670016 | tf_op jit(solution)/shard_map/cond/branch_2_fun/all_to_all | solution.py:365
  17.4 2.9 %window_conv.7 = (f32[128,1024]{1,0:T(8,128)S(1)}, f32[16,1024]{1,0:T(8,128)S(1)}) custom-call(bf16[128,1024]{1,0:T(8,128)(2,1)S(1)} %copy-done.8, f32[16,1024]{1,0:T(8,128)S(1)} %bitcast.75, f32[16,1024]{1,0:T(8,128)S(1)} %bitcast.80, f32[1,1024]{1,0:T(1,128)S(1)} %bitcast.86), custom_call_target="tpu_custom_call" | custom-call | flops 25165824 | bytes 786432 | tf_op jit(solution)/shard_map/cond/branch_2_fun/window_conv/pallas_call | solution.py:251
  20.2 0.0 copy-start.3
  20.3 1.7 %collective-permute-start.14 = (f32[16,128]{1,0:T(8,128)S(1)}, f32[16,128]{1,0:T(8,128)S(1)}, u32[]{:S(2)}, u32[]{:S(2)}) collective-permute-start(f32[16,128]{1,0:T(8,128)S(1)} %get-tuple-element.197), channel_id=1, source_target_pairs={{0,32},{32,64},{64,96},{96,128},{128,160},{160,192},{192,224},{224... | collective-permute-start | bytes 24584 | tf_op jit(solution)/shard_map/cond/branch_2_fun/ppermute | solution.py:351
  21.9 2.4 %collective-permute-start.15 = (f32[16,128]{1,0:T(8,128)S(1)}, f32[16,128]{1,0:T(8,128)S(1)}, u32[]{:S(2)}, u32[]{:S(2)}) collective-permute-start(f32[16,128]{1,0:T(8,128)S(1)} %get-tuple-element.196), channel_id=1, source_target_pairs={{0,64},{32,96},{64,128},{96,160},{128,192},{160,224},{192,0},{224,... | collective-permute-start | bytes 24584 | tf_op jit(solution)/shard_map/cond/branch_2_fun/ppermute | solution.py:351
  24.3 2.8 %collective-permute-start.16 = (f32[16,128]{1,0:T(8,128)S(1)}, f32[16,128]{1,0:T(8,128)S(1)}, u32[]{:S(2)}, u32[]{:S(2)}) collective-permute-start(f32[16,128]{1,0:T(8,128)S(1)} %get-tuple-element.195), channel_id=1, source_target_pairs={{0,96},{32,128},{64,160},{96,192},{128,224},{160,0},{192,32},{224,... | collective-permute-start | bytes 24584 | tf_op jit(solution)/shard_map/cond/branch_2_fun/ppermute | solution.py:351
  27.2 2.2 %collective-permute-start.17 = (f32[16,128]{1,0:T(8,128)S(1)}, f32[16,128]{1,0:T(8,128)S(1)}, u32[]{:S(2)}, u32[]{:S(2)}) collective-permute-start(f32[16,128]{1,0:T(8,128)S(1)} %get-tuple-element.194), channel_id=1, source_target_pairs={{0,128},{32,160},{64,192},{96,224},{128,0},{160,32},{192,64},{224,... | collective-permute-start | bytes 24584 | tf_op jit(solution)/shard_map/cond/branch_2_fun/ppermute | solution.py:351
  29.3 2.9 %collective-permute-start.18 = (f32[16,128]{1,0:T(8,128)S(1)}, f32[16,128]{1,0:T(8,128)S(1)}, u32[]{:S(2)}, u32[]{:S(2)}) collective-permute-start(f32[16,128]{1,0:T(8,128)S(1)} %get-tuple-element.193), channel_id=1, source_target_pairs={{0,160},{32,192},{64,224},{96,0},{128,32},{160,64},{192,96},{224,1... | collective-permute-start | bytes 24584 | tf_op jit(solution)/shard_map/cond/branch_2_fun/ppermute | solution.py:351
  32.3 0.3 convert_reduce_fusion.2
  32.6 0.1 dynamic-slice_bitcast_fusion.8.length_ref
  32.7 26.9 %collective-permute-done.14.rest_1_ = f32[16,128]{1,0:T(8,128)S(1)} collective-permute-done((f32[16,128]{1,0:T(8,128)S(1)}, f32[16,128]{1,0:T(8,128)S(1)}, u32[]{:S(2)}, u32[]{:S(2)}) %collective-permute-start.14) | collective-permute-done | bytes 8224 | tf_op jit(solution)/shard_map/cond/branch_2_fun/ppermute | solution.py:351
  59.6 2.3 %collective-permute-start.19 = (f32[16,128]{1,0:T(8,128)S(1)}, f32[16,128]{1,0:T(8,128)S(1)}, u32[]{:S(2)}, u32[]{:S(2)}) collective-permute-start(f32[16,128]{1,0:T(8,128)S(1)} %get-tuple-element.192), channel_id=1, source_target_pairs={{0,192},{32,224},{64,0},{96,32},{128,64},{160,96},{192,128},{224,1... | collective-permute-start | bytes 24584 | tf_op jit(solution)/shard_map/cond/branch_2_fun/ppermute | solution.py:351
  62.0 0.0 collective-permute-done.15.rest_2_
  62.0 2.5 %collective-permute-start.20 = (f32[16,128]{1,0:T(8,128)S(1)}, f32[16,128]{1,0:T(8,128)S(1)}, u32[]{:S(2)}, u32[]{:S(2)}) collective-permute-start(f32[16,128]{1,0:T(8,128)S(1)} %get-tuple-element.191), channel_id=1, source_target_pairs={{0,224},{32,0},{64,32},{96,64},{128,96},{160,128},{192,160},{224,1... | collective-permute-start | bytes 24584 | tf_op jit(solution)/shard_map/cond/branch_2_fun/ppermute | solution.py:351
  64.5 0.0 all-to-all-done.4
  64.5 5.0 %cache_conv.7 = (f32[1024,128]{1,0:T(8,128)S(1)}, f32[128,128]{1,0:T(8,128)S(1)}) custom-call(s32[512]{0:T(512)S(1)} %multiply_add_fusion.2.slots_ref, bf16[896,8,128]{2,1,0:T(8,128)(2,1)S(1)} %bitcast.65, s32[1,128]{1,0:T(1,128)S(1)} %dynamic-slice_bitcast_fusion.8.length_ref, f32[16,128]{1,0:T(8,128)S(1)} %get-tuple-element.200.decay_ref, ...), custom_call_target="tpu_custom_call" | custom-call | flops 335544320 | bytes 2097152 | tf_op jit(solution)/shard_map/cond/branch_2_fun/cache_conv/pallas_call | solution.py:271
  69.5 0.0 collective-permute-done.16.rest_3_
  69.5 0.0 collective-permute-done.17.rest_4_
  69.5 0.0 collective-permute-done.18.rest_5_
  69.5 0.0 collective-permute-done.19.rest_6_
  69.5 0.0 collective-permute-done.20.rest_7_
  69.5 1.7 %output_conv.7 = bf16[1024,128]{1,0:T(8,128)(2,1)S(1)} custom-call(s32[1]{0:T(128)} %bitcast.18.place_ref, s32[1,128]{1,0:T(1,128)S(1)} %dynamic-slice_bitcast_fusion.8.length_ref, f32[16,128]{1,0:T(8,128)S(1)} %get-tuple-element.200.decay_ref, f32[16,128]{1,0:T(8,128)S(1)} %get-tuple-element.199.weight_ref, f32[1024,128]{1,0:T(8,128)S(1)} %get-tuple-element.133.tail_ref, ...), custom_call_target="tpu_custom_call" | custom-call | tf_op jit(solution)/shard_map/cond/branch_2_fun/output_conv/pallas_call | solution.py:291
  71.2 14.4 %all_to_all.42.conv_ref = bf16[8,128,128]{2,1,0:T(8,128)(2,1)S(1)} all-to-all(bf16[8,128,128]{2,1,0:T(8,128)(2,1)S(1)} %bitcast.70), channel_id=1, replica_groups=mesh['ctx'=8,'chan'=8,'req'=4] {'ctx'}, dimensions={0} | all-to-all | bytes 524288 | tf_op jit(solution)/shard_map/cond/branch_2_fun/all_to_all | solution.py:378
  85.6 0.1 gate_out.7
  86.1 0.0 copy-start.22
  86.1 0.7 copy-done.22
  (16 shorter events, 0.1 us)
Async XLA Ops:
  0.0 2.1 %copy-start.21 = (s32[512]{0:T(512)S(1)}, s32[512]{0:T(512)}, u32[]{:S(2)}) copy-start(s32[512]{0:T(512)} %param.16) | copy-start | bytes 6148
  0.0 2.1 %copy-start = (bf16[16,8,8192]{2,1,0:T(8,128)(2,1)S(1)}, bf16[16,8,8192]{2,1,0:T(8,128)(2,1)}, u32[]{:S(2)}) copy-start(bf16[16,8,8192]{2,1,0:T(8,128)(2,1)} %_.1) | copy-start | bytes 6291460
  0.0 2.1 %copy-start.24 = (s32[1024]{0:T(1024)S(1)}, s32[1024]{0:T(1024)}, u32[]{:S(2)}) copy-start(s32[1024]{0:T(1024)} %param.17) | copy-start | bytes 12292
  0.0 2.1 %copy-start.23 = (f32[1024]{0:T(1024)S(1)}, f32[1024]{0:T(1024)}, u32[]{:S(2)}) copy-start(f32[1024]{0:T(1024)} %param.20) | copy-start | bytes 12292
  4.9 12.4 %copy-start.8 = (bf16[128,1024]{1,0:T(8,128)(2,1)S(1)}, bf16[128,1024]{1,0:T(8,128)(2,1)}, u32[]{:S(2)}) copy-start(bf16[128,1024]{1,0:T(8,128)(2,1)} %get-tuple-element.135.window_ref) | copy-start | bytes 786436 | tf_op jit(solution)/shard_map/cond
  4.9 12.4 %copy-start.13 = (f32[1024,16]{0,1:T(8,128)S(1)}, f32[1024,16]{0,1:T(8,128)}, u32[]{:S(2)}) copy-start(f32[1024,16]{0,1:T(8,128)} %get-tuple-element.128) | copy-start | bytes 196612 | tf_op jit(solution)/shard_map/cond
  4.9 12.4 %copy-start.18 = (f32[1024,16]{0,1:T(8,128)S(1)}, f32[1024,16]{0,1:T(8,128)}, u32[]{:S(2)}) copy-start(f32[1024,16]{0,1:T(8,128)} %get-tuple-element.129) | copy-start | bytes 196612 | tf_op jit(solution)/shard_map/cond
  5.0 59.5 %all-to-all-start.4 = ((bf16[64,14,8,128]{3,2,1,0:T(8,128)(2,1)}), bf16[64,14,8,128]{3,2,1,0:T(8,128)(2,1)S(1)}, u32[]{:S(2)}, u32[]{:S(2)}) async-start(bf16[64,14,8,128]{3,2,1,0:T(8,128)(2,1)} %parcel_of.7), calls=%async_computation.4 | async-start | bytes 3670016 | tf_op jit(solution)/shard_map/cond/branch_2_fun/all_to_all | solution.py:365
  20.2 65.4 %copy-start.3 = (bf16[128,1024]{1,0:T(8,128)(2,1)S(1)}, bf16[128,1024]{1,0:T(8,128)(2,1)}, u32[]{:S(2)}) copy-start(bf16[128,1024]{1,0:T(8,128)(2,1)} %get-tuple-element.139.gate_ref) | copy-start | bytes 786436 | tf_op jit(solution)/shard_map/cond
  20.3 39.3 %collective-permute-start.14 = (f32[16,128]{1,0:T(8,128)S(1)}, f32[16,128]{1,0:T(8,128)S(1)}, u32[]{:S(2)}, u32[]{:S(2)}) collective-permute-start(f32[16,128]{1,0:T(8,128)S(1)} %get-tuple-element.197), channel_id=1, source_target_pairs={{0,32},{32,64},{64,96},{96,128},{128,160},{160,192},{192,224},{224... | collective-permute-start | bytes 24584 | tf_op jit(solution)/shard_map/cond/branch_2_fun/ppermute | solution.py:351
  21.9 40.0 %collective-permute-start.15 = (f32[16,128]{1,0:T(8,128)S(1)}, f32[16,128]{1,0:T(8,128)S(1)}, u32[]{:S(2)}, u32[]{:S(2)}) collective-permute-start(f32[16,128]{1,0:T(8,128)S(1)} %get-tuple-element.196), channel_id=1, source_target_pairs={{0,64},{32,96},{64,128},{96,160},{128,192},{160,224},{192,0},{224,... | collective-permute-start | bytes 24584 | tf_op jit(solution)/shard_map/cond/branch_2_fun/ppermute | solution.py:351
  24.3 45.1 %collective-permute-start.16 = (f32[16,128]{1,0:T(8,128)S(1)}, f32[16,128]{1,0:T(8,128)S(1)}, u32[]{:S(2)}, u32[]{:S(2)}) collective-permute-start(f32[16,128]{1,0:T(8,128)S(1)} %get-tuple-element.195), channel_id=1, source_target_pairs={{0,96},{32,128},{64,160},{96,192},{128,224},{160,0},{192,32},{224,... | collective-permute-start | bytes 24584 | tf_op jit(solution)/shard_map/cond/branch_2_fun/ppermute | solution.py:351
  27.2 42.3 %collective-permute-start.17 = (f32[16,128]{1,0:T(8,128)S(1)}, f32[16,128]{1,0:T(8,128)S(1)}, u32[]{:S(2)}, u32[]{:S(2)}) collective-permute-start(f32[16,128]{1,0:T(8,128)S(1)} %get-tuple-element.194), channel_id=1, source_target_pairs={{0,128},{32,160},{64,192},{96,224},{128,0},{160,32},{192,64},{224,... | collective-permute-start | bytes 24584 | tf_op jit(solution)/shard_map/cond/branch_2_fun/ppermute | solution.py:351
  29.3 40.2 %collective-permute-start.18 = (f32[16,128]{1,0:T(8,128)S(1)}, f32[16,128]{1,0:T(8,128)S(1)}, u32[]{:S(2)}, u32[]{:S(2)}) collective-permute-start(f32[16,128]{1,0:T(8,128)S(1)} %get-tuple-element.193), channel_id=1, source_target_pairs={{0,160},{32,192},{64,224},{96,0},{128,32},{160,64},{192,96},{224,1... | collective-permute-start | bytes 24584 | tf_op jit(solution)/shard_map/cond/branch_2_fun/ppermute | solution.py:351
  59.6 9.9 %collective-permute-start.19 = (f32[16,128]{1,0:T(8,128)S(1)}, f32[16,128]{1,0:T(8,128)S(1)}, u32[]{:S(2)}, u32[]{:S(2)}) collective-permute-start(f32[16,128]{1,0:T(8,128)S(1)} %get-tuple-element.192), channel_id=1, source_target_pairs={{0,192},{32,224},{64,0},{96,32},{128,64},{160,96},{192,128},{224,1... | collective-permute-start | bytes 24584 | tf_op jit(solution)/shard_map/cond/branch_2_fun/ppermute | solution.py:351
  62.0 7.6 %collective-permute-start.20 = (f32[16,128]{1,0:T(8,128)S(1)}, f32[16,128]{1,0:T(8,128)S(1)}, u32[]{:S(2)}, u32[]{:S(2)}) collective-permute-start(f32[16,128]{1,0:T(8,128)S(1)} %get-tuple-element.191), channel_id=1, source_target_pairs={{0,224},{32,0},{64,32},{96,64},{128,96},{160,128},{192,160},{224,1... | collective-permute-start | bytes 24584 | tf_op jit(solution)/shard_map/cond/branch_2_fun/ppermute | solution.py:351
  86.1 0.7 copy-start.22
